TPU v7x, 32 devices: a whole 2x2x4 slice. The times are simulated.
32 devices in a mesh: group: 1, seq: 32 (over z, y, x, core).
Axes of the slice: x: 2, y: 2, z: 4, core: 2. Of those that a mesh axis runs over, the one named last changes fastest.
Arguments:
- enc_x: bfloat16 [256, 1280], P(('group', 'seq')), may hold values from -1.5 to 1.5
- enc_qkv: bfloat16 [256, 3, 640], P(('group', 'seq'))
- w_eo: bfloat16 [640, 1280], replicated, may hold values from -0.25 to 0.25
- w_kv: bfloat16 [1280, 2048], replicated, may hold values from -0.15625 to 0.15625
- dec_x: bfloat16 [32, 8192], P(('group', 'seq')), may hold values from -1.5 to 1.5
- w_q: bfloat16 [8192, 8192], P(None, 'seq'), may hold values from -0.0625 to 0.0625
- w_o: bfloat16 [8192, 8192], P(None, 'seq'), may hold values from -0.0625 to 0.0625
- cache_kv: bfloat16 [32, 4, 128, 2048], P(('group', 'seq'))
- doc_tile: int32 [32], P(('group', 'seq')), may hold values from 0 to 1
- cached_count: int32 [32], P(('group', 'seq')), may hold values from 0 to 3
Outputs:
- dec_out: bfloat16 [32, 8192], P(('group', 'seq'))
All inputs are finite; a program needn't handle non-finite values.
Results may differ from a plain program's by a relative error of at most 0.017.
The roundings to bfloat16 on the way count: a program that leaves them out, or rounds other values in their place, can miss the bound.
Values may be sent and summed in bfloat16 or wider, within the bound.
No kernel may reach another device: no remote copies, remote signals or barrier semaphores. Data moves between devices by JAX's collectives and lax.ppermute only.
A program may use at most 64 MiB of HBM per device.

v0:
```python
import jax
import jax.numpy as jnp
from jax import lax
from jax.sharding import PartitionSpec as P

EH = 8
EHD = 80
HD = 128
TILE_LEN = 128


def layer_norm(values):
    center = values - jnp.mean(values, axis=-1, keepdims=True)
    spread = jnp.mean(center * center, axis=-1, keepdims=True)
    return center * lax.rsqrt(spread + 1e-05)


def doc_attend(query_row, doc_kv, filled):
    length = doc_kv.shape[0]
    width = doc_kv.shape[1] // 2
    kv_heads = width // HD
    query_heads = query_row.reshape(kv_heads, -1, HD)
    key_heads = doc_kv[:, :width].reshape(length, kv_heads, HD)
    value_heads = doc_kv[:, width:].reshape(length, kv_heads, HD)
    scores = jnp.einsum(
        "gqd,kgd->gqk", query_heads, key_heads, preferred_element_type=jnp.float32
    ) * HD ** (-0.5)
    inside = jnp.arange(length, dtype=jnp.int32) // TILE_LEN <= filled
    scores = jnp.where(inside[None, None, :], scores, -jnp.inf)
    weights = jax.nn.softmax(scores, axis=-1).astype(jnp.bfloat16)
    result = jnp.einsum("gqk,kgd->gqd", weights, value_heads, preferred_element_type=jnp.float32)
    return result.reshape(1, -1).astype(jnp.bfloat16)


def local(enc_x, enc_qkv, w_eo, w_kv, dec_x, w_q, w_o, cache_kv, doc_tile, cached_count):
    tok_rows = enc_x.shape[0]
    query_heads = enc_qkv[:, 0].reshape(tok_rows, EH, EHD)
    key_piece = lax.all_gather(enc_qkv[:, 1], "seq", axis=0, tiled=True)
    value_piece = lax.all_gather(enc_qkv[:, 2], "seq", axis=0, tiled=True)
    length = key_piece.shape[0]
    key_heads = key_piece.reshape(length, EH, EHD)
    value_heads = value_piece.reshape(length, EH, EHD)
    scores = jnp.einsum(
        "qhd,khd->hqk", query_heads, key_heads, preferred_element_type=jnp.float32
    ) * EHD ** (-0.5)
    old_max = jnp.full((EH, tok_rows), -1e30, jnp.float32)
    new_max = jnp.maximum(old_max, jnp.max(scores, axis=-1))
    powers = jnp.exp(scores - new_max[:, :, None])
    new_total = jnp.sum(powers, axis=-1)
    new_acc = jnp.einsum(
        "hqk,khd->hqd", powers.astype(jnp.bfloat16), value_heads, preferred_element_type=jnp.float32
    )
    enc_attn = (
        (new_acc / new_total[:, :, None])
        .transpose(1, 0, 2)
        .reshape(tok_rows, -1)
        .astype(jnp.bfloat16)
    )
    resid = enc_x.astype(jnp.float32) + jnp.dot(enc_attn, w_eo, preferred_element_type=jnp.float32)
    features = layer_norm(resid).astype(jnp.bfloat16)
    tile_start = doc_tile[0] * TILE_LEN
    x_float = dec_x.astype(jnp.float32)
    normed = (
        x_float * lax.rsqrt(jnp.mean(x_float * x_float, axis=-1, keepdims=True) + 1e-05)
    ).astype(jnp.bfloat16)
    query_cols = jnp.dot(
        lax.all_gather(normed, "seq", axis=0, tiled=True), w_q, preferred_element_type=jnp.float32
    ).astype(jnp.bfloat16)
    query_row = lax.all_to_all(query_cols, "seq", split_axis=0, concat_axis=1, tiled=True)
    zero = jnp.zeros((), jnp.int32)
    filled = cached_count[0]
    local_kv = jnp.dot(features, w_kv, preferred_element_type=jnp.float32).astype(jnp.bfloat16)
    buffer = jnp.zeros((TILE_LEN, w_kv.shape[1]), jnp.bfloat16)
    piece = lax.all_gather(local_kv, "seq", axis=0, tiled=True)
    length = piece.shape[0]
    position = jnp.arange(length, dtype=jnp.int32) - tile_start
    inside = (position >= 0) & (position < buffer.shape[0])
    clipped = jnp.clip(position, 0, buffer.shape[0] - 1)
    tile_kv = buffer.at[clipped].add(jnp.where(inside[:, None], piece, jnp.zeros_like(piece)))
    doc_kv = lax.dynamic_update_slice(cache_kv[0], tile_kv[None], (filled, zero, zero))
    doc_kv = doc_kv.reshape(-1, doc_kv.shape[-1])
    dec_attn = doc_attend(query_row[0], doc_kv, filled)
    output_cols = jnp.dot(
        lax.all_gather(dec_attn, "seq", axis=0, tiled=True), w_o, preferred_element_type=jnp.float32
    ).astype(jnp.bfloat16)
    attn_out = lax.all_to_all(output_cols, "seq", split_axis=0, concat_axis=1, tiled=True)
    return (x_float + attn_out.astype(jnp.float32)).astype(jnp.bfloat16)


def solution(mesh):
    return jax.shard_map(
        local,
        mesh=mesh,
        in_specs=(
            P(("group", "seq"), None),
            P(("group", "seq"), None, None),
            P(),
            P(),
            P(("group", "seq"), None),
            P(None, "seq"),
            P(None, "seq"),
            P(("group", "seq"), None, None, None),
            P(("group", "seq")),
            P(("group", "seq")),
        ),
        out_specs=P(("group", "seq"), None),
        check_vma=False,
    )
```

profile of v0, /device:TPU:0, one launch (start us, length us, event | category | flops | bytes accessed | tf_op | source)
XLA Modules:
  0.0 227.0 jit_solution(8860197279776940830)
XLA Ops:
  6.5 3.3 %copy.64 = bf16[1,4,128,2048]{3,2,1,0:T(8,128)(2,1)} copy(bf16[1,4,128,2048]{3,2,1,0:T(8,128)(2,1)} %param.17) | data formatting | bytes 4194304
  9.9 44.1 %all-gather = bf16[256,1,640]{2,0,1:T(8,128)(2,1)S(1)} all-gather(bf16[8,1,640]{2,0,1:T(8,128)(2,1)S(1)} %get-tuple-element.9), channel_id=2, replica_groups=mesh['group'=1,'seq'=32] {'seq'}, dimensions={0}, use_global_device_ids=true | all-gather | bytes 337920 | tf_op jit(solution)/shard_map/all_gather | solution.py:38
  54.0 0.2 copy.31
  54.2 0.2 fusion.32
  54.5 37.5 %all-gather.1 = bf16[256,1,640]{2,0,1:T(8,128)(2,1)S(1)} all-gather(bf16[8,1,640]{2,0,1:T(8,128)(2,1)S(1)} %get-tuple-element.8), channel_id=3, replica_groups=mesh['group'=1,'seq'=32] {'seq'}, dimensions={0}, use_global_device_ids=true | all-gather | bytes 337920 | tf_op jit(solution)/shard_map/all_gather | solution.py:39
  92.0 0.2 copy.33
  92.2 0.2 fusion.18
  92.3 0.2 fusion.5
  92.7 0.4 fusion.33
  93.2 0.2 multiply_reduce_fusion
  93.4 3.9 %convolution_convert_fusion = bf16[8,2048]{1,0:T(8,128)(2,1)} fusion(bf16[1280,2048]{1,0:T(8,128)(2,1)} %param.13, f32[8,1280]{1,0:T(8,128)S(1)} %get-tuple-element.13, f32[8]{0:T(128)S(1)} %add_rsqrt_fusion, f32[8]{0:T(128)S(1)} %broadcast_multiply_fusion), kind=kOutput, calls=%fused_computation.3 | convolution fusion | flops 41990144 | bytes 5316672 | tf_op jit(solution)/shard_map/dot_general | solution.py:72
  97.3 0.6 multiply_reduce_fusion.1
  98.6 41.2 %all-gather.2 = bf16[32,1,8192]{2,1,0:T(2,128)(2,1)S(1)} all-gather(bf16[1,1,8192]{2,1,0:T(2,128)(2,1)S(1)} %convert_bitcast_fusion), channel_id=1, replica_groups=mesh['group'=1,'seq'=32] {'seq'}, dimensions={0}, use_global_device_ids=true | all-gather | bytes 540672 | tf_op jit(solution)/shard_map/all_gather | solution.py:67
  139.8 3.2 %fusion.6 = bf16[32,1,256]{2,0,1:T(8,128)(2,1)S(1)} fusion(bf16[8192,256]{1,0:T(8,128)(2,1)} %param.15, bf16[32,1,8192]{2,1,0:T(2,128)(2,1)S(1)} %all-gather.2), kind=kOutput, calls=%fused_computation.15 | convolution fusion | flops 134225920 | bytes 4734976 | tf_op jit(solution)/shard_map/dot_general | solution.py:66
  143.0 0.5 broadcast.127
  143.5 0.6 reduce.2
  144.2 0.6 reshape.152
  144.8 2.5 %all-to-all-start = ((bf16[32,2,128]{2,1,0:T(2,128)(2,1)}), bf16[32,2,128]{2,1,0:T(2,128)(2,1)S(1)}, u32[]{:S(2)}, u32[]{:S(2)}) async-start(bf16[32,2,128]{2,1,0:T(2,128)(2,1)} %reshape.152), calls=%async_computation | async-start | bytes 32768 | tf_op jit(solution)/shard_map/all_to_all | solution.py:69
  148.6 5.8 %all-to-all-done = bf16[32,2,128]{2,1,0:T(2,128)(2,1)S(1)} async-done(((bf16[32,2,128]{2,1,0:T(2,128)(2,1)}), bf16[32,2,128]{2,1,0:T(2,128)(2,1)S(1)}, u32[]{:S(2)}, u32[]{:S(2)}) %all-to-all-start) | async-done | bytes 16416 | tf_op jit(solution)/shard_map/all_to_all | solution.py:69
  154.5 4.8 %scatter_custom_fusion = bf16[128,2048]{1,0:T(8,128)(2,1)S(1)} fusion(s32[256]{0:T(256)S(1)} %bitcast.58, bf16[256,2048]{1,0:T(8,128)(2,1)} %all-gather.6.cloned.1.call-done, pred[256]{0:T(512)(128)(4,1)S(1)} %compare_and_fusion, bf16[]{:T(256)} %constant.44.clone.1), kind=kCustom, calls=%fused_computation.17 | custom fusion | flops 1048576 | bytes 1574400 | tf_op jit(solution)/shard_map/scatter-add | solution.py:79
  159.4 0.9 bitcast_dynamic-update-slice_fusion
  160.2 3.0 %fusion.30 = (bf16[512,1024]{1,0:T(8,128)(2,1)}, bf16[512,1024]{1,0:T(8,128)(2,1)}) fusion(bf16[512,2048]{1,0:T(8,128)(2,1)} %bitcast.51), kind=kLoop, calls=%fused_computation.55 | loop fusion | bytes 4194304 | tf_op jit(solution)/shard_map/slice | solution.py:23
  163.2 1.5 copy.44
  164.7 0.2 fusion.3
  165.0 0.2 fusion.34
  165.2 1.5 copy.45
  166.7 0.4 convolution_convert_fusion.2
  167.1 39.7 %all-gather.3 = bf16[32,1,8192]{2,1,0:T(2,128)(2,1)S(1)} all-gather(bf16[1,1,8192]{2,1,0:T(2,128)(2,1)S(1)} %reshape.146), channel_id=1, replica_groups=mesh['group'=1,'seq'=32] {'seq'}, dimensions={0}, use_global_device_ids=true | all-gather | bytes 540672 | tf_op jit(solution)/shard_map/all_gather | solution.py:84
  206.8 3.2 %fusion.7 = bf16[32,1,256]{2,0,1:T(8,128)(2,1)S(1)} fusion(bf16[8192,256]{1,0:T(8,128)(2,1)} %param.16, bf16[32,1,8192]{2,1,0:T(2,128)(2,1)S(1)} %all-gather.3), kind=kOutput, calls=%fused_computation.16 | convolution fusion | flops 134225920 | bytes 4734976 | tf_op jit(solution)/shard_map/dot_general | solution.py:83
  209.9 0.6 reduce.3
  210.6 8.9 %all_to_all.26 = bf16[32,2,128]{2,1,0:T(2,128)(2,1)S(1)} all-to-all(bf16[32,2,128]{2,1,0:T(2,128)(2,1)S(1)} %reshape.154), channel_id=1, replica_groups=mesh['group'=1,'seq'=32] {'seq'}, dimensions={0} | all-to-all | bytes 32768 | tf_op jit(solution)/shard_map/all_to_all | solution.py:86
  219.5 0.7 fusion.21
  (28 shorter events, 0.5 us)
Async XLA Ops:
  6.5 86.2 %copy-start = (bf16[640,1280]{1,0:T(8,128)(2,1)S(1)}, bf16[640,1280]{1,0:T(8,128)(2,1)}, u32[]{:S(2)}) copy-start(bf16[640,1280]{1,0:T(8,128)(2,1)} %param.12) | copy-start | bytes 4915204
  6.5 86.2 %copy-start.3 = (bf16[8,1280]{1,0:T(8,128)(2,1)S(1)}, bf16[8,1280]{1,0:T(8,128)(2,1)}, u32[]{:S(2)}) copy-start(bf16[8,1280]{1,0:T(8,128)(2,1)} %param.10) | copy-start | bytes 61444
  6.5 3.3 %copy-start.2 = (bf16[8,3,640]{2,0,1:T(8,128)(2,1)S(1)}, bf16[8,3,640]{2,0,1:T(8,128)(2,1)}, u32[]{:S(2)}) copy-start(bf16[8,3,640]{2,0,1:T(8,128)(2,1)} %param.11) | copy-start | bytes 92164
  6.5 148.0 %all-gather.6.cloned.1.call-start = ((), (), s32[]{:S(2)}) async-start(), calls=%async_computation.2 | async-start | bytes 1081344 | tf_op jit(solution)/shard_map/all_gather | solution.py:74
  92.0 5.4 %copy-start.1 = (bf16[1,8192]{1,0:T(2,128)(2,1)S(1)}, bf16[1,8192]{1,0:T(2,128)(2,1)}, u32[]{:S(2)}) copy-start(bf16[1,8192]{1,0:T(2,128)(2,1)} %param.14) | copy-start | bytes 49156
  144.8 9.6 %all-to-all-start = ((bf16[32,2,128]{2,1,0:T(2,128)(2,1)}), bf16[32,2,128]{2,1,0:T(2,128)(2,1)S(1)}, u32[]{:S(2)}, u32[]{:S(2)}) async-start(bf16[32,2,128]{2,1,0:T(2,128)(2,1)} %reshape.152), calls=%async_computation | async-start | bytes 32768 | tf_op jit(solution)/shard_map/all_to_all | solution.py:69
Sparse Core Ops, SparseCore 0:
  97.4 51.8 all-gather.5
where the time goes:
time: 227 us
  blocking collectives  171 us (75%)
  between operations  15.5 us (7%)
  local copies, waits for them, and re-layouts  11.9 us (5%)
  matrix products  11.8 us (5%)
  other arithmetic  8.08 us (4%)
  waiting for transfers between devices  5.84 us (3%)
  starting transfers between devices  2.46 us (1%)
    all_gather x1, blocking collectives, local(): key_piece = lax.all_gather(enc_qkv[:, 1], 'seq', axis=0, tiled=True)  44.1 us
    all_gather x1, blocking collectives, local(): lax.all_gather(normed, 'seq', axis=0, tiled=True)  41.2 us
    all_gather x1, blocking collectives, local(): lax.all_gather(dec_attn, 'seq', axis=0, tiled=True)  39.7 us
    all_gather x1, blocking collectives, local(): value_piece = lax.all_gather(enc_qkv[:, 2], 'seq', axis=0, tiled=True)  37.5 us
    all_to_all x1, blocking collectives, local(): lax.all_to_all(output_cols, 'seq', split_axis=0, concat_axis=1, tiled=True)  8.85 us
    unnamed x16, local copies, waits for them, and re-layouts  6.99 us
    all_to_all x1, waiting for transfers between devices, local(): lax.all_to_all(query_cols, 'seq', split_axis=0, concat_axis=1, tiled=True)  5.8 us
    scatter-add x1, other arithmetic, local(): buffer.at[clipped]  4.8 us
  transfers between devices with their start and end apart: 2, of which 1 were waited for; matrix products, arithmetic and copies ran while one was open for 3% of the time, Pallas kernels for 0%

commit v1 on v0

v1 whole, which is shorter than its diff:
```python
import jax
import jax.numpy as jnp
from jax import lax
from jax.experimental import pallas as pl
from jax.experimental.pallas import tpu as pltpu
from jax.sharding import PartitionSpec as P

EH = 8
EHD = 80
HD = 128
TILE_LEN = 128
LANES = 128
SUB = 8
VMEM = pl.BlockSpec(memory_space=pltpu.VMEM)
SMEM = pl.BlockSpec(memory_space=pltpu.SMEM)
F32 = jnp.float32
BF16 = jnp.bfloat16


def params(mib):
    return pltpu.CompilerParams(vmem_limit_bytes=mib * 1024 * 1024)


def pack_kernel(dec_x_ref, qkv_ref, enc_x_ref, out_ref, rows_ref):
    x = dec_x_ref[...].astype(F32)
    scale = lax.rsqrt(jnp.mean(x * x, axis=-1, keepdims=True) + 1e-05)
    normed = x * scale
    groups = x.shape[1] // LANES
    for k in range(groups):
        rows_ref[k : k + 1, :] = normed[:, k * LANES : (k + 1) * LANES]
    copies = out_ref.shape[0]

    def put(place, block):
        block = block.astype(BF16)
        for copy in range(copies):
            out_ref[copy, place] = block

    for i in range(groups // SUB):
        put(i, rows_ref[i * SUB : (i + 1) * SUB, :])
    place = groups // SUB
    qkv = qkv_ref[...].astype(F32)
    for i in range(3):
        part = qkv[:, i, :]
        for t in range(part.shape[1] // LANES):
            put(place, part[:, t * LANES : (t + 1) * LANES])
            place += 1
    enc_x = enc_x_ref[...]
    for t in range(enc_x.shape[1] // LANES):
        put(place, enc_x[:, t * LANES : (t + 1) * LANES])
        place += 1


def project_kernel(own_ref, other_ref, w_ref, out_ref, rows_ref, x_ref):
    chips = own_ref.shape[0]
    depth = w_ref.shape[0]
    for side, ref in enumerate((own_ref, other_ref)):
        for i in range(depth // (SUB * LANES)):
            rows_ref[...] = ref[:, i].astype(F32).reshape(chips * SUB, LANES)
            for j in range(SUB):
                k = i * SUB + j
                x_ref[side * chips : (side + 1) * chips, k * LANES : (k + 1) * LANES] = rows_ref[
                    pl.ds(j, chips, stride=SUB), :
                ].astype(BF16)
    result = jnp.dot(x_ref[...], w_ref[...], preferred_element_type=F32)
    core = lax.rem(lax.axis_index("seq"), 2)
    parts, lanes = out_ref.shape[2:]
    for side in range(2):
        half = result[side * chips : (side + 1) * chips]
        half = jnp.stack([half[:, p * lanes : (p + 1) * lanes] for p in range(parts)], axis=1)
        where = core if side == 0 else 1 - core
        out_ref[:, pl.ds(where, 1)] = half.astype(BF16)[:, None]


def encode_kernel(tile_ref, own_ref, other_ref, w_eo_ref, w_kv_ref, out_ref):
    width = w_eo_ref.shape[0]
    model = w_eo_ref.shape[1]
    tiles = width // LANES
    first = own_ref.shape[1] - 3 * tiles - model // LANES
    chips = TILE_LEN // (2 * SUB)
    mine = pl.ds(tile_ref[0] * chips, chips)

    def merge(block):
        return block.astype(F32).reshape(-1, LANES)

    def every(place):
        return jnp.concatenate([merge(own_ref[:, place]), merge(other_ref[:, place])], axis=0).astype(BF16)

    def tile_rows(place):
        return jnp.concatenate([merge(own_ref[mine, place]), merge(other_ref[mine, place])], axis=0)

    query = jnp.concatenate([tile_rows(first + t) for t in range(tiles)], axis=1).astype(BF16)
    keys = jnp.concatenate([every(first + tiles + t) for t in range(tiles)], axis=1)
    values = jnp.concatenate([every(first + 2 * tiles + t) for t in range(tiles)], axis=1)
    column = lax.broadcasted_iota(jnp.int32, (TILE_LEN, width), 1)
    attn = [jnp.zeros((TILE_LEN, LANES), F32) for _ in range(tiles)]
    for h in range(EH):
        lo, hi = h * EHD // LANES, (h * EHD + EHD - 1) // LANES + 1
        span = slice(lo * LANES, hi * LANES)
        inside = (column[:, span] >= h * EHD) & (column[:, span] < (h + 1) * EHD)
        head = jnp.where(inside, query[:, span], jnp.zeros((), BF16))
        scores = lax.dot_general(head, keys[:, span], (((1,), (1,)), ((), ())), preferred_element_type=F32)
        scores = scores * EHD ** (-0.5)
        powers = jnp.exp(scores - jnp.max(scores, axis=-1, keepdims=True))
        weights = (powers / jnp.sum(powers, axis=-1, keepdims=True)).astype(BF16)
        part = jnp.dot(weights, values[:, span], preferred_element_type=F32)
        part = jnp.where(inside, part, 0.0)
        for t in range(lo, hi):
            attn[t] = attn[t] + part[:, (t - lo) * LANES : (t - lo + 1) * LANES]
    attn = jnp.concatenate(attn, axis=1).astype(BF16)
    enc_x = jnp.concatenate([tile_rows(first + 3 * tiles + t) for t in range(model // LANES)], axis=1)
    resid = enc_x + jnp.dot(attn, w_eo_ref[...], preferred_element_type=F32)
    center = resid - jnp.mean(resid, axis=-1, keepdims=True)
    spread = jnp.mean(center * center, axis=-1, keepdims=True)
    features = (center * lax.rsqrt(spread + 1e-05)).astype(BF16)
    out_ref[...] = jnp.dot(features, w_kv_ref[...], preferred_element_type=F32).astype(BF16)


def attend_kernel(count_ref, query_ref, cache_ref, new_ref, out_ref):
    filled = count_ref[0]
    slots, length, both = cache_ref.shape[1:]
    width = both // 2
    kv_heads = width // HD
    per = query_ref.shape[0] // kv_heads
    query = query_ref[...]
    scores = []
    for g in range(kv_heads):
        head = query[g * per : (g + 1) * per]
        cols = slice(g * HD, (g + 1) * HD)
        keys = cache_ref[0, :, :, cols].reshape(slots * length, HD)
        old = lax.dot_general(head, keys, (((1,), (1,)), ((), ())), preferred_element_type=F32)
        new = lax.dot_general(head, new_ref[:, cols], (((1,), (1,)), ((), ())), preferred_element_type=F32)
        scores.append(jnp.concatenate([old, new], axis=1))
    scores = jnp.concatenate(scores, axis=0) * HD ** (-0.5)
    slot = lax.broadcasted_iota(jnp.int32, scores.shape, 1) // length
    scores = jnp.where((slot < filled) | (slot == slots), scores, -jnp.inf)
    powers = jnp.exp(scores - jnp.max(scores, axis=-1, keepdims=True))
    weights = (powers / jnp.sum(powers, axis=-1, keepdims=True)).astype(BF16)
    copies = out_ref.shape[0]
    for g in range(kv_heads):
        mine = weights[g * per : (g + 1) * per]
        cols = slice(width + g * HD, width + (g + 1) * HD)
        values = cache_ref[0, :, :, cols].reshape(slots * length, HD)
        part = jnp.dot(mine[:, : slots * length], values, preferred_element_type=F32)
        part = part + jnp.dot(mine[:, slots * length :], new_ref[:, cols], preferred_element_type=F32)
        part = part.astype(BF16)
        for copy in range(copies):
            out_ref[copy, g] = part


def finish_kernel(attn_ref, dec_x_ref, out_ref):
    attn = attn_ref[...].astype(F32)
    for k in range(attn.shape[0]):
        cols = slice(k * LANES, (k + 1) * LANES)
        out_ref[:, cols] = (dec_x_ref[:, cols].astype(F32) + attn[k : k + 1]).astype(BF16)


def solution(mesh):
    devices = mesh.shape["seq"]
    chips = devices // 2
    across = [[2 * chip + core for chip in range(chips)] for core in range(2)]
    swap = [(i, i ^ 1) for i in range(devices)]

    def gather(copies):
        own = lax.all_to_all(copies, "seq", 0, 0, tiled=True, axis_index_groups=across)
        return own, lax.ppermute(own, "seq", swap)

    def project(own, other, weight):
        depth, cols = weight.shape
        lanes = min(cols, LANES)
        out = pl.pallas_call(
            project_kernel,
            out_shape=jax.ShapeDtypeStruct((chips, 2, cols // lanes, lanes), BF16),
            in_specs=[VMEM] * 3,
            out_specs=VMEM,
            scratch_shapes=[pltpu.VMEM((chips * SUB, LANES), F32), pltpu.VMEM((2 * chips, depth), BF16)],
            compiler_params=params(24),
        )(own, other, weight)
        sent = out.reshape(devices, cols // lanes, lanes)
        return lax.all_to_all(sent, "seq", 0, 0, tiled=True).reshape(-1, LANES)

    def local(enc_x, enc_qkv, w_eo, w_kv, dec_x, w_q, w_o, cache_kv, doc_tile, cached_count):
        groups = (dec_x.size + enc_qkv.size + enc_x.size) // (SUB * LANES)
        packed = pl.pallas_call(
            pack_kernel,
            out_shape=jax.ShapeDtypeStruct((chips, groups, SUB, LANES), BF16),
            in_specs=[VMEM] * 3,
            out_specs=VMEM,
            scratch_shapes=[pltpu.VMEM((dec_x.shape[1] // LANES, LANES), F32)],
            compiler_params=params(16),
        )(dec_x, enc_qkv, enc_x)
        own, other = gather(packed)
        query = project(own, other, w_q)
        new_kv = pl.pallas_call(
            encode_kernel,
            out_shape=jax.ShapeDtypeStruct((TILE_LEN, w_kv.shape[1]), BF16),
            in_specs=[SMEM] + [VMEM] * 4,
            out_specs=VMEM,
            compiler_params=params(40),
        )(doc_tile, own, other, w_eo, w_kv)
        heads = query.shape[0]
        copies = pl.pallas_call(
            attend_kernel,
            out_shape=jax.ShapeDtypeStruct((chips, heads // SUB, SUB, LANES), BF16),
            in_specs=[SMEM] + [VMEM] * 3,
            out_specs=VMEM,
            compiler_params=params(24),
        )(cached_count, query, cache_kv, new_kv)
        own, other = gather(copies)
        attn_out = project(own, other, w_o)
        return pl.pallas_call(
            finish_kernel,
            out_shape=jax.ShapeDtypeStruct(dec_x.shape, BF16),
            in_specs=[VMEM] * 2,
            out_specs=VMEM,
            compiler_params=params(16),
        )(attn_out, dec_x)

    return jax.shard_map(
        local,
        mesh=mesh,
        in_specs=(
            P(("group", "seq"), None),
            P(("group", "seq"), None, None),
            P(),
            P(),
            P(("group", "seq"), None),
            P(None, "seq"),
            P(None, "seq"),
            P(("group", "seq"), None, None, None),
            P(("group", "seq")),
            P(("group", "seq")),
        ),
        out_specs=P(("group", "seq"), None),
        check_vma=False,
    )
```

time: 227 us -> 91.9 us (0.40)
  blocking collectives: 171 us -> 62.6 us
  between operations: 15.5 us -> 1.38 us
  matrix products: 11.8 us -> 0 us
  Pallas kernels: 0 us -> 8.29 us
  other arithmetic: 8.08 us -> 0 us
    all_gather x4 -> x0, blocking collectives: 163 us -> none  [the longest x1 44.1 us: local(): key_piece = lax.all_gather(enc_qkv[:, 1], 'seq', axis=0, tiled=True)]
    all_to_all x1 -> x3, blocking collectives: 8.85 us -> 62.6 us  [the longest x2 53.1 us: gather(): lax.all_to_all(copies, 'seq', 0, 0, tiled=True, axis_index_groups=across)]
    dot_general x8 -> x0, matrix products: 11.8 us -> none  [the longest x1 3.93 us: local(): jnp.dot(features, w_kv, preferred_element_type=jnp.float32)]
    pallas_call x0 -> x6, Pallas kernels: none -> 8.29 us  [the longest x1 4.04 us: local(): pl.pallas_call(encode_kernel, out_shape=jax.ShapeDtypeStruct((TILE_LEN, w...]
    all_to_all x1, waiting for transfers between devices: 5.8 us -> 0.01 us  [project(): return lax.all_to_all(sent, 'seq', 0, 0, tiled=True).reshape(-1, LANES)]
    unnamed x16 -> x17, local copies, waits for them, and re-layouts: 6.99 us -> 12.1 us
    scatter-add x1 -> x0, other arithmetic: 4.8 us -> none  [local(): buffer.at[clipped]]
    ppermute x0 -> x2, waiting for transfers between devices: none -> 4.24 us  [gather(): return (own, lax.ppermute(own, 'seq', swap))]
  transfers between devices with their start and end apart: 2 -> 3, of which waited for: 1 -> 2; matrix products, arithmetic and copies ran while one was open for 3% -> 0% of each run, Pallas kernels for 0% -> 4%
where the time goes in v1:
time: 91.9 us; the launch traced here: 91.2 us
  blocking collectives  62.6 us (68%)
  local copies, waits for them, and re-layouts  12.1 us (13%)
  Pallas kernels  8.29 us (9%)
  waiting for transfers between devices  4.24 us (5%)
  starting transfers between devices  2.55 us (3%)
  between operations  1.38 us (2%)
    all_to_all x2, blocking collectives, gather(): lax.all_to_all(copies, 'seq', 0, 0, tiled=True, axis_index_groups=across)  53.1 us
    unnamed x17, local copies, waits for them, and re-layouts  12.1 us
    all_to_all x1, blocking collectives, project(): return lax.all_to_all(sent, 'seq', 0, 0, tiled=True).reshape(-1, LANES)  9.48 us
    ppermute x2, waiting for transfers between devices, gather(): return (own, lax.ppermute(own, 'seq', swap))  4.24 us
    pallas_call x1, Pallas kernels, local(): pl.pallas_call(encode_kernel, out_shape=jax.ShapeDtypeStruct((TILE_LEN, w...  4.04 us
    all_to_all x1, starting transfers between devices, project(): return lax.all_to_all(sent, 'seq', 0, 0, tiled=True).reshape(-1, LANES)  2.54 us
    pallas_call x2, Pallas kernels, project(): pl.pallas_call(project_kernel, out_shape=jax.ShapeDtypeStruct((chips, 2,...  2.49 us
  transfers between devices with their start and end apart: 3, of which 2 were waited for; matrix products, arithmetic and copies ran while one was open for 0% of the time, Pallas kernels for 4%

profile of v1, /device:TPU:0, one launch (start us, length us, event | category | flops | bytes accessed | tf_op | source)
XLA Modules:
  0.0 91.2 jit_solution(8674593629658277916)
XLA Ops:
  0.0 0.8 copy.11.qkv_ref
  0.8 0.0 copy-start.5
  0.8 0.7 copy-done.5
  1.5 0.0 copy-start.7
  1.5 0.7 copy-done.7
  2.3 0.2 shard_map.100
  2.5 36.2 %all_to_all.20.own_ref = bf16[16,33,8,128]{3,2,1,0:T(8,128)(2,1)S(1)} all-to-all(bf16[16,33,8,128]{3,2,1,0:T(8,128)(2,1)S(1)} %shard_map.100), channel_id=1, replica_groups={{0,2,4,6,8,10,12,14,16,18,20,22,24,26,28,30},{1,3,5,7,9,11,13,15,17,19,..., dimensions={0} | all-to-all | bytes 2162688 | tf_op jit(solution)/shard_map/all_to_all | solution.py:164
  38.7 0.0 collective-permute-start
  38.7 2.7 %collective-permute-done.other_ref = bf16[16,33,8,128]{3,2,1,0:T(8,128)(2,1)S(1)} collective-permute-done((bf16[16,33,8,128]{3,2,1,0:T(8,128)(2,1)S(1)}, bf16[16,33,8,128]{3,2,1,0:T(8,128)(2,1)S(1)}, u32[]{:S(2)}, u32[]{:S(2)}) %collective-permute-start) | collective-permute-done | bytes 1081376 | tf_op jit(solution)/shard_map/ppermute | solution.py:165
  41.4 0.0 copy-start.1
  41.4 2.2 %copy-done.1 = bf16[8192,256]{1,0:T(8,128)(2,1)S(1)} copy-done((bf16[8192,256]{1,0:T(8,128)(2,1)S(1)}, bf16[8192,256]{1,0:T(8,128)(2,1)}, u32[]{:S(2)}) %copy-start.1) | copy-done | bytes 4194328
  43.6 1.5 %shard_map.101 = bf16[16,2,2,128]{3,2,1,0:T(2,128)(2,1)} custom-call(bf16[16,33,8,128]{3,2,1,0:T(8,128)(2,1)S(1)} %all_to_all.20.own_ref, bf16[16,33,8,128]{3,2,1,0:T(8,128)(2,1)S(1)} %collective-permute-done.other_ref, bf16[8192,256]{1,0:T(8,128)(2,1)S(1)} %copy-done.1), custom_call_target="tpu_custom_call" | custom-call | tf_op jit(solution)/shard_map/pallas_call | solution.py:170
  45.1 2.5 %all-to-all-start.1 = ((bf16[32,2,128]{2,1,0:T(2,128)(2,1)}), bf16[32,2,128]{2,1,0:T(2,128)(2,1)S(1)}, u32[]{:S(2)}, u32[]{:S(2)}) async-start(bf16[32,2,128]{2,1,0:T(2,128)(2,1)} %bitcast), calls=%async_computation.1 | async-start | bytes 32768 | tf_op jit(solution)/shard_map/all_to_all | solution.py:179
  49.0 0.0 copy-start
  49.0 2.5 %copy-done = bf16[1280,2048]{1,0:T(8,128)(2,1)S(1)} copy-done((bf16[1280,2048]{1,0:T(8,128)(2,1)S(1)}, bf16[1280,2048]{1,0:T(8,128)(2,1)}, u32[]{:S(2)}) %copy-start) | copy-done | bytes 5242904
  51.5 0.0 copy-start.4
  51.5 1.4 %copy-done.4 = bf16[640,1280]{1,0:T(8,128)(2,1)S(1)} copy-done((bf16[640,1280]{1,0:T(8,128)(2,1)S(1)}, bf16[640,1280]{1,0:T(8,128)(2,1)}, u32[]{:S(2)}) %copy-start.4) | copy-done | bytes 1638424
  52.9 4.0 %shard_map.102.new_ref = bf16[128,2048]{1,0:T(8,128)(2,1)S(1)} custom-call(s32[1]{0:T(128)S(6)} %copy.12.tile_ref, bf16[16,33,8,128]{3,2,1,0:T(8,128)(2,1)S(1)} %all_to_all.20.own_ref, bf16[16,33,8,128]{3,2,1,0:T(8,128)(2,1)S(1)} %collective-permute-done.other_ref, bf16[640,1280]{1,0:T(8,128)(2,1)S(1)} %copy-done.4, bf16[1280,2048]{1,0:T(8,128)(2,1)S(1)} %copy-done), custom_call_target="tpu_custom_call" | custom-call | tf_op jit(solution)/shard_map/pallas_call | solution.py:193
  56.9 0.0 all-to-all-done.1
  57.0 0.0 copy-start.3
  57.0 1.6 %copy-done.3 = bf16[1,4,128,2048]{3,2,1,0:T(8,128)(2,1)S(1)} copy-done((bf16[1,4,128,2048]{3,2,1,0:T(8,128)(2,1)S(1)}, bf16[1,4,128,2048]{3,2,1,0:T(8,128)(2,1)}, u32[]{:S(2)}) %copy-start.3) | copy-done | bytes 2097176
  58.5 0.9 shard_map.103
  59.4 0.0 copy-start.6
  59.4 17.0 %all_to_all.21.own_ref = bf16[16,8,8,128]{3,2,1,0:T(8,128)(2,1)S(1)} all-to-all(bf16[16,8,8,128]{3,2,1,0:T(8,128)(2,1)S(1)} %shard_map.103), channel_id=1, replica_groups={{0,2,4,6,8,10,12,14,16,18,20,22,24,26,28,30},{1,3,5,7,9,11,13,15,17,19,..., dimensions={0} | all-to-all | bytes 524288 | tf_op jit(solution)/shard_map/all_to_all | solution.py:164
  76.4 0.0 collective-permute-start.1
  76.4 1.5 %collective-permute-done.1.other_ref = bf16[16,8,8,128]{3,2,1,0:T(8,128)(2,1)S(1)} collective-permute-done((bf16[16,8,8,128]{3,2,1,0:T(8,128)(2,1)S(1)}, bf16[16,8,8,128]{3,2,1,0:T(8,128)(2,1)S(1)}, u32[]{:S(2)}, u32[]{:S(2)}) %collective-permute-start.1) | collective-permute-done | bytes 262176 | tf_op jit(solution)/shard_map/ppermute | solution.py:165
  77.9 0.0 copy-start.2
  77.9 2.2 %copy-done.2 = bf16[8192,256]{1,0:T(8,128)(2,1)S(1)} copy-done((bf16[8192,256]{1,0:T(8,128)(2,1)S(1)}, bf16[8192,256]{1,0:T(8,128)(2,1)}, u32[]{:S(2)}) %copy-start.2) | copy-done | bytes 4194328
  80.1 0.9 %shard_map.104 = bf16[16,2,2,128]{3,2,1,0:T(2,128)(2,1)S(1)} custom-call(bf16[16,8,8,128]{3,2,1,0:T(8,128)(2,1)S(1)} %all_to_all.21.own_ref, bf16[16,8,8,128]{3,2,1,0:T(8,128)(2,1)S(1)} %collective-permute-done.1.other_ref, bf16[8192,256]{1,0:T(8,128)(2,1)S(1)} %copy-done.2), custom_call_target="tpu_custom_call" | custom-call | tf_op jit(solution)/shard_map/pallas_call | solution.py:170
  81.1 9.5 %all_to_all.22 = bf16[32,2,128]{2,1,0:T(2,128)(2,1)S(1)} all-to-all(bf16[32,2,128]{2,1,0:T(2,128)(2,1)S(1)} %bitcast.5), channel_id=1, replica_groups=mesh['group'=1,'seq'=32] {'seq'}, dimensions={0} | all-to-all | bytes 32768 | tf_op jit(solution)/shard_map/all_to_all | solution.py:179
  90.5 0.0 copy-done.6
  90.5 0.7 shard_map.105
Async XLA Ops:
  0.8 0.8 copy-start.5
  1.5 0.7 copy-start.7
  38.7 2.7 %collective-permute-start = (bf16[16,33,8,128]{3,2,1,0:T(8,128)(2,1)S(1)}, bf16[16,33,8,128]{3,2,1,0:T(8,128)(2,1)S(1)}, u32[]{:S(2)}, u32[]{:S(2)}) collective-permute-start(bf16[16,33,8,128]{3,2,1,0:T(8,128)(2,1)S(1)} %all_to_all.20.own_ref), channel_id=1, source_target_pairs={{0,1},{1,0},{2,3},{3,2},{4,5},{5,4},{6,7},{7,6},{8,9},{9,8},{10,11... | collective-permute-start | bytes 3244040 | tf_op jit(solution)/shard_map/ppermute | solution.py:165
  41.4 2.2 %copy-start.1 = (bf16[8192,256]{1,0:T(8,128)(2,1)S(1)}, bf16[8192,256]{1,0:T(8,128)(2,1)}, u32[]{:S(2)}) copy-start(bf16[8192,256]{1,0:T(8,128)(2,1)} %w_ref.2) | copy-start | bytes 12582916
  45.1 11.8 %all-to-all-start.1 = ((bf16[32,2,128]{2,1,0:T(2,128)(2,1)}), bf16[32,2,128]{2,1,0:T(2,128)(2,1)S(1)}, u32[]{:S(2)}, u32[]{:S(2)}) async-start(bf16[32,2,128]{2,1,0:T(2,128)(2,1)} %bitcast), calls=%async_computation.1 | async-start | bytes 32768 | tf_op jit(solution)/shard_map/all_to_all | solution.py:179
  49.0 2.5 %copy-start = (bf16[1280,2048]{1,0:T(8,128)(2,1)S(1)}, bf16[1280,2048]{1,0:T(8,128)(2,1)}, u32[]{:S(2)}) copy-start(bf16[1280,2048]{1,0:T(8,128)(2,1)} %w_kv_ref.1) | copy-start | bytes 15728644
  51.5 1.4 %copy-start.4 = (bf16[640,1280]{1,0:T(8,128)(2,1)S(1)}, bf16[640,1280]{1,0:T(8,128)(2,1)}, u32[]{:S(2)}) copy-start(bf16[640,1280]{1,0:T(8,128)(2,1)} %w_eo_ref.1) | copy-start | bytes 4915204
  57.0 1.6 %copy-start.3 = (bf16[1,4,128,2048]{3,2,1,0:T(8,128)(2,1)S(1)}, bf16[1,4,128,2048]{3,2,1,0:T(8,128)(2,1)}, u32[]{:S(2)}) copy-start(bf16[1,4,128,2048]{3,2,1,0:T(8,128)(2,1)} %cache_ref.1) | copy-start | bytes 6291460
  59.4 31.1 %copy-start.6 = (bf16[1,8192]{1,0:T(2,128)(2,1)S(1)}, bf16[1,8192]{1,0:T(2,128)(2,1)}, u32[]{:S(2)}) copy-start(bf16[1,8192]{1,0:T(2,128)(2,1)} %dec_x_ref.3) | copy-start | bytes 49156
  76.4 1.5 %collective-permute-start.1 = (bf16[16,8,8,128]{3,2,1,0:T(8,128)(2,1)S(1)}, bf16[16,8,8,128]{3,2,1,0:T(8,128)(2,1)S(1)}, u32[]{:S(2)}, u32[]{:S(2)}) collective-permute-start(bf16[16,8,8,128]{3,2,1,0:T(8,128)(2,1)S(1)} %all_to_all.21.own_ref), channel_id=1, source_target_pairs={{0,1},{1,0},{2,3},{3,2},{4,5},{5,4},{6,7},{7,6},{8,9},{9,8},{10,11... | collective-permute-start | bytes 786440 | tf_op jit(solution)/shard_map/ppermute | solution.py:165
  77.9 2.2 %copy-start.2 = (bf16[8192,256]{1,0:T(8,128)(2,1)S(1)}, bf16[8192,256]{1,0:T(8,128)(2,1)}, u32[]{:S(2)}) copy-start(bf16[8192,256]{1,0:T(8,128)(2,1)} %w_ref.3) | copy-start | bytes 12582916

commit v2 on v1

v2 whole, which is shorter than its diff:
```python
import jax
import jax.numpy as jnp
from jax import lax
from jax.experimental import pallas as pl
from jax.experimental.pallas import tpu as pltpu
from jax.sharding import PartitionSpec as P

EH = 8
EHD = 80
HD = 128
TILE_LEN = 128
LANES = 128
SUB = 8
SHARES = 4
VMEM = pl.BlockSpec(memory_space=pltpu.VMEM)
ANY = pl.BlockSpec(memory_space=pl.ANY)
SMEM = pl.BlockSpec(memory_space=pltpu.SMEM)
LONG = pl.CostEstimate(flops=10**10, transcendentals=0, bytes_accessed=10**7)
F32 = jnp.float32
BF16 = jnp.bfloat16


def params(mib):
    return pltpu.CompilerParams(vmem_limit_bytes=mib * 1024 * 1024)


def pack_kernel(dec_x_hbm, qkv_hbm, enc_x_hbm, out_ref, dec_x_ref, qkv_ref, enc_x_ref, rows_ref, sems):
    copies = [
        pltpu.make_async_copy(src, dst, sems.at[i])
        for i, (src, dst) in enumerate(((dec_x_hbm, dec_x_ref), (qkv_hbm, qkv_ref), (enc_x_hbm, enc_x_ref)))
    ]
    for copy in copies:
        copy.start()
    for copy in copies:
        copy.wait()
    x = dec_x_ref[...].astype(F32)
    scale = lax.rsqrt(jnp.mean(x * x, axis=-1, keepdims=True) + 1e-05)
    normed = x * scale
    groups = x.shape[1] // LANES
    for k in range(groups):
        rows_ref[k : k + 1, :] = normed[:, k * LANES : (k + 1) * LANES]
    copies = out_ref.shape[0]

    def put(place, block, to):
        block = block.astype(BF16)
        for copy in to:
            out_ref[copy, place] = block

    for i in range(groups // SUB):
        put(i, rows_ref[i * SUB : (i + 1) * SUB, :], range(copies))
    blocks = []
    for i in range(3):
        part = qkv_ref[i]
        blocks += [part[:, t * LANES : (t + 1) * LANES] for t in range(part.shape[1] // LANES)]
    enc_x = enc_x_ref[...]
    blocks += [enc_x[:, t * LANES : (t + 1) * LANES] for t in range(enc_x.shape[1] // LANES)]
    share = len(blocks) // SHARES
    first = groups // SUB
    for i, block in enumerate(blocks[share * SHARES :]):
        put(first + i, block, range(copies))
    first = out_ref.shape[1] - share
    for i, block in enumerate(blocks[: share * SHARES]):
        put(first + i % share, block, range(i // share, copies, SHARES))


def regroup(ref, rows_ref, x_ref):
    chips = ref.shape[0]
    for i in range(x_ref.shape[1] // (SUB * LANES)):
        rows_ref[...] = ref[:, i].astype(F32).reshape(chips * SUB, LANES)
        for j in range(SUB):
            k = i * SUB + j
            x_ref[:, k * LANES : (k + 1) * LANES] = rows_ref[pl.ds(j, chips, stride=SUB), :].astype(BF16)


def own_kernel(own_ref, w_ref, result_ref, rows_ref, x_ref):
    regroup(own_ref, rows_ref, x_ref)
    result_ref[...] = jnp.dot(x_ref[...], w_ref[...], preferred_element_type=F32)


def other_kernel(other_ref, result_ref, w_ref, out_ref, rows_ref, x_ref):
    regroup(other_ref, rows_ref, x_ref)
    result = jnp.dot(x_ref[...], w_ref[...], preferred_element_type=F32)
    core = lax.rem(lax.axis_index("seq"), 2)
    parts, lanes = out_ref.shape[2:]
    for half, where in ((result_ref[...], core), (result, 1 - core)):
        half = jnp.stack([half[:, p * lanes : (p + 1) * lanes] for p in range(parts)], axis=1)
        out_ref[:, pl.ds(where, 1)] = half.astype(BF16)[:, None]


def share_kernel(own_ref, out_ref):
    share = out_ref.shape[1]
    out_ref[...] = own_ref[:, own_ref.shape[1] - share :]


def pass_kernel(query_ref, out_ref):
    out_ref[...] = query_ref[...]


def merge_kernel(query_ref, own_ref, own_1, own_2, own_3, out_ref):
    share = own_1.shape[1]
    last = own_ref.shape[1] - share
    place = lax.rem(lax.axis_index("seq") // 2, SHARES)

    def merge(block):
        return block.astype(F32).reshape(-1, LANES).astype(BF16)

    for j, ref in enumerate((own_ref, own_1, own_2, own_3)):
        start = jnp.bitwise_xor(place, j) * share
        for i in range(share):
            out_ref[start + i] = merge(ref[:, (last if j == 0 else 0) + i])
    for i in range(out_ref.shape[0] - share * SHARES):
        out_ref[share * SHARES + i] = merge(own_ref[:, last - 1 - i])


def encode_kernel(tile_ref, own_ref, other_ref, w_eo_ref, w_kv_ref, out_ref):
    width = w_eo_ref.shape[0]
    model = w_eo_ref.shape[1]
    tiles = width // LANES
    half = TILE_LEN // 2
    start = pl.multiple_of(tile_ref[0] * half, half)

    def tile_rows(place):
        return jnp.concatenate([own_ref[place, pl.ds(start, half)], other_ref[place, pl.ds(start, half)]], axis=0)

    def every(place):
        return jnp.concatenate([own_ref[place], other_ref[place]], axis=0)

    query = jnp.concatenate([tile_rows(t) for t in range(tiles)], axis=1)
    keys = jnp.concatenate([every(tiles + t) for t in range(tiles)], axis=1)
    values = jnp.concatenate([every(2 * tiles + t) for t in range(tiles)], axis=1)
    column = lax.broadcasted_iota(jnp.int32, (TILE_LEN, width), 1)
    attn = [jnp.zeros((TILE_LEN, LANES), F32) for _ in range(tiles)]
    for h in range(EH):
        lo, hi = h * EHD // LANES, (h * EHD + EHD - 1) // LANES + 1
        span = slice(lo * LANES, hi * LANES)
        inside = (column[:, span] >= h * EHD) & (column[:, span] < (h + 1) * EHD)
        head = jnp.where(inside, query[:, span], jnp.zeros((), BF16))
        scores = lax.dot_general(head, keys[:, span], (((1,), (1,)), ((), ())), preferred_element_type=F32)
        scores = scores * EHD ** (-0.5)
        powers = jnp.exp(scores - jnp.max(scores, axis=-1, keepdims=True))
        weights = (powers / jnp.sum(powers, axis=-1, keepdims=True)).astype(BF16)
        part = jnp.dot(weights, values[:, span], preferred_element_type=F32)
        part = jnp.where(inside, part, 0.0)
        for t in range(lo, hi):
            attn[t] = attn[t] + part[:, (t - lo) * LANES : (t - lo + 1) * LANES]
    attn = jnp.concatenate(attn, axis=1).astype(BF16)
    enc_x = jnp.concatenate([tile_rows(3 * tiles + t).astype(F32) for t in range(model // LANES)], axis=1)
    resid = enc_x + jnp.dot(attn, w_eo_ref[...], preferred_element_type=F32)
    center = resid - jnp.mean(resid, axis=-1, keepdims=True)
    spread = jnp.mean(center * center, axis=-1, keepdims=True)
    features = (center * lax.rsqrt(spread + 1e-05)).astype(BF16)
    out_ref[...] = jnp.dot(features, w_kv_ref[...], preferred_element_type=F32).astype(BF16)


def attend_kernel(count_ref, query_ref, cache_ref, new_ref, out_ref):
    filled = count_ref[0]
    slots, length, both = cache_ref.shape
    width = both // 2
    kv_heads = width // HD
    per = query_ref.shape[0] // kv_heads
    query = query_ref[...]
    scores = []
    for g in range(kv_heads):
        head = query[g * per : (g + 1) * per]
        cols = slice(g * HD, (g + 1) * HD)
        keys = cache_ref[:, :, cols].reshape(slots * length, HD)
        old = lax.dot_general(head, keys, (((1,), (1,)), ((), ())), preferred_element_type=F32)
        new = lax.dot_general(head, new_ref[:, cols], (((1,), (1,)), ((), ())), preferred_element_type=F32)
        scores.append(jnp.concatenate([old, new], axis=1))
    scores = jnp.concatenate(scores, axis=0) * HD ** (-0.5)
    slot = lax.broadcasted_iota(jnp.int32, scores.shape, 1) // length
    scores = jnp.where((slot < filled) | (slot == slots), scores, -jnp.inf)
    powers = jnp.exp(scores - jnp.max(scores, axis=-1, keepdims=True))
    weights = (powers / jnp.sum(powers, axis=-1, keepdims=True)).astype(BF16)
    copies = out_ref.shape[0]
    for g in range(kv_heads):
        mine = weights[g * per : (g + 1) * per]
        cols = slice(width + g * HD, width + (g + 1) * HD)
        values = cache_ref[:, :, cols].reshape(slots * length, HD)
        part = jnp.dot(mine[:, : slots * length], values, preferred_element_type=F32)
        part = part + jnp.dot(mine[:, slots * length :], new_ref[:, cols], preferred_element_type=F32)
        part = part.astype(BF16)
        for copy in range(copies):
            out_ref[copy, g] = part


def finish_kernel(attn_ref, dec_x_ref, out_ref):
    attn = attn_ref[...].astype(F32)
    for k in range(attn.shape[0]):
        cols = slice(k * LANES, (k + 1) * LANES)
        out_ref[:, cols] = (dec_x_ref[:, cols].astype(F32) + attn[k : k + 1]).astype(BF16)


def solution(mesh):
    devices = mesh.shape["seq"]
    chips = devices // 2
    across = [[2 * chip + core for chip in range(chips)] for core in range(2)]
    swap = [(i, i ^ 1) for i in range(devices)]

    def gather(copies):
        own = lax.all_to_all(copies, "seq", 0, 0, tiled=True, axis_index_groups=across)
        return own, lax.ppermute(own, "seq", swap)

    def project(own, other, weight):
        depth, cols = weight.shape
        lanes = min(cols, LANES)
        scratch = [pltpu.VMEM((chips * SUB, LANES), F32), pltpu.VMEM((chips, depth), BF16)]
        result = pl.pallas_call(
            own_kernel,
            out_shape=jax.ShapeDtypeStruct((chips, cols), F32),
            in_specs=[VMEM, VMEM],
            out_specs=VMEM,
            scratch_shapes=scratch,
            compiler_params=params(4),
            cost_estimate=LONG,
        )(own, weight)
        out = pl.pallas_call(
            other_kernel,
            out_shape=jax.ShapeDtypeStruct((chips, 2, cols // lanes, lanes), BF16),
            in_specs=[VMEM] * 3,
            out_specs=VMEM,
            scratch_shapes=scratch,
            compiler_params=params(4),
            cost_estimate=LONG,
        )(other, result, weight)
        sent = out.reshape(devices, cols // lanes, lanes)
        return lax.all_to_all(sent, "seq", 0, 0, tiled=True).reshape(-1, LANES)

    def local(enc_x, enc_qkv, w_eo, w_kv, dec_x, w_q, w_o, cache_kv, doc_tile, cached_count):
        qkv = enc_qkv.transpose(1, 0, 2)
        blocks = (enc_qkv.size + enc_x.size) // (SUB * LANES)
        share = blocks // SHARES
        groups = dec_x.size // (SUB * LANES) + blocks - share * (SHARES - 1)
        packed = pl.pallas_call(
            pack_kernel,
            out_shape=jax.ShapeDtypeStruct((chips, groups, SUB, LANES), BF16),
            in_specs=[ANY] * 3,
            out_specs=VMEM,
            scratch_shapes=[
                pltpu.VMEM(dec_x.shape, BF16),
                pltpu.VMEM(qkv.shape, BF16),
                pltpu.VMEM(enc_x.shape, BF16),
                pltpu.VMEM((dec_x.shape[1] // LANES, LANES), F32),
                pltpu.SemaphoreType.DMA((3,)),
            ],
            compiler_params=params(56),
            cost_estimate=LONG,
        )(dec_x, qkv, enc_x)
        own, other = gather(packed)
        mine = pl.pallas_call(
            share_kernel,
            out_shape=jax.ShapeDtypeStruct((chips, share, SUB, LANES), BF16),
            in_specs=[VMEM],
            out_specs=VMEM,
            compiler_params=params(1),
        )(own)
        shares = [lax.ppermute(mine, "seq", [(i, i ^ (2 * j)) for i in range(devices)]) for j in range(1, SHARES)]
        query = project(own, other, w_q)
        query = pl.pallas_call(
            pass_kernel,
            out_shape=jax.ShapeDtypeStruct(query.shape, BF16),
            in_specs=[VMEM],
            out_specs=VMEM,
            compiler_params=params(1),
        )(query)
        merged = pl.pallas_call(
            merge_kernel,
            out_shape=jax.ShapeDtypeStruct((blocks, chips * SUB, LANES), BF16),
            in_specs=[VMEM] * 5,
            out_specs=VMEM,
            compiler_params=params(2),
            cost_estimate=LONG,
        )(query, own, *shares)
        new_kv = pl.pallas_call(
            encode_kernel,
            out_shape=jax.ShapeDtypeStruct((TILE_LEN, w_kv.shape[1]), BF16),
            in_specs=[SMEM] + [VMEM] * 4,
            out_specs=VMEM,
            compiler_params=params(12),
            cost_estimate=LONG,
        )(doc_tile, merged, lax.ppermute(merged, "seq", swap), w_eo, w_kv)
        heads = query.shape[0]
        copies = pl.pallas_call(
            attend_kernel,
            out_shape=jax.ShapeDtypeStruct((chips, heads // SUB, SUB, LANES), BF16),
            in_specs=[SMEM] + [VMEM] * 3,
            out_specs=VMEM,
            compiler_params=params(4),
            cost_estimate=LONG,
        )(cached_count, query, cache_kv[0], new_kv)
        own, other = gather(copies)
        attn_out = project(own, other, w_o)
        return pl.pallas_call(
            finish_kernel,
            out_shape=jax.ShapeDtypeStruct(dec_x.shape, BF16),
            in_specs=[VMEM] * 2,
            out_specs=VMEM,
            compiler_params=params(2),
            cost_estimate=LONG,
        )(attn_out, dec_x)

    return jax.shard_map(
        local,
        mesh=mesh,
        in_specs=(
            P(("group", "seq"), None),
            P(("group", "seq"), None, None),
            P(),
            P(),
            P(("group", "seq"), None),
            P(None, "seq"),
            P(None, "seq"),
            P(("group", "seq"), None, None, None),
            P(("group", "seq")),
            P(("group", "seq")),
        ),
        out_specs=P(("group", "seq"), None),
        check_vma=False,
    )
```

time: 91.9 us -> 74.3 us (0.81)
  local copies, waits for them, and re-layouts: 12.1 us -> 0.47 us
  blocking collectives: 62.6 us -> 54.9 us
  Pallas kernels: 8.29 us -> 10.7 us
  waiting for transfers between devices: 4.24 us -> 2.26 us
  starting transfers between devices: 2.55 us -> 3.63 us
    all_to_all x2, blocking collectives: 53.1 us -> 35.7 us  [gather(): lax.all_to_all(copies, 'seq', 0, 0, tiled=True, axis_index_groups=across)]
    unnamed x17 -> x14, local copies, waits for them, and re-layouts: 12.1 us -> 0.47 us
    all_to_all x1 -> x2, blocking collectives: 9.48 us -> 19.2 us  [project(): return lax.all_to_all(sent, 'seq', 0, 0, tiled=True).reshape(-1, LANES)]
    ppermute x0 -> x4, starting transfers between devices: none -> 3.62 us  [the longest x3 3.55 us: local(): lax.ppermute(mine, 'seq', [(i, i ^ 2 * j) for i in range(devices)])]
    all_to_all x1 -> x0, starting transfers between devices: 2.54 us -> none  [project(): return lax.all_to_all(sent, 'seq', 0, 0, tiled=True).reshape(-1, LANES)]
    ppermute x2, waiting for transfers between devices: 4.24 us -> 1.92 us  [gather(): return (own, lax.ppermute(own, 'seq', swap))]
    pallas_call x1, Pallas kernels: 0.24 us -> 1.94 us  [local(): pl.pallas_call(pack_kernel, out_shape=jax.ShapeDtypeStruct((chips, groups...]
    pallas_call x2 -> x7, Pallas kernels: 2.49 us -> 3.19 us  [the longest x2 1.56 us: project(): pl.pallas_call(other_kernel, out_shape=jax.ShapeDtypeStruct((chips, 2, co...]
  transfers between devices with their start and end apart: 3 -> 6, of which waited for: 2 -> 3; matrix products, arithmetic and copies ran while one was open for 0% -> 0% of each run, Pallas kernels for 4% -> 3%
where the time goes in v2:
time: 74.3 us; the launch traced here: 74.1 us
  blocking collectives  54.9 us (74%)
  Pallas kernels  10.7 us (14%)
  starting transfers between devices  3.63 us (5%)
  waiting for transfers between devices  2.26 us (3%)
  between operations  2.1 us (3%)
    all_to_all x2, blocking collectives, gather(): lax.all_to_all(copies, 'seq', 0, 0, tiled=True, axis_index_groups=across)  35.7 us
    all_to_all x2, blocking collectives, project(): return lax.all_to_all(sent, 'seq', 0, 0, tiled=True).reshape(-1, LANES)  19.2 us
    pallas_call x1, Pallas kernels, local(): pl.pallas_call(encode_kernel, out_shape=jax.ShapeDtypeStruct((TILE_LEN, w...  4.04 us
    ppermute x3, starting transfers between devices, local(): lax.ppermute(mine, 'seq', [(i, i ^ 2 * j) for i in range(devices)])  3.55 us
    pallas_call x1, Pallas kernels, local(): pl.pallas_call(pack_kernel, out_shape=jax.ShapeDtypeStruct((chips, groups...  1.94 us
    ppermute x2, waiting for transfers between devices, gather(): return (own, lax.ppermute(own, 'seq', swap))  1.92 us
    pallas_call x2, Pallas kernels, project(): pl.pallas_call(other_kernel, out_shape=jax.ShapeDtypeStruct((chips, 2, co...  1.56 us
  transfers between devices with their start and end apart: 6, of which 3 were waited for; matrix products, arithmetic and copies ran while one was open for 0% of the time, Pallas kernels for 3%

profile of v2, /device:TPU:0, one launch (start us, length us, event | category | flops | bytes accessed | tf_op | source)
XLA Modules:
  0.0 74.1 jit_solution(8099310131154898587)
XLA Ops:
  0.0 1.9 %shard_map.100 = bf16[16,15,8,128]{3,2,1,0:T(8,128)(2,1)} custom-call(bf16[1,8192]{1,0:T(2,128)(2,1)} %dec_x_ref.1, bf16[3,8,640]{2,1,0:T(8,128)(2,1)} %bitcast.13, bf16[8,1280]{1,0:T(8,128)(2,1)} %enc_x_hbm.1), custom_call_target="tpu_custom_call" | custom-call | flops 10000000000 | bytes 10000000 | tf_op jit(solution)/shard_map/pallas_call | solution.py:234
  2.0 22.8 %all_to_all.20.own_ref = bf16[16,15,8,128]{3,2,1,0:T(8,128)(2,1)S(1)} all-to-all(bf16[16,15,8,128]{3,2,1,0:T(8,128)(2,1)} %shard_map.100), channel_id=1, replica_groups={{0,2,4,6,8,10,12,14,16,18,20,22,24,26,28,30},{1,3,5,7,9,11,13,15,17,19,..., dimensions={0} | all-to-all | bytes 983040 | tf_op jit(solution)/shard_map/all_to_all | solution.py:201
  24.8 0.6 collective-permute-start.1
  25.4 0.9 %collective-permute-start.2 = (bf16[16,6,8,128]{3,2,1,0:T(8,128)(2,1)S(1)}, bf16[16,6,8,128]{3,2,1,0:T(8,128)(2,1)S(1)}, u32[]{:S(2)}, u32[]{:S(2)}) collective-permute-start(bf16[16,6,8,128]{3,2,1,0:T(8,128)(2,1)S(1)} %shard_map.104), channel_id=1, source_target_pairs={{0,4},{1,5},{2,6},{3,7},{4,0},{5,1},{6,2},{7,3},{8,12},{9,13},{10,... | collective-permute-start | bytes 589832 | tf_op jit(solution)/shard_map/ppermute | solution.py:257
  26.3 2.0 %collective-permute-start.3 = (bf16[16,6,8,128]{3,2,1,0:T(8,128)(2,1)S(1)}, bf16[16,6,8,128]{3,2,1,0:T(8,128)(2,1)S(1)}, u32[]{:S(2)}, u32[]{:S(2)}) collective-permute-start(bf16[16,6,8,128]{3,2,1,0:T(8,128)(2,1)S(1)} %shard_map.104), channel_id=1, source_target_pairs={{0,6},{1,7},{2,4},{3,5},{4,2},{5,3},{6,0},{7,1},{8,14},{9,15},{10,... | collective-permute-start | bytes 589832 | tf_op jit(solution)/shard_map/ppermute | solution.py:257
  28.3 0.0 collective-permute-start
  28.4 0.0 copy-done
  28.4 0.7 shard_map.101.result_ref
  29.1 1.1 %collective-permute-done.other_ref = bf16[16,15,8,128]{3,2,1,0:T(8,128)(2,1)S(1)} collective-permute-done((bf16[16,15,8,128]{3,2,1,0:T(8,128)(2,1)S(1)}, bf16[16,15,8,128]{3,2,1,0:T(8,128)(2,1)S(1)}, u32[]{:S(2)}, u32[]{:S(2)}) %collective-permute-start) | collective-permute-done | bytes 491552 | tf_op jit(solution)/shard_map/ppermute | solution.py:202
  30.2 0.8 %shard_map.102 = bf16[16,2,2,128]{3,2,1,0:T(2,128)(2,1)S(1)} custom-call(bf16[16,15,8,128]{3,2,1,0:T(8,128)(2,1)S(1)} %collective-permute-done.other_ref, f32[16,256]{1,0:T(8,128)S(1)} %shard_map.101.result_ref, bf16[8192,256]{1,0:T(8,128)(2,1)S(1)} %copy-done), custom_call_target="tpu_custom_call" | custom-call | flops 10000000000 | bytes 10000000 | tf_op jit(solution)/shard_map/pallas_call | solution.py:217
  31.0 9.8 %all_to_all.21 = bf16[32,2,128]{2,1,0:T(2,128)(2,1)S(1)} all-to-all(bf16[32,2,128]{2,1,0:T(2,128)(2,1)S(1)} %bitcast.7), channel_id=1, replica_groups=mesh['group'=1,'seq'=32] {'seq'}, dimensions={0} | all-to-all | bytes 32768 | tf_op jit(solution)/shard_map/all_to_all | solution.py:227
  40.8 0.0 collective-permute-done.1.own_1
  40.8 0.0 collective-permute-done.2.own_2
  40.8 0.0 collective-permute-done.3.own_3
  40.8 0.1 shard_map.105.own_ref
  41.0 0.1 collective-permute-start.4
  43.0 0.0 copy-start.2
  43.0 0.3 collective-permute-done.4.other_ref
  43.4 0.0 slice-done
  43.4 0.0 slice-done.1
  43.4 0.4 copy-done.3
  43.8 4.0 %shard_map.106.new_ref = bf16[128,2048]{1,0:T(8,128)(2,1)S(1)} custom-call(s32[1]{0:T(128)S(6)} %copy.11.tile_ref, bf16[25,128,128]{2,1,0:T(8,128)(2,1)S(1)} %shard_map.105.own_ref, bf16[25,128,128]{2,1,0:T(8,128)(2,1)S(1)} %collective-permute-done.4.other_ref, bf16[640,1280]{1,0:T(8,128)(2,1)S(1)} %copy-done.3, bf16[1280,2048]{1,0:T(8,128)(2,1)S(1)} %bitcast.11), custom_call_target="tpu_custom_call" | custom-call | flops 10000000000 | bytes 10000000 | tf_op jit(solution)/shard_map/pallas_call | solution.py:274
  47.9 0.0 copy-done.2
  47.9 0.0 copy-start.1
  47.9 0.9 %shard_map.107 = bf16[16,8,8,128]{3,2,1,0:T(8,128)(2,1)S(1)} custom-call(s32[1]{0:T(128)S(6)} %copy.12.count_ref, bf16[64,128]{1,0:T(8,128)(2,1)S(1)} %shard_map.103.query_ref, bf16[4,128,2048]{2,1,0:T(8,128)(2,1)S(1)} %bitcast.12, bf16[128,2048]{1,0:T(8,128)(2,1)S(1)} %shard_map.106.new_ref), custom_call_target="tpu_custom_call" | custom-call | flops 10000000000 | bytes 10000000 | tf_op jit(solution)/shard_map/pallas_call | solution.py:283
  48.7 12.9 %all_to_all.22.own_ref = bf16[16,8,8,128]{3,2,1,0:T(8,128)(2,1)S(1)} all-to-all(bf16[16,8,8,128]{3,2,1,0:T(8,128)(2,1)S(1)} %shard_map.107), channel_id=1, replica_groups={{0,2,4,6,8,10,12,14,16,18,20,22,24,26,28,30},{1,3,5,7,9,11,13,15,17,19,..., dimensions={0} | all-to-all | bytes 524288 | tf_op jit(solution)/shard_map/all_to_all | solution.py:201
  61.6 0.0 collective-permute-start.5
  61.6 0.7 shard_map.108.result_ref
  62.4 0.8 %collective-permute-done.5.other_ref = bf16[16,8,8,128]{3,2,1,0:T(8,128)(2,1)S(1)} collective-permute-done((bf16[16,8,8,128]{3,2,1,0:T(8,128)(2,1)S(1)}, bf16[16,8,8,128]{3,2,1,0:T(8,128)(2,1)S(1)}, u32[]{:S(2)}, u32[]{:S(2)}) %collective-permute-start.5) | collective-permute-done | bytes 262176 | tf_op jit(solution)/shard_map/ppermute | solution.py:202
  63.2 0.8 %shard_map.109 = bf16[16,2,2,128]{3,2,1,0:T(2,128)(2,1)S(1)} custom-call(bf16[16,8,8,128]{3,2,1,0:T(8,128)(2,1)S(1)} %collective-permute-done.5.other_ref, f32[16,256]{1,0:T(8,128)S(1)} %shard_map.108.result_ref, bf16[8192,256]{1,0:T(8,128)(2,1)S(1)} %copy-done.1), custom_call_target="tpu_custom_call" | custom-call | flops 10000000000 | bytes 10000000 | tf_op jit(solution)/shard_map/pallas_call | solution.py:217
  64.0 9.4 %all_to_all.23 = bf16[32,2,128]{2,1,0:T(2,128)(2,1)S(1)} all-to-all(bf16[32,2,128]{2,1,0:T(2,128)(2,1)S(1)} %bitcast.8), channel_id=1, replica_groups=mesh['group'=1,'seq'=32] {'seq'}, dimensions={0} | all-to-all | bytes 32768 | tf_op jit(solution)/shard_map/all_to_all | solution.py:227
  73.4 0.7 shard_map.110
  (10 shorter events, 0.0 us)
Async XLA Ops:
  0.0 28.4 %copy-start = (bf16[8192,256]{1,0:T(8,128)(2,1)S(1)}, bf16[8192,256]{1,0:T(8,128)(2,1)}, u32[]{:S(2)}) copy-start(bf16[8192,256]{1,0:T(8,128)(2,1)} %w_ref.5) | copy-start | bytes 12582916
  24.8 16.0 %collective-permute-start.1 = (bf16[16,6,8,128]{3,2,1,0:T(8,128)(2,1)S(1)}, bf16[16,6,8,128]{3,2,1,0:T(8,128)(2,1)S(1)}, u32[]{:S(2)}, u32[]{:S(2)}) collective-permute-start(bf16[16,6,8,128]{3,2,1,0:T(8,128)(2,1)S(1)} %shard_map.104), channel_id=1, source_target_pairs={{0,2},{1,3},{2,0},{3,1},{4,6},{5,7},{6,4},{7,5},{8,10},{9,11},{10,... | collective-permute-start | bytes 589832 | tf_op jit(solution)/shard_map/ppermute | solution.py:257
  25.4 15.4 %collective-permute-start.2 = (bf16[16,6,8,128]{3,2,1,0:T(8,128)(2,1)S(1)}, bf16[16,6,8,128]{3,2,1,0:T(8,128)(2,1)S(1)}, u32[]{:S(2)}, u32[]{:S(2)}) collective-permute-start(bf16[16,6,8,128]{3,2,1,0:T(8,128)(2,1)S(1)} %shard_map.104), channel_id=1, source_target_pairs={{0,4},{1,5},{2,6},{3,7},{4,0},{5,1},{6,2},{7,3},{8,12},{9,13},{10,... | collective-permute-start | bytes 589832 | tf_op jit(solution)/shard_map/ppermute | solution.py:257
  26.3 14.5 %collective-permute-start.3 = (bf16[16,6,8,128]{3,2,1,0:T(8,128)(2,1)S(1)}, bf16[16,6,8,128]{3,2,1,0:T(8,128)(2,1)S(1)}, u32[]{:S(2)}, u32[]{:S(2)}) collective-permute-start(bf16[16,6,8,128]{3,2,1,0:T(8,128)(2,1)S(1)} %shard_map.104), channel_id=1, source_target_pairs={{0,6},{1,7},{2,4},{3,5},{4,2},{5,3},{6,0},{7,1},{8,14},{9,15},{10,... | collective-permute-start | bytes 589832 | tf_op jit(solution)/shard_map/ppermute | solution.py:257
  28.3 1.9 %collective-permute-start = (bf16[16,15,8,128]{3,2,1,0:T(8,128)(2,1)S(1)}, bf16[16,15,8,128]{3,2,1,0:T(8,128)(2,1)S(1)}, u32[]{:S(2)}, u32[]{:S(2)}) collective-permute-start(bf16[16,15,8,128]{3,2,1,0:T(8,128)(2,1)S(1)} %all_to_all.20.own_ref), channel_id=1, source_target_pairs={{0,1},{1,0},{2,3},{3,2},{4,5},{5,4},{6,7},{7,6},{8,9},{9,8},{10,11... | collective-permute-start | bytes 1474568 | tf_op jit(solution)/shard_map/ppermute | solution.py:202
  40.8 2.6 %slice-start = ((s8[5242880]{0:T(1024)(128)(4,1)}), s8[4194304]{0:T(1024)(128)(4,1)S(1)}, s32[]{:S(2)}) async-start(s8[5242880]{0:T(1024)(128)(4,1)} %bitcast.10), calls=%async_computation.4 | async-start | bytes 8388608
  40.8 2.6 %slice-start.1 = ((s8[5242880]{0:T(1024)(128)(4,1)}), s8[1048576]{0:T(1024)(128)(4,1)S(1)}, s32[]{:S(2)}) async-start(s8[5242880]{0:T(1024)(128)(4,1)} %bitcast.10), calls=%async_computation.5 | async-start | bytes 2097152
  40.8 3.0 %copy-start.3 = (bf16[640,1280]{1,0:T(8,128)(2,1)S(1)}, bf16[640,1280]{1,0:T(8,128)(2,1)}, u32[]{:S(2)}) copy-start(bf16[640,1280]{1,0:T(8,128)(2,1)} %w_eo_ref.1) | copy-start | bytes 4915204
  41.0 2.4 %collective-permute-start.4 = (bf16[25,128,128]{2,1,0:T(8,128)(2,1)S(1)}, bf16[25,128,128]{2,1,0:T(8,128)(2,1)S(1)}, u32[]{:S(2)}, u32[]{:S(2)}) collective-permute-start(bf16[25,128,128]{2,1,0:T(8,128)(2,1)S(1)} %shard_map.105.own_ref), channel_id=1, source_target_pairs={{0,1},{1,0},{2,3},{3,2},{4,5},{5,4},{6,7},{7,6},{8,9},{9,8},{10,11... | collective-permute-start | bytes 2457608 | tf_op jit(solution)/shard_map/ppermute | solution.py:281
  43.0 4.8 %copy-start.2 = (bf16[1,4,128,2048]{3,2,1,0:T(8,128)(2,1)S(1)}, bf16[1,4,128,2048]{3,2,1,0:T(8,128)(2,1)}, u32[]{:S(2)}) copy-start(bf16[1,4,128,2048]{3,2,1,0:T(8,128)(2,1)} %param.17) | copy-start | bytes 6291460
  47.9 13.8 %copy-start.1 = (bf16[8192,256]{1,0:T(8,128)(2,1)S(1)}, bf16[8192,256]{1,0:T(8,128)(2,1)}, u32[]{:S(2)}) copy-start(bf16[8192,256]{1,0:T(8,128)(2,1)} %w_ref.7) | copy-start | bytes 12582916
  61.6 1.5 %collective-permute-start.5 = (bf16[16,8,8,128]{3,2,1,0:T(8,128)(2,1)S(1)}, bf16[16,8,8,128]{3,2,1,0:T(8,128)(2,1)S(1)}, u32[]{:S(2)}, u32[]{:S(2)}) collective-permute-start(bf16[16,8,8,128]{3,2,1,0:T(8,128)(2,1)S(1)} %all_to_all.22.own_ref), channel_id=1, source_target_pairs={{0,1},{1,0},{2,3},{3,2},{4,5},{5,4},{6,7},{7,6},{8,9},{9,8},{10,11... | collective-permute-start | bytes 786440 | tf_op jit(solution)/shard_map/ppermute | solution.py:202
  62.4 11.0 %copy-start.4 = (bf16[1,8192]{1,0:T(2,128)(2,1)S(1)}, bf16[1,8192]{1,0:T(2,128)(2,1)}, u32[]{:S(2)}) copy-start(bf16[1,8192]{1,0:T(2,128)(2,1)} %dec_x_ref.1) | copy-start | bytes 49156

commit v3 on v2

v3 whole, which is shorter than its diff:
```python
import functools

import jax
import jax.numpy as jnp
from jax import lax
from jax.experimental import pallas as pl
from jax.experimental.pallas import tpu as pltpu
from jax.sharding import PartitionSpec as P

EH = 8
EHD = 80
HD = 128
TILE_LEN = 128
LANES = 128
SUB = 8
SHARES = 4
CHUNK = 512
VMEM = pl.BlockSpec(memory_space=pltpu.VMEM)
ANY = pl.BlockSpec(memory_space=pl.ANY)
SMEM = pl.BlockSpec(memory_space=pltpu.SMEM)
LONG = pl.CostEstimate(flops=10**10, transcendentals=0, bytes_accessed=10**7)
F32 = jnp.float32
BF16 = jnp.bfloat16


def params(mib):
    return pltpu.CompilerParams(vmem_limit_bytes=mib * 1024 * 1024)


def pack_kernel(dec_x_hbm, qkv_hbm, enc_x_hbm, out_ref, dec_x_ref, qkv_ref, enc_x_ref, rows_ref, sems):
    copies = [
        pltpu.make_async_copy(src, dst, sems.at[i])
        for i, (src, dst) in enumerate(((dec_x_hbm, dec_x_ref), (qkv_hbm, qkv_ref), (enc_x_hbm, enc_x_ref)))
    ]
    for copy in copies:
        copy.start()
    for copy in copies:
        copy.wait()
    x = dec_x_ref[...].astype(F32)
    scale = lax.rsqrt(jnp.mean(x * x, axis=-1, keepdims=True) + 1e-05)
    normed = x * scale
    groups = x.shape[1] // LANES
    for k in range(groups):
        rows_ref[k : k + 1, :] = normed[:, k * LANES : (k + 1) * LANES]
    copies = out_ref.shape[0]

    def put(place, block, to):
        block = block.astype(BF16)
        for copy in to:
            out_ref[copy, place] = block

    halves = groups // SUB // 2
    for i in range(2 * halves):
        put(i % halves, rows_ref[i * SUB : (i + 1) * SUB, :], range(i // halves, copies, 2))
    blocks = []
    for i in range(3):
        part = qkv_ref[i]
        blocks += [part[:, t * LANES : (t + 1) * LANES] for t in range(part.shape[1] // LANES)]
    enc_x = enc_x_ref[...]
    blocks += [enc_x[:, t * LANES : (t + 1) * LANES] for t in range(enc_x.shape[1] // LANES)]
    share = len(blocks) // (2 * SHARES)
    for i, block in enumerate(blocks[2 * SHARES * share :]):
        put(halves + i, block, range(copies))
    first = out_ref.shape[1] - share
    for i, block in enumerate(blocks[: 2 * SHARES * share]):
        core, chip = divmod(i // share, SHARES)
        put(first + i % share, block, range(2 * chip + core, copies, 2 * SHARES))


def project_kernel(sent_ref, w_ref, mate_ref, *refs):
    out_ref, rows_ref, x_ref = refs[-3:]
    docs, half = x_ref.shape
    for i in range(half // (SUB * LANES)):
        rows_ref[...] = sent_ref[:, i].astype(F32).reshape(docs * SUB, LANES)
        for j in range(SUB):
            k = i * SUB + j
            x_ref[:, k * LANES : (k + 1) * LANES] = rows_ref[pl.ds(j, docs, stride=SUB), :].astype(BF16)
    core = lax.rem(lax.axis_index("seq"), 2)
    parts, lanes = out_ref.shape[2:]

    def multiply(side):
        for ref, place in ((w_ref, side), (mate_ref, 1 - side)):
            result = jnp.zeros((docs, ref.shape[1]), F32)
            for k in range(0, half, CHUNK):
                rows = slice(side * half + k, side * half + k + CHUNK)
                result += jnp.dot(x_ref[:, k : k + CHUNK], ref[rows, :], preferred_element_type=F32)
            result = jnp.stack([result[:, p * lanes : (p + 1) * lanes] for p in range(parts)], axis=1)
            out_ref[:, place] = result

    for side in range(2):
        pl.when(core == side)(functools.partial(multiply, side))


def add_halves(sums_ref, rows_ref):
    devices, cores, parts, _ = sums_ref.shape
    for chip in range(devices // 2):
        for core in range(cores):
            row = (chip * cores + core) * parts
            rows_ref[row : row + parts, :] = sums_ref[2 * chip, core] + sums_ref[2 * chip + 1, core]
    return rows_ref[...].astype(BF16)


def collect_kernel(sums_ref, out_ref, rows_ref):
    out_ref[...] = add_halves(sums_ref, rows_ref)


def share_kernel(own_ref, out_ref):
    share = out_ref.shape[1]
    out_ref[...] = own_ref[:, own_ref.shape[1] - share :]


def merge(block):
    return block.astype(F32).reshape(-1, LANES).astype(BF16)


def merge_kernel(query_ref, own_0, own_1, own_2, own_3, out_ref):
    share = own_0.shape[1]
    place = lax.rem(lax.axis_index("seq") // 2, SHARES)
    for j, ref in enumerate((own_0, own_1, own_2, own_3)):
        start = jnp.bitwise_xor(place, j) * share
        for i in range(share):
            out_ref[start + i] = merge(ref[:, i])


def encode_kernel(tile_ref, sent_ref, own_ref, other_ref, w_eo_ref, w_kv_ref, out_ref):
    width, model = w_eo_ref.shape
    tiles = width // LANES
    held = own_ref.shape[0]
    rest = 3 * tiles + model // LANES - 2 * held
    first = sent_ref.shape[1] - held // SHARES - rest
    core = lax.rem(lax.axis_index("seq"), 2)
    mine = pl.ds(pl.multiple_of(tile_ref[0] * TILE_LEN, TILE_LEN), TILE_LEN)

    def pick(place, rows):
        if place >= 2 * held:
            chunk = TILE_LEN // SUB
            block = sent_ref[pl.ds(tile_ref[0] * chunk, chunk), first + place - 2 * held]
            return merge(block)
        side, index = divmod(place, held)
        return jnp.where(core == side, own_ref[index, rows], other_ref[index, rows])

    every = slice(None)
    query = jnp.concatenate([pick(t, mine) for t in range(tiles)], axis=1)
    keys = jnp.concatenate([pick(tiles + t, every) for t in range(tiles)], axis=1)
    values = jnp.concatenate([pick(2 * tiles + t, every) for t in range(tiles)], axis=1)
    column = lax.broadcasted_iota(jnp.int32, (TILE_LEN, width), 1)
    attn = [jnp.zeros((TILE_LEN, LANES), F32) for _ in range(tiles)]
    for h in range(EH):
        lo, hi = h * EHD // LANES, (h * EHD + EHD - 1) // LANES + 1
        span = slice(lo * LANES, hi * LANES)
        inside = (column[:, span] >= h * EHD) & (column[:, span] < (h + 1) * EHD)
        head = jnp.where(inside, query[:, span], jnp.zeros((), BF16))
        scores = lax.dot_general(head, keys[:, span], (((1,), (1,)), ((), ())), preferred_element_type=F32)
        scores = scores * EHD ** (-0.5)
        powers = jnp.exp(scores - jnp.max(scores, axis=-1, keepdims=True))
        weights = (powers / jnp.sum(powers, axis=-1, keepdims=True)).astype(BF16)
        part = jnp.dot(weights, values[:, span], preferred_element_type=F32)
        part = jnp.where(inside, part, 0.0)
        for t in range(lo, hi):
            attn[t] = attn[t] + part[:, (t - lo) * LANES : (t - lo + 1) * LANES]
    attn = jnp.concatenate(attn, axis=1).astype(BF16)
    enc_x = jnp.concatenate([pick(3 * tiles + t, mine).astype(F32) for t in range(model // LANES)], axis=1)
    resid = enc_x + jnp.dot(attn, w_eo_ref[...], preferred_element_type=F32)
    center = resid - jnp.mean(resid, axis=-1, keepdims=True)
    spread = jnp.mean(center * center, axis=-1, keepdims=True)
    features = (center * lax.rsqrt(spread + 1e-05)).astype(BF16)
    out_ref[...] = jnp.dot(features, w_kv_ref[...], preferred_element_type=F32).astype(BF16)


def attend_kernel(count_ref, query_ref, cache_ref, new_ref, out_ref):
    filled = count_ref[0]
    slots, length, both = cache_ref.shape
    width = both // 2
    kv_heads = width // HD
    per = query_ref.shape[0] // kv_heads
    query = query_ref[...]
    scores = []
    for g in range(kv_heads):
        head = query[g * per : (g + 1) * per]
        cols = slice(g * HD, (g + 1) * HD)
        keys = cache_ref[:, :, cols].reshape(slots * length, HD)
        old = lax.dot_general(head, keys, (((1,), (1,)), ((), ())), preferred_element_type=F32)
        new = lax.dot_general(head, new_ref[:, cols], (((1,), (1,)), ((), ())), preferred_element_type=F32)
        scores.append(jnp.concatenate([old, new], axis=1))
    scores = jnp.concatenate(scores, axis=0) * HD ** (-0.5)
    slot = lax.broadcasted_iota(jnp.int32, scores.shape, 1) // length
    scores = jnp.where((slot < filled) | (slot == slots), scores, -jnp.inf)
    powers = jnp.exp(scores - jnp.max(scores, axis=-1, keepdims=True))
    weights = (powers / jnp.sum(powers, axis=-1, keepdims=True)).astype(BF16)
    copies = out_ref.shape[0]
    for g in range(kv_heads):
        mine = weights[g * per : (g + 1) * per]
        cols = slice(width + g * HD, width + (g + 1) * HD)
        values = cache_ref[:, :, cols].reshape(slots * length, HD)
        part = jnp.dot(mine[:, : slots * length], values, preferred_element_type=F32)
        part = part + jnp.dot(mine[:, slots * length :], new_ref[:, cols], preferred_element_type=F32)
        part = part.astype(BF16)
        halves = kv_heads // 2
        for copy in range(g // halves, copies, 2):
            out_ref[copy, g % halves] = part


def finish_kernel(attn_ref, dec_x_ref, out_ref):
    attn = attn_ref[...].astype(F32)
    for k in range(attn.shape[0]):
        cols = slice(k * LANES, (k + 1) * LANES)
        out_ref[:, cols] = (dec_x_ref[:, cols].astype(F32) + attn[k : k + 1]).astype(BF16)


def finish_sums_kernel(sums_ref, dec_x_ref, out_ref, rows_ref, attn_ref):
    attn_ref[...] = add_halves(sums_ref, rows_ref)
    finish_kernel(attn_ref, dec_x_ref, out_ref)


def solution(mesh):
    devices = mesh.shape["seq"]
    swap = [(i, i ^ 1) for i in range(devices)]

    def exchange(sent):
        return lax.all_to_all(sent, "seq", 0, 0, tiled=True)

    def project(copies, weight, mate, *ready):
        depth, cols = weight.shape
        lanes = min(cols, LANES)
        sums = pl.pallas_call(
            project_kernel,
            out_shape=jax.ShapeDtypeStruct((devices, 2, cols // lanes, lanes), F32),
            in_specs=[VMEM] * 3 + [ANY] * len(ready),
            out_specs=VMEM,
            scratch_shapes=[pltpu.VMEM((devices * SUB, LANES), F32), pltpu.VMEM((devices, depth // 2), BF16)],
            compiler_params=params(8),
            cost_estimate=LONG,
        )(copies, weight, mate, *ready)
        return exchange(sums)

    def add_up(sums):
        sums = sums.reshape(devices // 2, 2, -1)
        return (sums[:, 0] + sums[:, 1]).astype(BF16).reshape(-1, LANES)

    def local(enc_x, enc_qkv, w_eo, w_kv, dec_x, w_q, w_o, cache_kv, doc_tile, cached_count):
        qkv = enc_qkv.transpose(1, 0, 2)
        w_q_mate = lax.ppermute(w_q, "seq", swap)
        w_o_mate = lax.ppermute(w_o, "seq", swap)
        blocks = (enc_qkv.size + enc_x.size) // (SUB * LANES)
        share = blocks // (2 * SHARES)
        rest = blocks - 2 * SHARES * share
        groups = dec_x.size // (2 * SUB * LANES) + rest + share
        rows = pltpu.VMEM((dec_x.shape[1] // LANES, LANES), F32)
        packed = pl.pallas_call(
            pack_kernel,
            out_shape=jax.ShapeDtypeStruct((devices, groups, SUB, LANES), BF16),
            in_specs=[ANY] * 3,
            out_specs=VMEM,
            scratch_shapes=[
                pltpu.VMEM(dec_x.shape, BF16),
                pltpu.VMEM(qkv.shape, BF16),
                pltpu.VMEM(enc_x.shape, BF16),
                rows,
                pltpu.SemaphoreType.DMA((3,)),
            ],
            compiler_params=params(40),
            cost_estimate=LONG,
        )(dec_x, qkv, enc_x)
        copies = exchange(packed)
        mine = pl.pallas_call(
            share_kernel,
            out_shape=jax.ShapeDtypeStruct((devices, share, SUB, LANES), BF16),
            in_specs=[VMEM],
            out_specs=VMEM,
            compiler_params=params(1),
        )(copies)
        shares = [lax.ppermute(mine, "seq", [(i, i ^ (2 * j)) for i in range(devices)]) for j in range(1, SHARES)]
        sums = project(copies, w_q, w_q_mate, w_o_mate)
        if sums.shape[-1] == LANES:
            query = pl.pallas_call(
                collect_kernel,
                out_shape=jax.ShapeDtypeStruct((sums.size // (2 * LANES), LANES), BF16),
                in_specs=[VMEM],
                out_specs=VMEM,
                scratch_shapes=[rows],
                compiler_params=params(1),
            )(sums)
        else:
            query = add_up(sums)
        merged = pl.pallas_call(
            merge_kernel,
            out_shape=jax.ShapeDtypeStruct((SHARES * share, devices * SUB, LANES), BF16),
            in_specs=[VMEM] * 5,
            out_specs=VMEM,
            compiler_params=params(4),
            cost_estimate=LONG,
        )(query, mine, *shares)
        new_kv = pl.pallas_call(
            encode_kernel,
            out_shape=jax.ShapeDtypeStruct((TILE_LEN, w_kv.shape[1]), BF16),
            in_specs=[SMEM] + [VMEM] * 5,
            out_specs=VMEM,
            compiler_params=params(12),
            cost_estimate=LONG,
        )(doc_tile, copies, merged, lax.ppermute(merged, "seq", swap), w_eo, w_kv)
        heads = query.shape[0]
        copies = pl.pallas_call(
            attend_kernel,
            out_shape=jax.ShapeDtypeStruct((devices, heads // (2 * SUB), SUB, LANES), BF16),
            in_specs=[SMEM] + [VMEM] * 3,
            out_specs=VMEM,
            compiler_params=params(4),
            cost_estimate=LONG,
        )(cached_count, query, cache_kv[0], new_kv)
        sums = project(exchange(copies), w_o, w_o_mate)
        if sums.shape[-1] == LANES:
            kernel, scratch, attn = finish_sums_kernel, [rows, pltpu.VMEM((heads, LANES), BF16)], sums
        else:
            kernel, scratch, attn = finish_kernel, [], add_up(sums)
        return pl.pallas_call(
            kernel,
            out_shape=jax.ShapeDtypeStruct(dec_x.shape, BF16),
            in_specs=[VMEM] * 2,
            out_specs=VMEM,
            scratch_shapes=scratch,
            compiler_params=params(2),
            cost_estimate=LONG,
        )(attn, dec_x)

    return jax.shard_map(
        local,
        mesh=mesh,
        in_specs=(
            P(("group", "seq"), None),
            P(("group", "seq"), None, None),
            P(),
            P(),
            P(("group", "seq"), None),
            P(None, "seq"),
            P(None, "seq"),
            P(("group", "seq"), None, None, None),
            P(("group", "seq")),
            P(("group", "seq")),
        ),
        out_specs=P(("group", "seq"), None),
        check_vma=False,
    )
```

time: 74.3 us -> 72.7 us (0.978)
  Pallas kernels: 10.7 us -> 8.15 us
  local copies, waits for them, and re-layouts: 0.47 us -> 2.73 us
  waiting for transfers between devices: 2.26 us -> 0.06 us
    pallas_call x10 -> x8, Pallas kernels: 6.65 us -> 4.1 us  [the longest x2 2.02 us: project(): pl.pallas_call(project_kernel, out_shape=jax.ShapeDtypeStruct((devices, 2...]
    unnamed x14 -> x18, local copies, waits for them, and re-layouts: 0.47 us -> 2.73 us
    ppermute x2, waiting for transfers between devices: 1.92 us -> 0.01 us  [the longest x1 0.01 us: local(): w_q_mate = lax.ppermute(w_q, 'seq', swap)]
  transfers between devices with their start and end apart: 6 -> 6, of which waited for: 3 -> 0; matrix products, arithmetic and copies ran while one was open for 0% -> 0% of each run, Pallas kernels for 3% -> 2%
where the time goes in v3:
time: 72.7 us; the launch traced here: 72.3 us
  blocking collectives  54.9 us (76%)
  Pallas kernels  8.15 us (11%)
  starting transfers between devices  4.24 us (6%)
  local copies, waits for them, and re-layouts  2.73 us (4%)
  between operations  2.24 us (3%)
    all_to_all x4, blocking collectives, exchange(): return lax.all_to_all(sent, 'seq', 0, 0, tiled=True)  54.9 us
    pallas_call x1, Pallas kernels, local(): pl.pallas_call(encode_kernel, out_shape=jax.ShapeDtypeStruct((TILE_LEN, w...  4.05 us
    ppermute x3, starting transfers between devices, local(): lax.ppermute(mine, 'seq', [(i, i ^ 2 * j) for i in range(devices)])  3.55 us
    unnamed x18, local copies, waits for them, and re-layouts  2.73 us
    pallas_call x2, Pallas kernels, project(): pl.pallas_call(project_kernel, out_shape=jax.ShapeDtypeStruct((devices, 2...  2.02 us
  transfers between devices with their start and end apart: 6, of which 0 were waited for; matrix products, arithmetic and copies ran while one was open for 0% of the time, Pallas kernels for 2%

profile of v3, /device:TPU:0, one launch (start us, length us, event | category | flops | bytes accessed | tf_op | source)
XLA Modules:
  0.0 72.3 jit_solution(17454328966264666786)
XLA Ops:
  0.0 0.5 collective-permute-start
  0.5 0.1 collective-permute-start.1
  0.5 0.8 %copy-done.4 = bf16[1,8192]{1,0:T(2,128)(2,1)S(1)} copy-done((bf16[1,8192]{1,0:T(2,128)(2,1)S(1)}, bf16[1,8192]{1,0:T(2,128)(2,1)}, u32[]{:S(2)}) %copy-start.4) | copy-done | bytes 16408
  1.3 0.8 %copy-done.5 = bf16[8,3,640]{2,0,1:T(8,128)(2,1)S(1)} copy-done((bf16[8,3,640]{2,0,1:T(8,128)(2,1)S(1)}, bf16[8,3,640]{2,0,1:T(8,128)(2,1)}, u32[]{:S(2)}) %copy-start.5) | copy-done | bytes 30744
  2.0 0.7 %copy-done.6 = bf16[8,1280]{1,0:T(8,128)(2,1)S(1)} copy-done((bf16[8,1280]{1,0:T(8,128)(2,1)S(1)}, bf16[8,1280]{1,0:T(8,128)(2,1)}, u32[]{:S(2)}) %copy-start.6) | copy-done | bytes 20504
  2.8 0.3 shard_map.100
  3.1 22.7 %all_to_all.20.sent_ref.own_ref = bf16[32,8,8,128]{3,2,1,0:T(8,128)(2,1)S(1)} all-to-all(bf16[32,8,8,128]{3,2,1,0:T(8,128)(2,1)S(1)} %shard_map.100), channel_id=1, replica_groups=mesh['group'=1,'seq'=32] {'seq'}, dimensions={0} | all-to-all | bytes 1048576 | tf_op jit(solution)/shard_map/all_to_all | solution.py:220
  25.8 1.0 %collective-permute-start.2 = (bf16[32,3,8,128]{3,2,1,0:T(8,128)(2,1)S(1)}, bf16[32,3,8,128]{3,2,1,0:T(8,128)(2,1)S(1)}, u32[]{:S(2)}, u32[]{:S(2)}) collective-permute-start(bf16[32,3,8,128]{3,2,1,0:T(8,128)(2,1)S(1)} %shard_map.103.own_0), channel_id=1, source_target_pairs={{0,2},{1,3},{2,0},{3,1},{4,6},{5,7},{6,4},{7,5},{8,10},{9,11},{10,... | collective-permute-start | bytes 589832 | tf_op jit(solution)/shard_map/ppermute | solution.py:272
  26.8 1.5 %collective-permute-start.3 = (bf16[32,3,8,128]{3,2,1,0:T(8,128)(2,1)S(1)}, bf16[32,3,8,128]{3,2,1,0:T(8,128)(2,1)S(1)}, u32[]{:S(2)}, u32[]{:S(2)}) collective-permute-start(bf16[32,3,8,128]{3,2,1,0:T(8,128)(2,1)S(1)} %shard_map.103.own_0), channel_id=1, source_target_pairs={{0,4},{1,5},{2,6},{3,7},{4,0},{5,1},{6,2},{7,3},{8,12},{9,13},{10,... | collective-permute-start | bytes 589832 | tf_op jit(solution)/shard_map/ppermute | solution.py:272
  28.3 1.1 %collective-permute-start.4 = (bf16[32,3,8,128]{3,2,1,0:T(8,128)(2,1)S(1)}, bf16[32,3,8,128]{3,2,1,0:T(8,128)(2,1)S(1)}, u32[]{:S(2)}, u32[]{:S(2)}) collective-permute-start(bf16[32,3,8,128]{3,2,1,0:T(8,128)(2,1)S(1)} %shard_map.103.own_0), channel_id=1, source_target_pairs={{0,6},{1,7},{2,4},{3,5},{4,2},{5,3},{6,0},{7,1},{8,14},{9,15},{10,... | collective-permute-start | bytes 589832 | tf_op jit(solution)/shard_map/ppermute | solution.py:272
  29.3 0.0 collective-permute-done.mate_ref
  29.3 0.0 collective-permute-done.1.refs_0_.mate_ref
  29.3 1.0 %shard_map.101 = f32[32,2,2,128]{3,2,1,0:T(2,128)S(1)} custom-call(bf16[32,8,8,128]{3,2,1,0:T(8,128)(2,1)S(1)} %all_to_all.20.sent_ref.own_ref, bf16[8192,256]{1,0:T(8,128)(2,1)S(1)} %copy-done, bf16[8192,256]{1,0:T(8,128)(2,1)S(1)} %collective-permute-done.mate_ref, bf16[8192,256]{1,0:T(8,128)(2,1)S(1)} %collective-permute-done.1.refs_0_.mate_ref), custom_call_target="tpu_custom_call" | custom-call | flops 10000000000 | bytes 10000000 | tf_op jit(solution)/shard_map/pallas_call | solution.py:225
  30.4 10.3 %all_to_all.21.sums_ref = f32[32,2,2,128]{3,2,1,0:T(2,128)S(1)} all-to-all(f32[32,2,2,128]{3,2,1,0:T(2,128)S(1)} %shard_map.101), channel_id=1, replica_groups=mesh['group'=1,'seq'=32] {'seq'}, dimensions={0} | all-to-all | bytes 131072 | tf_op jit(solution)/shard_map/all_to_all | solution.py:220
  40.7 0.0 slice-start.1
  40.7 0.0 copy-start.3
  40.7 0.0 collective-permute-done.2.own_1
  40.7 0.0 collective-permute-done.3.own_2
  40.7 0.0 collective-permute-done.4.own_3
  40.8 0.1 shard_map.104.own_ref
  40.9 0.2 collective-permute-start.5
  43.2 0.0 copy-start.2
  43.2 0.0 collective-permute-done.5.other_ref
  43.3 0.0 slice-done
  43.3 0.5 copy-done.3
  43.7 4.1 %shard_map.105.new_ref = bf16[128,2048]{1,0:T(8,128)(2,1)S(1)} custom-call(s32[1]{0:T(128)S(6)} %copy.11.tile_ref, bf16[32,8,8,128]{3,2,1,0:T(8,128)(2,1)S(1)} %all_to_all.20.sent_ref.own_ref, bf16[12,256,128]{2,1,0:T(8,128)(2,1)S(1)} %shard_map.104.own_ref, bf16[12,256,128]{2,1,0:T(8,128)(2,1)S(1)} %collective-permute-done.5.other_ref, ...), custom_call_target="tpu_custom_call" | custom-call | flops 10000000000 | bytes 10000000 | tf_op jit(solution)/shard_map/pallas_call | solution.py:293
  47.8 0.0 copy-start.1
  47.8 0.9 %shard_map.106 = bf16[32,4,8,128]{3,2,1,0:T(8,128)(2,1)S(1)} custom-call(s32[1]{0:T(128)S(6)} %copy.12.count_ref, bf16[64,128]{1,0:T(8,128)(2,1)S(1)} %shard_map.102.query_ref, bf16[4,128,2048]{2,1,0:T(8,128)(2,1)S(1)} %bitcast.4, bf16[128,2048]{1,0:T(8,128)(2,1)S(1)} %shard_map.105.new_ref), custom_call_target="tpu_custom_call" | custom-call | flops 10000000000 | bytes 10000000 | tf_op jit(solution)/shard_map/pallas_call | solution.py:302
  48.7 12.4 %all_to_all.22.sent_ref = bf16[32,4,8,128]{3,2,1,0:T(8,128)(2,1)S(1)} all-to-all(bf16[32,4,8,128]{3,2,1,0:T(8,128)(2,1)S(1)} %shard_map.106), channel_id=1, replica_groups=mesh['group'=1,'seq'=32] {'seq'}, dimensions={0} | all-to-all | bytes 524288 | tf_op jit(solution)/shard_map/all_to_all | solution.py:220
  61.1 1.0 %shard_map.107 = f32[32,2,2,128]{3,2,1,0:T(2,128)S(1)} custom-call(bf16[32,4,8,128]{3,2,1,0:T(8,128)(2,1)S(1)} %all_to_all.22.sent_ref, bf16[8192,256]{1,0:T(8,128)(2,1)S(1)} %copy-done.1, bf16[8192,256]{1,0:T(8,128)(2,1)S(1)} %collective-permute-done.1.refs_0_.mate_ref), custom_call_target="tpu_custom_call" | custom-call | flops 10000000000 | bytes 10000000 | tf_op jit(solution)/shard_map/pallas_call | solution.py:225
  62.1 9.5 %all_to_all.23.sums_ref = f32[32,2,2,128]{3,2,1,0:T(2,128)S(1)} all-to-all(f32[32,2,2,128]{3,2,1,0:T(2,128)S(1)} %shard_map.107), channel_id=1, replica_groups=mesh['group'=1,'seq'=32] {'seq'}, dimensions={0} | all-to-all | bytes 131072 | tf_op jit(solution)/shard_map/all_to_all | solution.py:220
  71.6 0.7 shard_map.108
  (12 shorter events, 0.1 us)
Async XLA Ops:
  0.0 29.3 %collective-permute-start = (bf16[8192,256]{1,0:T(8,128)(2,1)}, bf16[8192,256]{1,0:T(8,128)(2,1)S(1)}, u32[]{:S(2)}, u32[]{:S(2)}) collective-permute-start(bf16[8192,256]{1,0:T(8,128)(2,1)} %w_ref.2), channel_id=1, source_target_pairs={{0,1},{1,0},{2,3},{3,2},{4,5},{5,4},{6,7},{7,6},{8,9},{9,8},{10,11... | collective-permute-start | bytes 12582920 | tf_op jit(solution)/shard_map/ppermute | solution.py:242
  0.5 28.9 %collective-permute-start.1 = (bf16[8192,256]{1,0:T(8,128)(2,1)}, bf16[8192,256]{1,0:T(8,128)(2,1)S(1)}, u32[]{:S(2)}, u32[]{:S(2)}) collective-permute-start(bf16[8192,256]{1,0:T(8,128)(2,1)} %w_ref.3), channel_id=1, source_target_pairs={{0,1},{1,0},{2,3},{3,2},{4,5},{5,4},{6,7},{7,6},{8,9},{9,8},{10,11... | collective-permute-start | bytes 12582920 | tf_op jit(solution)/shard_map/ppermute | solution.py:243
  0.5 0.8 %copy-start.4 = (bf16[1,8192]{1,0:T(2,128)(2,1)S(1)}, bf16[1,8192]{1,0:T(2,128)(2,1)}, u32[]{:S(2)}) copy-start(bf16[1,8192]{1,0:T(2,128)(2,1)} %dec_x_ref.1) | copy-start | bytes 49156
  1.3 0.8 %copy-start.5 = (bf16[8,3,640]{2,0,1:T(8,128)(2,1)S(1)}, bf16[8,3,640]{2,0,1:T(8,128)(2,1)}, u32[]{:S(2)}) copy-start(bf16[8,3,640]{2,0,1:T(8,128)(2,1)} %param.11) | copy-start | bytes 92164
  2.0 0.7 %copy-start.6 = (bf16[8,1280]{1,0:T(8,128)(2,1)S(1)}, bf16[8,1280]{1,0:T(8,128)(2,1)}, u32[]{:S(2)}) copy-start(bf16[8,1280]{1,0:T(8,128)(2,1)} %enc_x_hbm.1) | copy-start | bytes 61444
  2.8 26.6 %copy-start = (bf16[8192,256]{1,0:T(8,128)(2,1)S(1)}, bf16[8192,256]{1,0:T(8,128)(2,1)}, u32[]{:S(2)}) copy-start(bf16[8192,256]{1,0:T(8,128)(2,1)} %w_ref.2) | copy-start | bytes 12582916
  25.8 14.9 %collective-permute-start.2 = (bf16[32,3,8,128]{3,2,1,0:T(8,128)(2,1)S(1)}, bf16[32,3,8,128]{3,2,1,0:T(8,128)(2,1)S(1)}, u32[]{:S(2)}, u32[]{:S(2)}) collective-permute-start(bf16[32,3,8,128]{3,2,1,0:T(8,128)(2,1)S(1)} %shard_map.103.own_0), channel_id=1, source_target_pairs={{0,2},{1,3},{2,0},{3,1},{4,6},{5,7},{6,4},{7,5},{8,10},{9,11},{10,... | collective-permute-start | bytes 589832 | tf_op jit(solution)/shard_map/ppermute | solution.py:272
  26.8 14.0 %collective-permute-start.3 = (bf16[32,3,8,128]{3,2,1,0:T(8,128)(2,1)S(1)}, bf16[32,3,8,128]{3,2,1,0:T(8,128)(2,1)S(1)}, u32[]{:S(2)}, u32[]{:S(2)}) collective-permute-start(bf16[32,3,8,128]{3,2,1,0:T(8,128)(2,1)S(1)} %shard_map.103.own_0), channel_id=1, source_target_pairs={{0,4},{1,5},{2,6},{3,7},{4,0},{5,1},{6,2},{7,3},{8,12},{9,13},{10,... | collective-permute-start | bytes 589832 | tf_op jit(solution)/shard_map/ppermute | solution.py:272
  28.3 12.5 %collective-permute-start.4 = (bf16[32,3,8,128]{3,2,1,0:T(8,128)(2,1)S(1)}, bf16[32,3,8,128]{3,2,1,0:T(8,128)(2,1)S(1)}, u32[]{:S(2)}, u32[]{:S(2)}) collective-permute-start(bf16[32,3,8,128]{3,2,1,0:T(8,128)(2,1)S(1)} %shard_map.103.own_0), channel_id=1, source_target_pairs={{0,6},{1,7},{2,4},{3,5},{4,2},{5,3},{6,0},{7,1},{8,14},{9,15},{10,... | collective-permute-start | bytes 589832 | tf_op jit(solution)/shard_map/ppermute | solution.py:272
  40.7 2.6 %slice-start = ((s8[5242880]{0:T(1024)(128)(4,1)}), s8[4194304]{0:T(1024)(128)(4,1)S(1)}, s32[]{:S(2)}) async-start(s8[5242880]{0:T(1024)(128)(4,1)} %bitcast.2), calls=%async_computation.4 | async-start | bytes 8388608
  40.7 2.6 %slice-start.1 = ((s8[5242880]{0:T(1024)(128)(4,1)}), s8[1048576]{0:T(1024)(128)(4,1)S(1)}, s32[]{:S(2)}) async-start(s8[5242880]{0:T(1024)(128)(4,1)} %bitcast.2), calls=%async_computation.5 | async-start | bytes 2097152
  40.7 3.0 %copy-start.3 = (bf16[640,1280]{1,0:T(8,128)(2,1)S(1)}, bf16[640,1280]{1,0:T(8,128)(2,1)}, u32[]{:S(2)}) copy-start(bf16[640,1280]{1,0:T(8,128)(2,1)} %w_eo_ref.1) | copy-start | bytes 4915204
  40.9 2.4 %collective-permute-start.5 = (bf16[12,256,128]{2,1,0:T(8,128)(2,1)S(1)}, bf16[12,256,128]{2,1,0:T(8,128)(2,1)S(1)}, u32[]{:S(2)}, u32[]{:S(2)}) collective-permute-start(bf16[12,256,128]{2,1,0:T(8,128)(2,1)S(1)} %shard_map.104.own_ref), channel_id=1, source_target_pairs={{0,1},{1,0},{2,3},{3,2},{4,5},{5,4},{6,7},{7,6},{8,9},{9,8},{10,11... | collective-permute-start | bytes 2359304 | tf_op jit(solution)/shard_map/ppermute | solution.py:300
  43.2 4.6 %copy-start.2 = (bf16[1,4,128,2048]{3,2,1,0:T(8,128)(2,1)S(1)}, bf16[1,4,128,2048]{3,2,1,0:T(8,128)(2,1)}, u32[]{:S(2)}) copy-start(bf16[1,4,128,2048]{3,2,1,0:T(8,128)(2,1)} %param.17) | copy-start | bytes 6291460
  47.8 13.3 %copy-start.1 = (bf16[8192,256]{1,0:T(8,128)(2,1)S(1)}, bf16[8192,256]{1,0:T(8,128)(2,1)}, u32[]{:S(2)}) copy-start(bf16[8192,256]{1,0:T(8,128)(2,1)} %w_ref.3) | copy-start | bytes 12582916

commit v4 on v3

--- a/solution.py
+++ b/solution.py
@@ -27,16 +27,8 @@
     return pltpu.CompilerParams(vmem_limit_bytes=mib * 1024 * 1024)
 
 
-def pack_kernel(dec_x_hbm, qkv_hbm, enc_x_hbm, out_ref, dec_x_ref, qkv_ref, enc_x_ref, rows_ref, sems):
-    copies = [
-        pltpu.make_async_copy(src, dst, sems.at[i])
-        for i, (src, dst) in enumerate(((dec_x_hbm, dec_x_ref), (qkv_hbm, qkv_ref), (enc_x_hbm, enc_x_ref)))
-    ]
-    for copy in copies:
-        copy.start()
-    for copy in copies:
-        copy.wait()
-    x = dec_x_ref[...].astype(F32)
+def pack_kernel(width, rows_in_ref, out_ref, rows_ref):
+    x = rows_in_ref[SUB : SUB + 1, :].astype(F32)
     scale = lax.rsqrt(jnp.mean(x * x, axis=-1, keepdims=True) + 1e-05)
     normed = x * scale
     groups = x.shape[1] // LANES
@@ -52,12 +44,7 @@
     halves = groups // SUB // 2
     for i in range(2 * halves):
         put(i % halves, rows_ref[i * SUB : (i + 1) * SUB, :], range(i // halves, copies, 2))
-    blocks = []
-    for i in range(3):
-        part = qkv_ref[i]
-        blocks += [part[:, t * LANES : (t + 1) * LANES] for t in range(part.shape[1] // LANES)]
-    enc_x = enc_x_ref[...]
-    blocks += [enc_x[:, t * LANES : (t + 1) * LANES] for t in range(enc_x.shape[1] // LANES)]
+    blocks = [rows_in_ref[:SUB, t : t + LANES] for t in range(0, width, LANES)]
     share = len(blocks) // (2 * SHARES)
     for i, block in enumerate(blocks[2 * SHARES * share :]):
         put(halves + i, block, range(copies))
@@ -144,20 +131,24 @@
     keys = jnp.concatenate([pick(tiles + t, every) for t in range(tiles)], axis=1)
     values = jnp.concatenate([pick(2 * tiles + t, every) for t in range(tiles)], axis=1)
     column = lax.broadcasted_iota(jnp.int32, (TILE_LEN, width), 1)
-    attn = [jnp.zeros((TILE_LEN, LANES), F32) for _ in range(tiles)]
+    spans, insides, scores, weights = [], [], [], []
     for h in range(EH):
-        lo, hi = h * EHD // LANES, (h * EHD + EHD - 1) // LANES + 1
-        span = slice(lo * LANES, hi * LANES)
+        span = slice(h * EHD // LANES * LANES, ((h + 1) * EHD - 1) // LANES * LANES + LANES)
         inside = (column[:, span] >= h * EHD) & (column[:, span] < (h + 1) * EHD)
         head = jnp.where(inside, query[:, span], jnp.zeros((), BF16))
-        scores = lax.dot_general(head, keys[:, span], (((1,), (1,)), ((), ())), preferred_element_type=F32)
-        scores = scores * EHD ** (-0.5)
-        powers = jnp.exp(scores - jnp.max(scores, axis=-1, keepdims=True))
-        weights = (powers / jnp.sum(powers, axis=-1, keepdims=True)).astype(BF16)
-        part = jnp.dot(weights, values[:, span], preferred_element_type=F32)
-        part = jnp.where(inside, part, 0.0)
-        for t in range(lo, hi):
-            attn[t] = attn[t] + part[:, (t - lo) * LANES : (t - lo + 1) * LANES]
+        score = lax.dot_general(head, keys[:, span], (((1,), (1,)), ((), ())), preferred_element_type=F32)
+        spans.append(span)
+        insides.append(inside)
+        scores.append(score * EHD ** (-0.5))
+    for score in scores:
+        powers = jnp.exp(score - jnp.max(score, axis=-1, keepdims=True))
+        weights.append((powers / jnp.sum(powers, axis=-1, keepdims=True)).astype(BF16))
+    attn = [jnp.zeros((TILE_LEN, LANES), F32) for _ in range(tiles)]
+    for span, inside, weight in zip(spans, insides, weights):
+        part = jnp.where(inside, jnp.dot(weight, values[:, span], preferred_element_type=F32), 0.0)
+        for t in range(span.start // LANES, span.stop // LANES):
+            start = t * LANES - span.start
+            attn[t] = attn[t] + part[:, start : start + LANES]
     attn = jnp.concatenate(attn, axis=1).astype(BF16)
     enc_x = jnp.concatenate([pick(3 * tiles + t, mine).astype(F32) for t in range(model // LANES)], axis=1)
     resid = enc_x + jnp.dot(attn, w_eo_ref[...], preferred_element_type=F32)
@@ -238,7 +229,10 @@
         return (sums[:, 0] + sums[:, 1]).astype(BF16).reshape(-1, LANES)
 
     def local(enc_x, enc_qkv, w_eo, w_kv, dec_x, w_q, w_o, cache_kv, doc_tile, cached_count):
-        qkv = enc_qkv.transpose(1, 0, 2)
+        width = (enc_qkv.size + enc_x.size) // SUB
+        spare = jnp.zeros((SUB, dec_x.shape[1] - width), BF16)
+        rows_in = jnp.concatenate([enc_qkv.reshape(SUB, -1), enc_x, spare], axis=1)
+        rows_in = jnp.concatenate([rows_in, dec_x], axis=0)
         w_q_mate = lax.ppermute(w_q, "seq", swap)
         w_o_mate = lax.ppermute(w_o, "seq", swap)
         blocks = (enc_qkv.size + enc_x.size) // (SUB * LANES)
@@ -247,20 +241,14 @@
         groups = dec_x.size // (2 * SUB * LANES) + rest + share
         rows = pltpu.VMEM((dec_x.shape[1] // LANES, LANES), F32)
         packed = pl.pallas_call(
-            pack_kernel,
+            functools.partial(pack_kernel, width),
             out_shape=jax.ShapeDtypeStruct((devices, groups, SUB, LANES), BF16),
-            in_specs=[ANY] * 3,
-            out_specs=VMEM,
-            scratch_shapes=[
-                pltpu.VMEM(dec_x.shape, BF16),
-                pltpu.VMEM(qkv.shape, BF16),
-                pltpu.VMEM(enc_x.shape, BF16),
-                rows,
-                pltpu.SemaphoreType.DMA((3,)),
-            ],
-            compiler_params=params(40),
-            cost_estimate=LONG,
-        )(dec_x, qkv, enc_x)
+            in_specs=[VMEM],
+            out_specs=VMEM,
+            scratch_shapes=[rows],
+            compiler_params=params(2),
+            cost_estimate=LONG,
+        )(rows_in)
         copies = exchange(packed)
         mine = pl.pallas_call(
             share_kernel,

time: 72.7 us -> 69.2 us (0.952)
  local copies, waits for them, and re-layouts: 2.73 us -> 0.51 us
  Pallas kernels: 8.15 us -> 6.19 us
  other arithmetic: 0.01 us -> 0.83 us
    unnamed x18 -> x14, local copies, waits for them, and re-layouts: 2.73 us -> 0.5 us
    pallas_call x1, Pallas kernels: 4.05 us -> 2.23 us  [local(): pl.pallas_call(encode_kernel, out_shape=jax.ShapeDtypeStruct((TILE_LEN, w...]
    concatenate x0 -> x1, other arithmetic: none -> 0.83 us  [local(): rows_in = jnp.concatenate([rows_in, dec_x], axis=0)]
  transfers between devices with their start and end apart: 6 -> 6, of which waited for: 0 -> 0; matrix products, arithmetic and copies ran while one was open for 0% -> 1% of each run, Pallas kernels for 2% -> 2%
where the time goes in v4:
time: 69.2 us; the launch traced here: 69 us
  blocking collectives  54.9 us (79%)
  Pallas kernels  6.19 us (9%)
  starting transfers between devices  4.24 us (6%)
  between operations  2.25 us (3%)
  other arithmetic  0.83 us (1%)
    all_to_all x4, blocking collectives, exchange(): return lax.all_to_all(sent, 'seq', 0, 0, tiled=True)  54.9 us
    ppermute x3, starting transfers between devices, local(): lax.ppermute(mine, 'seq', [(i, i ^ 2 * j) for i in range(devices)])  3.55 us
    pallas_call x1, Pallas kernels, local(): pl.pallas_call(encode_kernel, out_shape=jax.ShapeDtypeStruct((TILE_LEN, w...  2.23 us
    pallas_call x2, Pallas kernels, project(): pl.pallas_call(project_kernel, out_shape=jax.ShapeDtypeStruct((devices, 2...  2.02 us
  transfers between devices with their start and end apart: 6, of which 0 were waited for; matrix products, arithmetic and copies ran while one was open for 1% of the time, Pallas kernels for 2%

profile of v4, /device:TPU:0, one launch (start us, length us, event | category | flops | bytes accessed | tf_op | source)
XLA Modules:
  0.0 69.0 jit_solution(8702776657147989448)
XLA Ops:
  0.0 0.5 collective-permute-start
  0.5 0.1 collective-permute-start.1
  0.5 0.8 %pad_maximum_fusion.rows_in_ref = bf16[9,8192]{1,0:T(8,128)(2,1)S(1)} fusion(bf16[1,8192]{1,0:T(2,128)(2,1)} %dec_x_ref.1, bf16[8,4992]{1,0:T(8,128)(2,1)S(1)} %broadcast_in_dim.3, bf16[8,1280]{1,0:T(8,128)(2,1)} %param.10, bf16[8,1920]{1,0:T(8,128)(2,1)} %bitcast.5), kind=kLoop, calls=%fused_computation | loop fusion | flops 589824 | bytes 294912 | tf_op jit(solution)/shard_map/concatenate | solution.py:235
  1.4 0.0 copy-start.1
  1.4 0.2 shard_map.100
  1.6 22.7 %all_to_all.20.sent_ref.own_ref = bf16[32,8,8,128]{3,2,1,0:T(8,128)(2,1)S(1)} all-to-all(bf16[32,8,8,128]{3,2,1,0:T(8,128)(2,1)S(1)} %shard_map.100), channel_id=1, replica_groups=mesh['group'=1,'seq'=32] {'seq'}, dimensions={0} | all-to-all | bytes 1048576 | tf_op jit(solution)/shard_map/all_to_all | solution.py:211
  24.3 1.0 %collective-permute-start.2 = (bf16[32,3,8,128]{3,2,1,0:T(8,128)(2,1)S(1)}, bf16[32,3,8,128]{3,2,1,0:T(8,128)(2,1)S(1)}, u32[]{:S(2)}, u32[]{:S(2)}) collective-permute-start(bf16[32,3,8,128]{3,2,1,0:T(8,128)(2,1)S(1)} %shard_map.103.own_0), channel_id=1, source_target_pairs={{0,2},{1,3},{2,0},{3,1},{4,6},{5,7},{6,4},{7,5},{8,10},{9,11},{10,... | collective-permute-start | bytes 589832 | tf_op jit(solution)/shard_map/ppermute | solution.py:260
  25.3 1.5 %collective-permute-start.3 = (bf16[32,3,8,128]{3,2,1,0:T(8,128)(2,1)S(1)}, bf16[32,3,8,128]{3,2,1,0:T(8,128)(2,1)S(1)}, u32[]{:S(2)}, u32[]{:S(2)}) collective-permute-start(bf16[32,3,8,128]{3,2,1,0:T(8,128)(2,1)S(1)} %shard_map.103.own_0), channel_id=1, source_target_pairs={{0,4},{1,5},{2,6},{3,7},{4,0},{5,1},{6,2},{7,3},{8,12},{9,13},{10,... | collective-permute-start | bytes 589832 | tf_op jit(solution)/shard_map/ppermute | solution.py:260
  26.7 1.1 %collective-permute-start.4 = (bf16[32,3,8,128]{3,2,1,0:T(8,128)(2,1)S(1)}, bf16[32,3,8,128]{3,2,1,0:T(8,128)(2,1)S(1)}, u32[]{:S(2)}, u32[]{:S(2)}) collective-permute-start(bf16[32,3,8,128]{3,2,1,0:T(8,128)(2,1)S(1)} %shard_map.103.own_0), channel_id=1, source_target_pairs={{0,6},{1,7},{2,4},{3,5},{4,2},{5,3},{6,0},{7,1},{8,14},{9,15},{10,... | collective-permute-start | bytes 589832 | tf_op jit(solution)/shard_map/ppermute | solution.py:260
  27.8 0.0 collective-permute-done.mate_ref
  27.8 0.0 collective-permute-done.1.refs_0_.mate_ref
  27.8 0.0 copy-done.1
  27.8 1.0 %shard_map.101 = f32[32,2,2,128]{3,2,1,0:T(2,128)S(1)} custom-call(bf16[32,8,8,128]{3,2,1,0:T(8,128)(2,1)S(1)} %all_to_all.20.sent_ref.own_ref, bf16[8192,256]{1,0:T(8,128)(2,1)S(1)} %copy-done.1, bf16[8192,256]{1,0:T(8,128)(2,1)S(1)} %collective-permute-done.mate_ref, bf16[8192,256]{1,0:T(8,128)(2,1)S(1)} %collective-permute-done.1.refs_0_.mate_ref), custom_call_target="tpu_custom_call" | custom-call | flops 10000000000 | bytes 10000000 | tf_op jit(solution)/shard_map/pallas_call | solution.py:216
  28.9 10.3 %all_to_all.21.sums_ref = f32[32,2,2,128]{3,2,1,0:T(2,128)S(1)} all-to-all(f32[32,2,2,128]{3,2,1,0:T(2,128)S(1)} %shard_map.101), channel_id=1, replica_groups=mesh['group'=1,'seq'=32] {'seq'}, dimensions={0} | all-to-all | bytes 131072 | tf_op jit(solution)/shard_map/all_to_all | solution.py:211
  39.2 0.0 slice-start.1
  39.2 0.0 copy-start.4
  39.2 0.0 collective-permute-done.2.own_1
  39.2 0.0 collective-permute-done.3.own_2
  39.2 0.0 collective-permute-done.4.own_3
  39.2 0.1 shard_map.104.own_ref
  39.4 0.2 collective-permute-start.5
  41.7 0.0 copy-start.3
  41.7 0.0 collective-permute-done.5.other_ref
  41.7 0.5 copy-done.4
  42.2 2.2 %shard_map.105.new_ref = bf16[128,2048]{1,0:T(8,128)(2,1)S(1)} custom-call(s32[1]{0:T(128)S(6)} %copy.11.tile_ref, bf16[32,8,8,128]{3,2,1,0:T(8,128)(2,1)S(1)} %all_to_all.20.sent_ref.own_ref, bf16[12,256,128]{2,1,0:T(8,128)(2,1)S(1)} %shard_map.104.own_ref, bf16[12,256,128]{2,1,0:T(8,128)(2,1)S(1)} %collective-permute-done.5.other_ref, ...), custom_call_target="tpu_custom_call" | custom-call | flops 10000000000 | bytes 10000000 | tf_op jit(solution)/shard_map/pallas_call | solution.py:281
  44.5 0.0 copy-start.2
  44.5 0.9 %shard_map.106 = bf16[32,4,8,128]{3,2,1,0:T(8,128)(2,1)S(1)} custom-call(s32[1]{0:T(128)S(6)} %copy.12.count_ref, bf16[64,128]{1,0:T(8,128)(2,1)S(1)} %shard_map.102.query_ref, bf16[4,128,2048]{2,1,0:T(8,128)(2,1)S(1)} %bitcast.4, bf16[128,2048]{1,0:T(8,128)(2,1)S(1)} %shard_map.105.new_ref), custom_call_target="tpu_custom_call" | custom-call | flops 10000000000 | bytes 10000000 | tf_op jit(solution)/shard_map/pallas_call | solution.py:290
  45.3 12.4 %all_to_all.22.sent_ref = bf16[32,4,8,128]{3,2,1,0:T(8,128)(2,1)S(1)} all-to-all(bf16[32,4,8,128]{3,2,1,0:T(8,128)(2,1)S(1)} %shard_map.106), channel_id=1, replica_groups=mesh['group'=1,'seq'=32] {'seq'}, dimensions={0} | all-to-all | bytes 524288 | tf_op jit(solution)/shard_map/all_to_all | solution.py:211
  57.8 1.0 %shard_map.107 = f32[32,2,2,128]{3,2,1,0:T(2,128)S(1)} custom-call(bf16[32,4,8,128]{3,2,1,0:T(8,128)(2,1)S(1)} %all_to_all.22.sent_ref, bf16[8192,256]{1,0:T(8,128)(2,1)S(1)} %copy-done.2, bf16[8192,256]{1,0:T(8,128)(2,1)S(1)} %collective-permute-done.1.refs_0_.mate_ref), custom_call_target="tpu_custom_call" | custom-call | flops 10000000000 | bytes 10000000 | tf_op jit(solution)/shard_map/pallas_call | solution.py:216
  58.8 9.5 %all_to_all.23.sums_ref = f32[32,2,2,128]{3,2,1,0:T(2,128)S(1)} all-to-all(f32[32,2,2,128]{3,2,1,0:T(2,128)S(1)} %shard_map.107), channel_id=1, replica_groups=mesh['group'=1,'seq'=32] {'seq'}, dimensions={0} | all-to-all | bytes 131072 | tf_op jit(solution)/shard_map/all_to_all | solution.py:211
  68.3 0.0 copy-done
  68.3 0.7 shard_map.108
  (10 shorter events, 0.1 us)
Async XLA Ops:
  0.0 27.8 %collective-permute-start = (bf16[8192,256]{1,0:T(8,128)(2,1)}, bf16[8192,256]{1,0:T(8,128)(2,1)S(1)}, u32[]{:S(2)}, u32[]{:S(2)}) collective-permute-start(bf16[8192,256]{1,0:T(8,128)(2,1)} %w_ref.2), channel_id=1, source_target_pairs={{0,1},{1,0},{2,3},{3,2},{4,5},{5,4},{6,7},{7,6},{8,9},{9,8},{10,11... | collective-permute-start | bytes 12582920 | tf_op jit(solution)/shard_map/ppermute | solution.py:236
  0.5 27.4 %collective-permute-start.1 = (bf16[8192,256]{1,0:T(8,128)(2,1)}, bf16[8192,256]{1,0:T(8,128)(2,1)S(1)}, u32[]{:S(2)}, u32[]{:S(2)}) collective-permute-start(bf16[8192,256]{1,0:T(8,128)(2,1)} %w_ref.3), channel_id=1, source_target_pairs={{0,1},{1,0},{2,3},{3,2},{4,5},{5,4},{6,7},{7,6},{8,9},{9,8},{10,11... | collective-permute-start | bytes 12582920 | tf_op jit(solution)/shard_map/ppermute | solution.py:237
  1.4 26.5 %copy-start.1 = (bf16[8192,256]{1,0:T(8,128)(2,1)S(1)}, bf16[8192,256]{1,0:T(8,128)(2,1)}, u32[]{:S(2)}) copy-start(bf16[8192,256]{1,0:T(8,128)(2,1)} %w_ref.2) | copy-start | bytes 12582916
  24.3 14.9 %collective-permute-start.2 = (bf16[32,3,8,128]{3,2,1,0:T(8,128)(2,1)S(1)}, bf16[32,3,8,128]{3,2,1,0:T(8,128)(2,1)S(1)}, u32[]{:S(2)}, u32[]{:S(2)}) collective-permute-start(bf16[32,3,8,128]{3,2,1,0:T(8,128)(2,1)S(1)} %shard_map.103.own_0), channel_id=1, source_target_pairs={{0,2},{1,3},{2,0},{3,1},{4,6},{5,7},{6,4},{7,5},{8,10},{9,11},{10,... | collective-permute-start | bytes 589832 | tf_op jit(solution)/shard_map/ppermute | solution.py:260
  25.3 14.0 %collective-permute-start.3 = (bf16[32,3,8,128]{3,2,1,0:T(8,128)(2,1)S(1)}, bf16[32,3,8,128]{3,2,1,0:T(8,128)(2,1)S(1)}, u32[]{:S(2)}, u32[]{:S(2)}) collective-permute-start(bf16[32,3,8,128]{3,2,1,0:T(8,128)(2,1)S(1)} %shard_map.103.own_0), channel_id=1, source_target_pairs={{0,4},{1,5},{2,6},{3,7},{4,0},{5,1},{6,2},{7,3},{8,12},{9,13},{10,... | collective-permute-start | bytes 589832 | tf_op jit(solution)/shard_map/ppermute | solution.py:260
  26.7 12.5 %collective-permute-start.4 = (bf16[32,3,8,128]{3,2,1,0:T(8,128)(2,1)S(1)}, bf16[32,3,8,128]{3,2,1,0:T(8,128)(2,1)S(1)}, u32[]{:S(2)}, u32[]{:S(2)}) collective-permute-start(bf16[32,3,8,128]{3,2,1,0:T(8,128)(2,1)S(1)} %shard_map.103.own_0), channel_id=1, source_target_pairs={{0,6},{1,7},{2,4},{3,5},{4,2},{5,3},{6,0},{7,1},{8,14},{9,15},{10,... | collective-permute-start | bytes 589832 | tf_op jit(solution)/shard_map/ppermute | solution.py:260
  39.2 2.6 %slice-start = ((s8[5242880]{0:T(1024)(128)(4,1)}), s8[4194304]{0:T(1024)(128)(4,1)S(1)}, s32[]{:S(2)}) async-start(s8[5242880]{0:T(1024)(128)(4,1)} %bitcast.2), calls=%async_computation.4 | async-start | bytes 8388608
  39.2 2.6 %slice-start.1 = ((s8[5242880]{0:T(1024)(128)(4,1)}), s8[1048576]{0:T(1024)(128)(4,1)S(1)}, s32[]{:S(2)}) async-start(s8[5242880]{0:T(1024)(128)(4,1)} %bitcast.2), calls=%async_computation.5 | async-start | bytes 2097152
  39.2 3.0 %copy-start.4 = (bf16[640,1280]{1,0:T(8,128)(2,1)S(1)}, bf16[640,1280]{1,0:T(8,128)(2,1)}, u32[]{:S(2)}) copy-start(bf16[640,1280]{1,0:T(8,128)(2,1)} %w_eo_ref.1) | copy-start | bytes 4915204
  39.4 2.4 %collective-permute-start.5 = (bf16[12,256,128]{2,1,0:T(8,128)(2,1)S(1)}, bf16[12,256,128]{2,1,0:T(8,128)(2,1)S(1)}, u32[]{:S(2)}, u32[]{:S(2)}) collective-permute-start(bf16[12,256,128]{2,1,0:T(8,128)(2,1)S(1)} %shard_map.104.own_ref), channel_id=1, source_target_pairs={{0,1},{1,0},{2,3},{3,2},{4,5},{5,4},{6,7},{7,6},{8,9},{9,8},{10,11... | collective-permute-start | bytes 2359304 | tf_op jit(solution)/shard_map/ppermute | solution.py:288
  41.7 2.8 %copy-start.3 = (bf16[1,4,128,2048]{3,2,1,0:T(8,128)(2,1)S(1)}, bf16[1,4,128,2048]{3,2,1,0:T(8,128)(2,1)}, u32[]{:S(2)}) copy-start(bf16[1,4,128,2048]{3,2,1,0:T(8,128)(2,1)} %param.17) | copy-start | bytes 6291460
  44.5 13.3 %copy-start.2 = (bf16[8192,256]{1,0:T(8,128)(2,1)S(1)}, bf16[8192,256]{1,0:T(8,128)(2,1)}, u32[]{:S(2)}) copy-start(bf16[8192,256]{1,0:T(8,128)(2,1)} %w_ref.3) | copy-start | bytes 12582916
  57.8 10.5 %copy-start = (bf16[1,8192]{1,0:T(2,128)(2,1)S(1)}, bf16[1,8192]{1,0:T(2,128)(2,1)}, u32[]{:S(2)}) copy-start(bf16[1,8192]{1,0:T(2,128)(2,1)} %dec_x_ref.1) | copy-start | bytes 49156

commit v5 on v4

--- a/solution.py
+++ b/solution.py
@@ -14,10 +14,11 @@
 LANES = 128
 SUB = 8
 SHARES = 4
+EARLY = 2
 CHUNK = 512
 VMEM = pl.BlockSpec(memory_space=pltpu.VMEM)
+SMEM = pl.BlockSpec(memory_space=pltpu.SMEM)
 ANY = pl.BlockSpec(memory_space=pl.ANY)
-SMEM = pl.BlockSpec(memory_space=pltpu.SMEM)
 LONG = pl.CostEstimate(flops=10**10, transcendentals=0, bytes_accessed=10**7)
 F32 = jnp.float32
 BF16 = jnp.bfloat16
@@ -50,8 +51,12 @@
         put(halves + i, block, range(copies))
     first = out_ref.shape[1] - share
     for i, block in enumerate(blocks[: 2 * SHARES * share]):
-        core, chip = divmod(i // share, SHARES)
-        put(first + i % share, block, range(2 * chip + core, copies, 2 * SHARES))
+        early = i < 2 * SHARES * EARLY
+        each = EARLY if early else share - EARLY
+        piece, place = divmod(i if early else i - 2 * SHARES * EARLY, each)
+        core, chip = divmod(piece, SHARES)
+        place += first if early else first + EARLY
+        put(place, block, range(2 * chip + core, copies, 2 * SHARES))
 
 
 def project_kernel(sent_ref, w_ref, mate_ref, *refs):
@@ -100,36 +105,33 @@
     return block.astype(F32).reshape(-1, LANES).astype(BF16)
 
 
-def merge_kernel(query_ref, own_0, own_1, own_2, own_3, out_ref):
-    share = own_0.shape[1]
+def merge_kernel(start, query_ref, own_0, own_1, own_2, own_3, out_ref):
+    share = out_ref.shape[0] // SHARES
     place = lax.rem(lax.axis_index("seq") // 2, SHARES)
     for j, ref in enumerate((own_0, own_1, own_2, own_3)):
-        start = jnp.bitwise_xor(place, j) * share
         for i in range(share):
-            out_ref[start + i] = merge(ref[:, i])
-
-
-def encode_kernel(tile_ref, sent_ref, own_ref, other_ref, w_eo_ref, w_kv_ref, out_ref):
-    width, model = w_eo_ref.shape
+            out_ref[jnp.bitwise_xor(place, j) * share + i] = merge(ref[:, start + i])
+
+
+def pick(place, rows, own_ref, other_ref):
+    held = own_ref.shape[0]
+    core = lax.rem(lax.axis_index("seq"), 2)
+    side, index = divmod(place, held)
+    return jnp.where(core == side, own_ref[index, rows], other_ref[index, rows])
+
+
+def rows_of(tile_ref):
+    return pl.ds(pl.multiple_of(tile_ref[0] * TILE_LEN, TILE_LEN), TILE_LEN)
+
+
+def attention_kernel(tile_ref, own_ref, other_ref, out_ref):
+    width = out_ref.shape[1]
     tiles = width // LANES
-    held = own_ref.shape[0]
-    rest = 3 * tiles + model // LANES - 2 * held
-    first = sent_ref.shape[1] - held // SHARES - rest
-    core = lax.rem(lax.axis_index("seq"), 2)
-    mine = pl.ds(pl.multiple_of(tile_ref[0] * TILE_LEN, TILE_LEN), TILE_LEN)
-
-    def pick(place, rows):
-        if place >= 2 * held:
-            chunk = TILE_LEN // SUB
-            block = sent_ref[pl.ds(tile_ref[0] * chunk, chunk), first + place - 2 * held]
-            return merge(block)
-        side, index = divmod(place, held)
-        return jnp.where(core == side, own_ref[index, rows], other_ref[index, rows])
-
+    mine = rows_of(tile_ref)
     every = slice(None)
-    query = jnp.concatenate([pick(t, mine) for t in range(tiles)], axis=1)
-    keys = jnp.concatenate([pick(tiles + t, every) for t in range(tiles)], axis=1)
-    values = jnp.concatenate([pick(2 * tiles + t, every) for t in range(tiles)], axis=1)
+    query = jnp.concatenate([pick(t, mine, own_ref, other_ref) for t in range(tiles)], axis=1)
+    keys = jnp.concatenate([pick(tiles + t, every, own_ref, other_ref) for t in range(tiles)], axis=1)
+    values = jnp.concatenate([pick(2 * tiles + t, every, own_ref, other_ref) for t in range(tiles)], axis=1)
     column = lax.broadcasted_iota(jnp.int32, (TILE_LEN, width), 1)
     spans, insides, scores, weights = [], [], [], []
     for h in range(EH):
@@ -149,33 +151,56 @@
         for t in range(span.start // LANES, span.stop // LANES):
             start = t * LANES - span.start
             attn[t] = attn[t] + part[:, start : start + LANES]
-    attn = jnp.concatenate(attn, axis=1).astype(BF16)
-    enc_x = jnp.concatenate([pick(3 * tiles + t, mine).astype(F32) for t in range(model // LANES)], axis=1)
-    resid = enc_x + jnp.dot(attn, w_eo_ref[...], preferred_element_type=F32)
+    out_ref[...] = jnp.concatenate(attn, axis=1).astype(BF16)
+
+
+def features_kernel(
+    tile_ref, attn_ref, sent_ref, own_ref, other_ref, own_late, other_late, w_eo_ref, w_kv_ref, out_ref
+):
+    width, model = w_eo_ref.shape
+    mine = rows_of(tile_ref)
+    early, late = 2 * own_ref.shape[0], 2 * own_late.shape[0]
+    first = 3 * width // LANES
+    enc_x = [pick(t, mine, own_ref, other_ref) for t in range(first, early)]
+    enc_x += [pick(t, mine, own_late, other_late) for t in range(late)]
+    chunk = TILE_LEN // SUB
+    rest = first + model // LANES - early - late
+    last = sent_ref.shape[1] - (early + late) // (2 * SHARES)
+    enc_x += [merge(sent_ref[pl.ds(tile_ref[0] * chunk, chunk), t]) for t in range(last - rest, last)]
+    enc_x = jnp.concatenate(enc_x, axis=1).astype(F32)
+    resid = enc_x + jnp.dot(attn_ref[...], w_eo_ref[...], preferred_element_type=F32)
     center = resid - jnp.mean(resid, axis=-1, keepdims=True)
     spread = jnp.mean(center * center, axis=-1, keepdims=True)
     features = (center * lax.rsqrt(spread + 1e-05)).astype(BF16)
     out_ref[...] = jnp.dot(features, w_kv_ref[...], preferred_element_type=F32).astype(BF16)
 
 
-def attend_kernel(count_ref, query_ref, cache_ref, new_ref, out_ref):
-    filled = count_ref[0]
+def scores_kernel(query_ref, keys_ref, _, out_ref):
+    slots, length, width = keys_ref.shape[0], keys_ref.shape[1], keys_ref.shape[2] // 2
+    kv_heads = width // HD
+    per = query_ref.shape[0] // kv_heads
+    for g in range(kv_heads):
+        keys = keys_ref[:, :, g * HD : (g + 1) * HD].reshape(slots * length, HD)
+        rows = slice(g * per, (g + 1) * per)
+        out_ref[rows, :] = lax.dot_general(
+            query_ref[rows, :], keys, (((1,), (1,)), ((), ())), preferred_element_type=F32
+        ) * HD ** (-0.5)
+
+
+def attend_kernel(count_ref, query_ref, scores_ref, cache_ref, new_ref, out_ref):
     slots, length, both = cache_ref.shape
     width = both // 2
     kv_heads = width // HD
     per = query_ref.shape[0] // kv_heads
-    query = query_ref[...]
     scores = []
     for g in range(kv_heads):
-        head = query[g * per : (g + 1) * per]
-        cols = slice(g * HD, (g + 1) * HD)
-        keys = cache_ref[:, :, cols].reshape(slots * length, HD)
-        old = lax.dot_general(head, keys, (((1,), (1,)), ((), ())), preferred_element_type=F32)
-        new = lax.dot_general(head, new_ref[:, cols], (((1,), (1,)), ((), ())), preferred_element_type=F32)
-        scores.append(jnp.concatenate([old, new], axis=1))
+        keys = new_ref[:, g * HD : (g + 1) * HD]
+        head = query_ref[g * per : (g + 1) * per, :]
+        scores.append(lax.dot_general(head, keys, (((1,), (1,)), ((), ())), preferred_element_type=F32))
     scores = jnp.concatenate(scores, axis=0) * HD ** (-0.5)
-    slot = lax.broadcasted_iota(jnp.int32, scores.shape, 1) // length
-    scores = jnp.where((slot < filled) | (slot == slots), scores, -jnp.inf)
+    slot = lax.broadcasted_iota(jnp.int32, scores_ref.shape, 1) // length
+    old = jnp.where(slot < count_ref[0], scores_ref[...], -jnp.inf)
+    scores = jnp.concatenate([old, scores], axis=1)
     powers = jnp.exp(scores - jnp.max(scores, axis=-1, keepdims=True))
     weights = (powers / jnp.sum(powers, axis=-1, keepdims=True)).astype(BF16)
     copies = out_ref.shape[0]
@@ -270,31 +295,50 @@
             )(sums)
         else:
             query = add_up(sums)
-        merged = pl.pallas_call(
-            merge_kernel,
-            out_shape=jax.ShapeDtypeStruct((SHARES * share, devices * SUB, LANES), BF16),
-            in_specs=[VMEM] * 5,
+        def merge_part(start, count):
+            merged = pl.pallas_call(
+                functools.partial(merge_kernel, start),
+                out_shape=jax.ShapeDtypeStruct((SHARES * count, devices * SUB, LANES), BF16),
+                in_specs=[VMEM] * 5,
+                out_specs=VMEM,
+                compiler_params=params(4),
+            )(query, mine, *shares)
+            return merged, lax.ppermute(merged, "seq", swap)
+
+        early = merge_part(0, EARLY)
+        late = merge_part(EARLY, share - EARLY)
+        cache = cache_kv[0]
+        scores = pl.pallas_call(
+            scores_kernel,
+            out_shape=jax.ShapeDtypeStruct((query.shape[0], cache.shape[0] * TILE_LEN), F32),
+            in_specs=[VMEM] * 2 + [ANY],
             out_specs=VMEM,
             compiler_params=params(4),
-            cost_estimate=LONG,
-        )(query, mine, *shares)
+        )(query, cache, early[0])
+        attn = pl.pallas_call(
+            attention_kernel,
+            out_shape=jax.ShapeDtypeStruct((TILE_LEN, w_eo.shape[0]), BF16),
+            in_specs=[SMEM] + [VMEM] * 2,
+            out_specs=VMEM,
+            compiler_params=params(8),
+        )(doc_tile, *early)
         new_kv = pl.pallas_call(
-            encode_kernel,
+            features_kernel,
             out_shape=jax.ShapeDtypeStruct((TILE_LEN, w_kv.shape[1]), BF16),
-            in_specs=[SMEM] + [VMEM] * 5,
-            out_specs=VMEM,
-            compiler_params=params(12),
-            cost_estimate=LONG,
-        )(doc_tile, copies, merged, lax.ppermute(merged, "seq", swap), w_eo, w_kv)
+            in_specs=[SMEM] + [VMEM] * 8,
+            out_specs=VMEM,
+            compiler_params=params(8),
+            cost_estimate=LONG,
+        )(doc_tile, attn, copies, *early, *late, w_eo, w_kv)
         heads = query.shape[0]
         copies = pl.pallas_call(
             attend_kernel,
             out_shape=jax.ShapeDtypeStruct((devices, heads // (2 * SUB), SUB, LANES), BF16),
-            in_specs=[SMEM] + [VMEM] * 3,
+            in_specs=[SMEM] + [VMEM] * 4,
             out_specs=VMEM,
             compiler_params=params(4),
             cost_estimate=LONG,
-        )(cached_count, query, cache_kv[0], new_kv)
+        )(cached_count, query, scores, cache, new_kv)
         sums = project(exchange(copies), w_o, w_o_mate)
         if sums.shape[-1] == LANES:
             kernel, scratch, attn = finish_sums_kernel, [rows, pltpu.VMEM((heads, LANES), BF16)], sums

time: 69.2 us -> 68.8 us (level)
  between operations: 2.25 us -> 1.48 us
    pallas_call x2 -> x5, Pallas kernels: 2.37 us -> 2.82 us  [the longest x1 1.47 us: local(): pl.pallas_call(features_kernel, out_shape=jax.ShapeDtypeStruct((TILE_LEN,...]
  transfers between devices with their start and end apart: 6 -> 7, of which waited for: 0 -> 0; matrix products, arithmetic and copies ran while one was open for 1% -> 1% of each run, Pallas kernels for 2% -> 4%
where the time goes in v5:
time: 68.8 us; the launch traced here: 68.5 us
  blocking collectives  54.9 us (80%)
  Pallas kernels  6.53 us (9%)
  starting transfers between devices  4.7 us (7%)
  between operations  1.48 us (2%)
  other arithmetic  0.83 us (1%)
    all_to_all x4, blocking collectives, exchange(): return lax.all_to_all(sent, 'seq', 0, 0, tiled=True)  54.9 us
    ppermute x3, starting transfers between devices, local(): lax.ppermute(mine, 'seq', [(i, i ^ 2 * j) for i in range(devices)])  3.55 us
    pallas_call x2, Pallas kernels, project(): pl.pallas_call(project_kernel, out_shape=jax.ShapeDtypeStruct((devices, 2...  2.02 us
    pallas_call x1, Pallas kernels, local(): pl.pallas_call(features_kernel, out_shape=jax.ShapeDtypeStruct((TILE_LEN,...  1.47 us
  transfers between devices with their start and end apart: 7, of which 0 were waited for; matrix products, arithmetic and copies ran while one was open for 1% of the time, Pallas kernels for 4%

profile of v5, /device:TPU:0, one launch (start us, length us, event | category | flops | bytes accessed | tf_op | source)
XLA Modules:
  0.0 68.5 jit_solution(17594805687092851153)
XLA Ops:
  0.0 0.5 collective-permute-start
  0.5 0.1 collective-permute-start.1
  0.5 0.8 %pad_maximum_fusion.rows_in_ref = bf16[9,8192]{1,0:T(8,128)(2,1)S(1)} fusion(bf16[1,8192]{1,0:T(2,128)(2,1)} %dec_x_ref.1, bf16[8,4992]{1,0:T(8,128)(2,1)S(1)} %broadcast_in_dim.3, bf16[8,1280]{1,0:T(8,128)(2,1)} %param.10, bf16[8,1920]{1,0:T(8,128)(2,1)} %bitcast.6), kind=kLoop, calls=%fused_computation | loop fusion | flops 589824 | bytes 294912 | tf_op jit(solution)/shard_map/concatenate | solution.py:260
  1.4 0.0 copy-start.2
  1.4 0.2 shard_map.100
  1.6 22.7 %all_to_all.20.sent_ref.own_ref = bf16[32,8,8,128]{3,2,1,0:T(8,128)(2,1)S(1)} all-to-all(bf16[32,8,8,128]{3,2,1,0:T(8,128)(2,1)S(1)} %shard_map.100), channel_id=1, replica_groups=mesh['group'=1,'seq'=32] {'seq'}, dimensions={0} | all-to-all | bytes 1048576 | tf_op jit(solution)/shard_map/all_to_all | solution.py:236
  24.3 0.0 copy-start
  24.3 0.0 slice-start.1
  24.3 1.0 %collective-permute-start.2 = (bf16[32,3,8,128]{3,2,1,0:T(8,128)(2,1)S(1)}, bf16[32,3,8,128]{3,2,1,0:T(8,128)(2,1)S(1)}, u32[]{:S(2)}, u32[]{:S(2)}) collective-permute-start(bf16[32,3,8,128]{3,2,1,0:T(8,128)(2,1)S(1)} %shard_map.103.own_0), channel_id=1, source_target_pairs={{0,2},{1,3},{2,0},{3,1},{4,6},{5,7},{6,4},{7,5},{8,10},{9,11},{10,... | collective-permute-start | bytes 589832 | tf_op jit(solution)/shard_map/ppermute | solution.py:285
  25.3 1.5 %collective-permute-start.3 = (bf16[32,3,8,128]{3,2,1,0:T(8,128)(2,1)S(1)}, bf16[32,3,8,128]{3,2,1,0:T(8,128)(2,1)S(1)}, u32[]{:S(2)}, u32[]{:S(2)}) collective-permute-start(bf16[32,3,8,128]{3,2,1,0:T(8,128)(2,1)S(1)} %shard_map.103.own_0), channel_id=1, source_target_pairs={{0,4},{1,5},{2,6},{3,7},{4,0},{5,1},{6,2},{7,3},{8,12},{9,13},{10,... | collective-permute-start | bytes 589832 | tf_op jit(solution)/shard_map/ppermute | solution.py:285
  26.8 1.1 %collective-permute-start.4 = (bf16[32,3,8,128]{3,2,1,0:T(8,128)(2,1)S(1)}, bf16[32,3,8,128]{3,2,1,0:T(8,128)(2,1)S(1)}, u32[]{:S(2)}, u32[]{:S(2)}) collective-permute-start(bf16[32,3,8,128]{3,2,1,0:T(8,128)(2,1)S(1)} %shard_map.103.own_0), channel_id=1, source_target_pairs={{0,6},{1,7},{2,4},{3,5},{4,2},{5,3},{6,0},{7,1},{8,14},{9,15},{10,... | collective-permute-start | bytes 589832 | tf_op jit(solution)/shard_map/ppermute | solution.py:285
  27.9 0.0 collective-permute-done.mate_ref
  27.9 0.0 collective-permute-done.1.refs_0_.mate_ref
  27.9 1.0 %shard_map.101 = f32[32,2,2,128]{3,2,1,0:T(2,128)S(1)} custom-call(bf16[32,8,8,128]{3,2,1,0:T(8,128)(2,1)S(1)} %all_to_all.20.sent_ref.own_ref, bf16[8192,256]{1,0:T(8,128)(2,1)S(1)} %copy-done.2, bf16[8192,256]{1,0:T(8,128)(2,1)S(1)} %collective-permute-done.mate_ref, bf16[8192,256]{1,0:T(8,128)(2,1)S(1)} %collective-permute-done.1.refs_0_.mate_ref), custom_call_target="tpu_custom_call" | custom-call | flops 10000000000 | bytes 10000000 | tf_op jit(solution)/shard_map/pallas_call | solution.py:241
  28.9 0.0 copy-start.4
  28.9 10.3 %all_to_all.21.sums_ref = f32[32,2,2,128]{3,2,1,0:T(2,128)S(1)} all-to-all(f32[32,2,2,128]{3,2,1,0:T(2,128)S(1)} %shard_map.101), channel_id=1, replica_groups=mesh['group'=1,'seq'=32] {'seq'}, dimensions={0} | all-to-all | bytes 131072 | tf_op jit(solution)/shard_map/all_to_all | solution.py:236
  39.2 0.0 collective-permute-done.2.own_1
  39.2 0.0 collective-permute-done.3.own_2
  39.2 0.0 collective-permute-done.4.own_3
  39.3 0.1 shard_map.104._.own_ref
  39.4 0.2 collective-permute-start.5
  39.6 0.5 collective-permute-start.6
  41.4 0.4 shard_map.105.scores_ref
  41.7 0.0 collective-permute-done.5.other_ref
  41.8 0.8 %shard_map.106.attn_ref = bf16[128,640]{1,0:T(8,128)(2,1)S(1)} custom-call(s32[1]{0:T(128)S(6)} %copy.11.tile_ref, bf16[8,256,128]{2,1,0:T(8,128)(2,1)S(1)} %shard_map.104._.own_ref, bf16[8,256,128]{2,1,0:T(8,128)(2,1)S(1)} %collective-permute-done.5.other_ref), custom_call_target="tpu_custom_call" | custom-call | tf_op jit(solution)/shard_map/pallas_call | solution.py:318
  42.6 1.5 %shard_map.108.new_ref = bf16[128,2048]{1,0:T(8,128)(2,1)S(1)} custom-call(s32[1]{0:T(128)S(6)} %copy.11.tile_ref, bf16[128,640]{1,0:T(8,128)(2,1)S(1)} %shard_map.106.attn_ref, bf16[32,8,8,128]{3,2,1,0:T(8,128)(2,1)S(1)} %all_to_all.20.sent_ref.own_ref, bf16[8,256,128]{2,1,0:T(8,128)(2,1)S(1)} %shard_map.104._.own_ref, ...), custom_call_target="tpu_custom_call" | custom-call | flops 10000000000 | bytes 10000000 | tf_op jit(solution)/shard_map/pallas_call | solution.py:325
  44.1 0.0 copy-start.3
  44.1 0.7 %shard_map.109 = bf16[32,4,8,128]{3,2,1,0:T(8,128)(2,1)S(1)} custom-call(s32[1]{0:T(128)S(6)} %copy.12.count_ref, bf16[64,128]{1,0:T(8,128)(2,1)S(1)} %shard_map.102.query_ref, f32[64,512]{1,0:T(8,128)S(1)} %shard_map.105.scores_ref, bf16[4,128,2048]{2,1,0:T(8,128)(2,1)S(1)} %bitcast.3, bf16[128,2048]{1,0:T(8,128)(2,1)S(1)} %shard_map.108.new_ref), custom_call_target="tpu_custom_call" | custom-call | flops 10000000000 | bytes 10000000 | tf_op jit(solution)/shard_map/pallas_call | solution.py:334
  44.9 12.4 %all_to_all.22.sent_ref = bf16[32,4,8,128]{3,2,1,0:T(8,128)(2,1)S(1)} all-to-all(bf16[32,4,8,128]{3,2,1,0:T(8,128)(2,1)S(1)} %shard_map.109), channel_id=1, replica_groups=mesh['group'=1,'seq'=32] {'seq'}, dimensions={0} | all-to-all | bytes 524288 | tf_op jit(solution)/shard_map/all_to_all | solution.py:236
  57.3 1.0 %shard_map.110 = f32[32,2,2,128]{3,2,1,0:T(2,128)S(1)} custom-call(bf16[32,4,8,128]{3,2,1,0:T(8,128)(2,1)S(1)} %all_to_all.22.sent_ref, bf16[8192,256]{1,0:T(8,128)(2,1)S(1)} %copy-done.3, bf16[8192,256]{1,0:T(8,128)(2,1)S(1)} %collective-permute-done.1.refs_0_.mate_ref), custom_call_target="tpu_custom_call" | custom-call | flops 10000000000 | bytes 10000000 | tf_op jit(solution)/shard_map/pallas_call | solution.py:241
  58.3 9.5 %all_to_all.23.sums_ref = f32[32,2,2,128]{3,2,1,0:T(2,128)S(1)} all-to-all(f32[32,2,2,128]{3,2,1,0:T(2,128)S(1)} %shard_map.110), channel_id=1, replica_groups=mesh['group'=1,'seq'=32] {'seq'}, dimensions={0} | all-to-all | bytes 131072 | tf_op jit(solution)/shard_map/all_to_all | solution.py:236
  67.8 0.7 shard_map.111
  (15 shorter events, 0.1 us)
Async XLA Ops:
  0.0 27.9 %collective-permute-start = (bf16[8192,256]{1,0:T(8,128)(2,1)}, bf16[8192,256]{1,0:T(8,128)(2,1)S(1)}, u32[]{:S(2)}, u32[]{:S(2)}) collective-permute-start(bf16[8192,256]{1,0:T(8,128)(2,1)} %w_ref.2), channel_id=1, source_target_pairs={{0,1},{1,0},{2,3},{3,2},{4,5},{5,4},{6,7},{7,6},{8,9},{9,8},{10,11... | collective-permute-start | bytes 12582920 | tf_op jit(solution)/shard_map/ppermute | solution.py:261
  0.5 27.4 %collective-permute-start.1 = (bf16[8192,256]{1,0:T(8,128)(2,1)}, bf16[8192,256]{1,0:T(8,128)(2,1)S(1)}, u32[]{:S(2)}, u32[]{:S(2)}) collective-permute-start(bf16[8192,256]{1,0:T(8,128)(2,1)} %w_ref.3), channel_id=1, source_target_pairs={{0,1},{1,0},{2,3},{3,2},{4,5},{5,4},{6,7},{7,6},{8,9},{9,8},{10,11... | collective-permute-start | bytes 12582920 | tf_op jit(solution)/shard_map/ppermute | solution.py:262
  1.4 26.5 %copy-start.2 = (bf16[8192,256]{1,0:T(8,128)(2,1)S(1)}, bf16[8192,256]{1,0:T(8,128)(2,1)}, u32[]{:S(2)}) copy-start(bf16[8192,256]{1,0:T(8,128)(2,1)} %w_ref.2) | copy-start | bytes 12582916
  24.3 18.3 %slice-start = ((s8[5242880]{0:T(1024)(128)(4,1)}), s8[4194304]{0:T(1024)(128)(4,1)S(1)}, s32[]{:S(2)}) async-start(s8[5242880]{0:T(1024)(128)(4,1)} %bitcast.4), calls=%async_computation.4 | async-start | bytes 8388608
  24.3 17.1 %copy-start = (bf16[1,4,128,2048]{3,2,1,0:T(8,128)(2,1)S(1)}, bf16[1,4,128,2048]{3,2,1,0:T(8,128)(2,1)}, u32[]{:S(2)}) copy-start(bf16[1,4,128,2048]{3,2,1,0:T(8,128)(2,1)} %param.17) | copy-start | bytes 6291460
  24.3 18.3 %slice-start.1 = ((s8[5242880]{0:T(1024)(128)(4,1)}), s8[1048576]{0:T(1024)(128)(4,1)S(1)}, s32[]{:S(2)}) async-start(s8[5242880]{0:T(1024)(128)(4,1)} %bitcast.4), calls=%async_computation.5 | async-start | bytes 2097152
  24.3 14.9 %collective-permute-start.2 = (bf16[32,3,8,128]{3,2,1,0:T(8,128)(2,1)S(1)}, bf16[32,3,8,128]{3,2,1,0:T(8,128)(2,1)S(1)}, u32[]{:S(2)}, u32[]{:S(2)}) collective-permute-start(bf16[32,3,8,128]{3,2,1,0:T(8,128)(2,1)S(1)} %shard_map.103.own_0), channel_id=1, source_target_pairs={{0,2},{1,3},{2,0},{3,1},{4,6},{5,7},{6,4},{7,5},{8,10},{9,11},{10,... | collective-permute-start | bytes 589832 | tf_op jit(solution)/shard_map/ppermute | solution.py:285
  25.3 13.9 %collective-permute-start.3 = (bf16[32,3,8,128]{3,2,1,0:T(8,128)(2,1)S(1)}, bf16[32,3,8,128]{3,2,1,0:T(8,128)(2,1)S(1)}, u32[]{:S(2)}, u32[]{:S(2)}) collective-permute-start(bf16[32,3,8,128]{3,2,1,0:T(8,128)(2,1)S(1)} %shard_map.103.own_0), channel_id=1, source_target_pairs={{0,4},{1,5},{2,6},{3,7},{4,0},{5,1},{6,2},{7,3},{8,12},{9,13},{10,... | collective-permute-start | bytes 589832 | tf_op jit(solution)/shard_map/ppermute | solution.py:285
  26.8 12.5 %collective-permute-start.4 = (bf16[32,3,8,128]{3,2,1,0:T(8,128)(2,1)S(1)}, bf16[32,3,8,128]{3,2,1,0:T(8,128)(2,1)S(1)}, u32[]{:S(2)}, u32[]{:S(2)}) collective-permute-start(bf16[32,3,8,128]{3,2,1,0:T(8,128)(2,1)S(1)} %shard_map.103.own_0), channel_id=1, source_target_pairs={{0,6},{1,7},{2,4},{3,5},{4,2},{5,3},{6,0},{7,1},{8,14},{9,15},{10,... | collective-permute-start | bytes 589832 | tf_op jit(solution)/shard_map/ppermute | solution.py:285
  28.9 13.7 %copy-start.4 = (bf16[640,1280]{1,0:T(8,128)(2,1)S(1)}, bf16[640,1280]{1,0:T(8,128)(2,1)}, u32[]{:S(2)}) copy-start(bf16[640,1280]{1,0:T(8,128)(2,1)} %w_eo_ref.1) | copy-start | bytes 4915204
  39.4 2.4 %collective-permute-start.5 = (bf16[8,256,128]{2,1,0:T(8,128)(2,1)S(1)}, bf16[8,256,128]{2,1,0:T(8,128)(2,1)S(1)}, u32[]{:S(2)}, u32[]{:S(2)}) collective-permute-start(bf16[8,256,128]{2,1,0:T(8,128)(2,1)S(1)} %shard_map.104._.own_ref), channel_id=1, source_target_pairs={{0,1},{1,0},{2,3},{3,2},{4,5},{5,4},{6,7},{7,6},{8,9},{9,8},{10,11... | collective-permute-start | bytes 1572872 | tf_op jit(solution)/shard_map/ppermute | solution.py:306
  39.6 3.0 %collective-permute-start.6 = (bf16[4,256,128]{2,1,0:T(8,128)(2,1)S(1)}, bf16[4,256,128]{2,1,0:T(8,128)(2,1)S(1)}, u32[]{:S(2)}, u32[]{:S(2)}) collective-permute-start(bf16[4,256,128]{2,1,0:T(8,128)(2,1)S(1)} %shard_map.107.own_late), channel_id=1, source_target_pairs={{0,1},{1,0},{2,3},{3,2},{4,5},{5,4},{6,7},{7,6},{8,9},{9,8},{10,11... | collective-permute-start | bytes 786440 | tf_op jit(solution)/shard_map/ppermute | solution.py:306
  44.1 13.2 %copy-start.3 = (bf16[8192,256]{1,0:T(8,128)(2,1)S(1)}, bf16[8192,256]{1,0:T(8,128)(2,1)}, u32[]{:S(2)}) copy-start(bf16[8192,256]{1,0:T(8,128)(2,1)} %w_ref.3) | copy-start | bytes 12582916
  57.3 10.5 %copy-start.1 = (bf16[1,8192]{1,0:T(2,128)(2,1)S(1)}, bf16[1,8192]{1,0:T(2,128)(2,1)}, u32[]{:S(2)}) copy-start(bf16[1,8192]{1,0:T(2,128)(2,1)} %dec_x_ref.1) | copy-start | bytes 49156

commit v6 on v5

--- a/solution.py
+++ b/solution.py
@@ -14,7 +14,6 @@
 LANES = 128
 SUB = 8
 SHARES = 4
-EARLY = 2
 CHUNK = 512
 VMEM = pl.BlockSpec(memory_space=pltpu.VMEM)
 SMEM = pl.BlockSpec(memory_space=pltpu.SMEM)
@@ -51,12 +50,8 @@
         put(halves + i, block, range(copies))
     first = out_ref.shape[1] - share
     for i, block in enumerate(blocks[: 2 * SHARES * share]):
-        early = i < 2 * SHARES * EARLY
-        each = EARLY if early else share - EARLY
-        piece, place = divmod(i if early else i - 2 * SHARES * EARLY, each)
-        core, chip = divmod(piece, SHARES)
-        place += first if early else first + EARLY
-        put(place, block, range(2 * chip + core, copies, 2 * SHARES))
+        core, chip = divmod(i // share, SHARES)
+        put(first + i % share, block, range(2 * chip + core, copies, 2 * SHARES))
 
 
 def project_kernel(sent_ref, w_ref, mate_ref, *refs):
@@ -105,12 +100,12 @@
     return block.astype(F32).reshape(-1, LANES).astype(BF16)
 
 
-def merge_kernel(start, query_ref, own_0, own_1, own_2, own_3, out_ref):
+def merge_kernel(query_ref, own_0, own_1, own_2, own_3, out_ref):
     share = out_ref.shape[0] // SHARES
     place = lax.rem(lax.axis_index("seq") // 2, SHARES)
     for j, ref in enumerate((own_0, own_1, own_2, own_3)):
         for i in range(share):
-            out_ref[jnp.bitwise_xor(place, j) * share + i] = merge(ref[:, start + i])
+            out_ref[jnp.bitwise_xor(place, j) * share + i] = merge(ref[:, i])
 
 
 def pick(place, rows, own_ref, other_ref):
@@ -124,8 +119,7 @@
     return pl.ds(pl.multiple_of(tile_ref[0] * TILE_LEN, TILE_LEN), TILE_LEN)
 
 
-def attention_kernel(tile_ref, own_ref, other_ref, out_ref):
-    width = out_ref.shape[1]
+def attention_of(tile_ref, own_ref, other_ref, width):
     tiles = width // LANES
     mine = rows_of(tile_ref)
     every = slice(None)
@@ -151,28 +145,24 @@
         for t in range(span.start // LANES, span.stop // LANES):
             start = t * LANES - span.start
             attn[t] = attn[t] + part[:, start : start + LANES]
-    out_ref[...] = jnp.concatenate(attn, axis=1).astype(BF16)
-
-
-def features_kernel(
-    tile_ref, attn_ref, sent_ref, own_ref, other_ref, own_late, other_late, w_eo_ref, w_kv_ref, out_ref
-):
+    return jnp.concatenate(attn, axis=1).astype(BF16)
+
+
+def features_of(tile_ref, sent_ref, own_ref, other_ref, w_eo_ref):
     width, model = w_eo_ref.shape
     mine = rows_of(tile_ref)
-    early, late = 2 * own_ref.shape[0], 2 * own_late.shape[0]
-    first = 3 * width // LANES
-    enc_x = [pick(t, mine, own_ref, other_ref) for t in range(first, early)]
-    enc_x += [pick(t, mine, own_late, other_late) for t in range(late)]
+    first, held = 3 * width // LANES, 2 * own_ref.shape[0]
+    enc_x = [pick(t, mine, own_ref, other_ref) for t in range(first, held)]
     chunk = TILE_LEN // SUB
-    rest = first + model // LANES - early - late
-    last = sent_ref.shape[1] - (early + late) // (2 * SHARES)
+    last = sent_ref.shape[1] - held // (2 * SHARES)
+    rest = first + model // LANES - held
     enc_x += [merge(sent_ref[pl.ds(tile_ref[0] * chunk, chunk), t]) for t in range(last - rest, last)]
     enc_x = jnp.concatenate(enc_x, axis=1).astype(F32)
-    resid = enc_x + jnp.dot(attn_ref[...], w_eo_ref[...], preferred_element_type=F32)
+    attn = attention_of(tile_ref, own_ref, other_ref, width)
+    resid = enc_x + jnp.dot(attn, w_eo_ref[...], preferred_element_type=F32)
     center = resid - jnp.mean(resid, axis=-1, keepdims=True)
     spread = jnp.mean(center * center, axis=-1, keepdims=True)
-    features = (center * lax.rsqrt(spread + 1e-05)).astype(BF16)
-    out_ref[...] = jnp.dot(features, w_kv_ref[...], preferred_element_type=F32).astype(BF16)
+    return (center * lax.rsqrt(spread + 1e-05)).astype(BF16)
 
 
 def scores_kernel(query_ref, keys_ref, _, out_ref):
@@ -187,16 +177,20 @@
         ) * HD ** (-0.5)
 
 
-def attend_kernel(count_ref, query_ref, scores_ref, cache_ref, new_ref, out_ref):
+def attend_kernel(count_ref, query_ref, scores_ref, cache_ref, w_kv_ref, *refs):
+    out_ref = refs[-1]
     slots, length, both = cache_ref.shape
     width = both // 2
     kv_heads = width // HD
     per = query_ref.shape[0] // kv_heads
+    features = features_of(*refs[:-1])
+    new_keys = jnp.dot(features, w_kv_ref[:, :width], preferred_element_type=F32).astype(BF16)
     scores = []
     for g in range(kv_heads):
-        keys = new_ref[:, g * HD : (g + 1) * HD]
+        keys = new_keys[:, g * HD : (g + 1) * HD]
         head = query_ref[g * per : (g + 1) * per, :]
         scores.append(lax.dot_general(head, keys, (((1,), (1,)), ((), ())), preferred_element_type=F32))
+    new_values = jnp.dot(features, w_kv_ref[:, width:], preferred_element_type=F32).astype(BF16)
     scores = jnp.concatenate(scores, axis=0) * HD ** (-0.5)
     slot = lax.broadcasted_iota(jnp.int32, scores_ref.shape, 1) // length
     old = jnp.where(slot < count_ref[0], scores_ref[...], -jnp.inf)
@@ -204,14 +198,14 @@
     powers = jnp.exp(scores - jnp.max(scores, axis=-1, keepdims=True))
     weights = (powers / jnp.sum(powers, axis=-1, keepdims=True)).astype(BF16)
     copies = out_ref.shape[0]
+    halves = kv_heads // 2
     for g in range(kv_heads):
         mine = weights[g * per : (g + 1) * per]
-        cols = slice(width + g * HD, width + (g + 1) * HD)
-        values = cache_ref[:, :, cols].reshape(slots * length, HD)
+        values = cache_ref[:, :, width + g * HD : width + (g + 1) * HD].reshape(slots * length, HD)
         part = jnp.dot(mine[:, : slots * length], values, preferred_element_type=F32)
-        part = part + jnp.dot(mine[:, slots * length :], new_ref[:, cols], preferred_element_type=F32)
+        values = new_values[:, g * HD : (g + 1) * HD]
+        part = part + jnp.dot(mine[:, slots * length :], values, preferred_element_type=F32)
         part = part.astype(BF16)
-        halves = kv_heads // 2
         for copy in range(g // halves, copies, 2):
             out_ref[copy, g % halves] = part
 
@@ -295,18 +289,14 @@
             )(sums)
         else:
             query = add_up(sums)
-        def merge_part(start, count):
-            merged = pl.pallas_call(
-                functools.partial(merge_kernel, start),
-                out_shape=jax.ShapeDtypeStruct((SHARES * count, devices * SUB, LANES), BF16),
-                in_specs=[VMEM] * 5,
-                out_specs=VMEM,
-                compiler_params=params(4),
-            )(query, mine, *shares)
-            return merged, lax.ppermute(merged, "seq", swap)
-
-        early = merge_part(0, EARLY)
-        late = merge_part(EARLY, share - EARLY)
+        merged = pl.pallas_call(
+            merge_kernel,
+            out_shape=jax.ShapeDtypeStruct((SHARES * share, devices * SUB, LANES), BF16),
+            in_specs=[VMEM] * 5,
+            out_specs=VMEM,
+            compiler_params=params(4),
+        )(query, mine, *shares)
+        swapped = lax.ppermute(merged, "seq", swap)
         cache = cache_kv[0]
         scores = pl.pallas_call(
             scores_kernel,
@@ -314,31 +304,16 @@
             in_specs=[VMEM] * 2 + [ANY],
             out_specs=VMEM,
             compiler_params=params(4),
-        )(query, cache, early[0])
-        attn = pl.pallas_call(
-            attention_kernel,
-            out_shape=jax.ShapeDtypeStruct((TILE_LEN, w_eo.shape[0]), BF16),
-            in_specs=[SMEM] + [VMEM] * 2,
-            out_specs=VMEM,
-            compiler_params=params(8),
-        )(doc_tile, *early)
-        new_kv = pl.pallas_call(
-            features_kernel,
-            out_shape=jax.ShapeDtypeStruct((TILE_LEN, w_kv.shape[1]), BF16),
-            in_specs=[SMEM] + [VMEM] * 8,
-            out_specs=VMEM,
-            compiler_params=params(8),
-            cost_estimate=LONG,
-        )(doc_tile, attn, copies, *early, *late, w_eo, w_kv)
+        )(query, cache, merged)
         heads = query.shape[0]
         copies = pl.pallas_call(
             attend_kernel,
             out_shape=jax.ShapeDtypeStruct((devices, heads // (2 * SUB), SUB, LANES), BF16),
-            in_specs=[SMEM] + [VMEM] * 4,
-            out_specs=VMEM,
-            compiler_params=params(4),
+            in_specs=[SMEM] + [VMEM] * 4 + [SMEM] + [VMEM] * 4,
+            out_specs=VMEM,
+            compiler_params=params(16),
             cost_estimate=LONG,
-        )(cached_count, query, scores, cache, new_kv)
+        )(cached_count, query, scores, cache, w_kv, doc_tile, copies, merged, swapped, w_eo)
         sums = project(exchange(copies), w_o, w_o_mate)
         if sums.shape[-1] == LANES:
             kernel, scratch, attn = finish_sums_kernel, [rows, pltpu.VMEM((heads, LANES), BF16)], sums

time: 68.8 us -> 68.2 us (level)
    pallas_call x4 -> x1, Pallas kernels: 2.44 us -> 0.14 us  [local(): pl.pallas_call(merge_kernel, out_shape=jax.ShapeDtypeStruct((SHARES * sha...]
    pallas_call x1, Pallas kernels: 0.74 us -> 2.63 us  [local(): pl.pallas_call(attend_kernel, out_shape=jax.ShapeDtypeStruct((devices, he...]
  transfers between devices with their start and end apart: 7 -> 6, of which waited for: 0 -> 1; matrix products, arithmetic and copies ran while one was open for 1% -> 1% of each run, Pallas kernels for 4% -> 2%
where the time goes in v6:
time: 68.2 us; the launch traced here: 68 us
  blocking collectives  54.8 us (80%)
  Pallas kernels  6.12 us (9%)
  starting transfers between devices  4.24 us (6%)
  between operations  1.44 us (2%)
  other arithmetic  0.83 us (1%)
    all_to_all x4, blocking collectives, exchange(): return lax.all_to_all(sent, 'seq', 0, 0, tiled=True)  54.8 us
    ppermute x3, starting transfers between devices, local(): lax.ppermute(mine, 'seq', [(i, i ^ 2 * j) for i in range(devices)])  3.55 us
    pallas_call x1, Pallas kernels, local(): pl.pallas_call(attend_kernel, out_shape=jax.ShapeDtypeStruct((devices, he...  2.63 us
    pallas_call x2, Pallas kernels, project(): pl.pallas_call(project_kernel, out_shape=jax.ShapeDtypeStruct((devices, 2...  2.02 us
  transfers between devices with their start and end apart: 6, of which 1 were waited for; matrix products, arithmetic and copies ran while one was open for 1% of the time, Pallas kernels for 2%

profile of v6, /device:TPU:0, one launch (start us, length us, event | category | flops | bytes accessed | tf_op | source)
XLA Modules:
  0.0 68.0 jit_solution(9211854879735547407)
XLA Ops:
  0.0 0.5 collective-permute-start.1
  0.5 0.1 collective-permute-start
  0.5 0.8 %pad_maximum_fusion.rows_in_ref = bf16[9,8192]{1,0:T(8,128)(2,1)S(1)} fusion(bf16[1,8192]{1,0:T(2,128)(2,1)} %dec_x_ref.1, bf16[8,4992]{1,0:T(8,128)(2,1)S(1)} %broadcast_in_dim.3, bf16[8,1280]{1,0:T(8,128)(2,1)} %param.10, bf16[8,1920]{1,0:T(8,128)(2,1)} %bitcast.6), kind=kLoop, calls=%fused_computation | loop fusion | flops 589824 | bytes 294912 | tf_op jit(solution)/shard_map/concatenate | solution.py:254
  1.4 0.0 copy-start.2
  1.4 0.2 shard_map.100
  1.6 0.0 slice-start
  1.6 22.7 %all_to_all.20.sent_ref.own_ref.refs_1_ = bf16[32,8,8,128]{3,2,1,0:T(8,128)(2,1)S(1)} all-to-all(bf16[32,8,8,128]{3,2,1,0:T(8,128)(2,1)S(1)} %shard_map.100), channel_id=1, replica_groups=mesh['group'=1,'seq'=32] {'seq'}, dimensions={0} | all-to-all | bytes 1048576 | tf_op jit(solution)/shard_map/all_to_all | solution.py:230
  24.3 0.0 copy-start
  24.3 0.0 slice-start.1
  24.3 1.0 %collective-permute-start.2 = (bf16[32,3,8,128]{3,2,1,0:T(8,128)(2,1)S(1)}, bf16[32,3,8,128]{3,2,1,0:T(8,128)(2,1)S(1)}, u32[]{:S(2)}, u32[]{:S(2)}) collective-permute-start(bf16[32,3,8,128]{3,2,1,0:T(8,128)(2,1)S(1)} %shard_map.103.own_0), channel_id=1, source_target_pairs={{0,2},{1,3},{2,0},{3,1},{4,6},{5,7},{6,4},{7,5},{8,10},{9,11},{10,... | collective-permute-start | bytes 589832 | tf_op jit(solution)/shard_map/ppermute | solution.py:279
  25.3 1.5 %collective-permute-start.3 = (bf16[32,3,8,128]{3,2,1,0:T(8,128)(2,1)S(1)}, bf16[32,3,8,128]{3,2,1,0:T(8,128)(2,1)S(1)}, u32[]{:S(2)}, u32[]{:S(2)}) collective-permute-start(bf16[32,3,8,128]{3,2,1,0:T(8,128)(2,1)S(1)} %shard_map.103.own_0), channel_id=1, source_target_pairs={{0,4},{1,5},{2,6},{3,7},{4,0},{5,1},{6,2},{7,3},{8,12},{9,13},{10,... | collective-permute-start | bytes 589832 | tf_op jit(solution)/shard_map/ppermute | solution.py:279
  26.8 1.1 %collective-permute-start.4 = (bf16[32,3,8,128]{3,2,1,0:T(8,128)(2,1)S(1)}, bf16[32,3,8,128]{3,2,1,0:T(8,128)(2,1)S(1)}, u32[]{:S(2)}, u32[]{:S(2)}) collective-permute-start(bf16[32,3,8,128]{3,2,1,0:T(8,128)(2,1)S(1)} %shard_map.103.own_0), channel_id=1, source_target_pairs={{0,6},{1,7},{2,4},{3,5},{4,2},{5,3},{6,0},{7,1},{8,14},{9,15},{10,... | collective-permute-start | bytes 589832 | tf_op jit(solution)/shard_map/ppermute | solution.py:279
  27.9 0.0 collective-permute-done.1.refs_0_.mate_ref
  27.9 0.0 collective-permute-done.mate_ref
  27.9 0.0 copy-done.2
  27.9 1.0 %shard_map.101 = f32[32,2,2,128]{3,2,1,0:T(2,128)S(1)} custom-call(bf16[32,8,8,128]{3,2,1,0:T(8,128)(2,1)S(1)} %all_to_all.20.sent_ref.own_ref.refs_1_, bf16[8192,256]{1,0:T(8,128)(2,1)S(1)} %copy-done.2, bf16[8192,256]{1,0:T(8,128)(2,1)S(1)} %collective-permute-done.mate_ref, bf16[8192,256]{1,0:T(8,128)(2,1)S(1)} %collective-permute-done.1.refs_0_.mate_ref), custom_call_target="tpu_custom_call" | custom-call | flops 10000000000 | bytes 10000000 | tf_op jit(solution)/shard_map/pallas_call | solution.py:235
  28.9 0.0 copy-start.4
  28.9 10.3 %all_to_all.21.sums_ref = f32[32,2,2,128]{3,2,1,0:T(2,128)S(1)} all-to-all(f32[32,2,2,128]{3,2,1,0:T(2,128)S(1)} %shard_map.101), channel_id=1, replica_groups=mesh['group'=1,'seq'=32] {'seq'}, dimensions={0} | all-to-all | bytes 131072 | tf_op jit(solution)/shard_map/all_to_all | solution.py:230
  39.2 0.0 collective-permute-done.2.own_1
  39.2 0.0 collective-permute-done.3.own_2
  39.3 0.0 collective-permute-done.4.own_3
  39.3 0.1 shard_map.104._.refs_2_
  39.4 0.2 collective-permute-start.5
  40.9 0.0 copy-done
  40.9 0.4 shard_map.105.scores_ref
  41.3 0.5 collective-permute-done.5.refs_3_
  41.8 0.0 slice-done
  41.8 2.6 %shard_map.106 = bf16[32,4,8,128]{3,2,1,0:T(8,128)(2,1)S(1)} custom-call(s32[1]{0:T(128)S(6)} %copy.12.count_ref, bf16[64,128]{1,0:T(8,128)(2,1)S(1)} %shard_map.102.query_ref, f32[64,512]{1,0:T(8,128)S(1)} %shard_map.105.scores_ref, bf16[4,128,2048]{2,1,0:T(8,128)(2,1)S(1)} %bitcast.3, bf16[1280,2048]{1,0:T(8,128)(2,1)S(1)} %bitcast.5, s32[1]{0:T(128)S(6)} %copy.11.refs_0_, ...), custom_call_target="tpu_custom_call" | custom-call | flops 10000000000 | bytes 10000000 | tf_op jit(solution)/shard_map/pallas_call | solution.py:309
  44.4 12.3 %all_to_all.22.sent_ref = bf16[32,4,8,128]{3,2,1,0:T(8,128)(2,1)S(1)} all-to-all(bf16[32,4,8,128]{3,2,1,0:T(8,128)(2,1)S(1)} %shard_map.106), channel_id=1, replica_groups=mesh['group'=1,'seq'=32] {'seq'}, dimensions={0} | all-to-all | bytes 524288 | tf_op jit(solution)/shard_map/all_to_all | solution.py:230
  56.7 1.0 %shard_map.107 = f32[32,2,2,128]{3,2,1,0:T(2,128)S(1)} custom-call(bf16[32,4,8,128]{3,2,1,0:T(8,128)(2,1)S(1)} %all_to_all.22.sent_ref, bf16[8192,256]{1,0:T(8,128)(2,1)S(1)} %copy-done.3, bf16[8192,256]{1,0:T(8,128)(2,1)S(1)} %collective-permute-done.1.refs_0_.mate_ref), custom_call_target="tpu_custom_call" | custom-call | flops 10000000000 | bytes 10000000 | tf_op jit(solution)/shard_map/pallas_call | solution.py:235
  57.7 9.5 %all_to_all.23.sums_ref = f32[32,2,2,128]{3,2,1,0:T(2,128)S(1)} all-to-all(f32[32,2,2,128]{3,2,1,0:T(2,128)S(1)} %shard_map.107), channel_id=1, replica_groups=mesh['group'=1,'seq'=32] {'seq'}, dimensions={0} | all-to-all | bytes 131072 | tf_op jit(solution)/shard_map/all_to_all | solution.py:230
  67.3 0.7 %shard_map.108 = bf16[1,8192]{1,0:T(2,128)(2,1)} custom-call(f32[32,2,2,128]{3,2,1,0:T(2,128)S(1)} %all_to_all.23.sums_ref, bf16[1,8192]{1,0:T(2,128)(2,1)S(1)} %copy-done.1), custom_call_target="tpu_custom_call" | custom-call | flops 10000000000 | bytes 10000000 | tf_op jit(solution)/shard_map/pallas_call | solution.py:322
  (10 shorter events, 0.1 us)
Async XLA Ops:
  0.0 27.9 %collective-permute-start.1 = (bf16[8192,256]{1,0:T(8,128)(2,1)}, bf16[8192,256]{1,0:T(8,128)(2,1)S(1)}, u32[]{:S(2)}, u32[]{:S(2)}) collective-permute-start(bf16[8192,256]{1,0:T(8,128)(2,1)} %w_ref.3), channel_id=1, source_target_pairs={{0,1},{1,0},{2,3},{3,2},{4,5},{5,4},{6,7},{7,6},{8,9},{9,8},{10,11... | collective-permute-start | bytes 12582920 | tf_op jit(solution)/shard_map/ppermute | solution.py:256
  0.5 27.4 %collective-permute-start = (bf16[8192,256]{1,0:T(8,128)(2,1)}, bf16[8192,256]{1,0:T(8,128)(2,1)S(1)}, u32[]{:S(2)}, u32[]{:S(2)}) collective-permute-start(bf16[8192,256]{1,0:T(8,128)(2,1)} %w_ref.2), channel_id=1, source_target_pairs={{0,1},{1,0},{2,3},{3,2},{4,5},{5,4},{6,7},{7,6},{8,9},{9,8},{10,11... | collective-permute-start | bytes 12582920 | tf_op jit(solution)/shard_map/ppermute | solution.py:255
  1.4 26.5 %copy-start.2 = (bf16[8192,256]{1,0:T(8,128)(2,1)S(1)}, bf16[8192,256]{1,0:T(8,128)(2,1)}, u32[]{:S(2)}) copy-start(bf16[8192,256]{1,0:T(8,128)(2,1)} %w_ref.2) | copy-start | bytes 12582916
  1.6 40.2 %slice-start = ((s8[5242880]{0:T(1024)(128)(4,1)}), s8[4194304]{0:T(1024)(128)(4,1)S(1)}, s32[]{:S(2)}) async-start(s8[5242880]{0:T(1024)(128)(4,1)} %bitcast.4), calls=%async_computation.4 | async-start | bytes 8388608
  24.3 16.6 %copy-start = (bf16[1,4,128,2048]{3,2,1,0:T(8,128)(2,1)S(1)}, bf16[1,4,128,2048]{3,2,1,0:T(8,128)(2,1)}, u32[]{:S(2)}) copy-start(bf16[1,4,128,2048]{3,2,1,0:T(8,128)(2,1)} %param.17) | copy-start | bytes 6291460
  24.3 17.5 %slice-start.1 = ((s8[5242880]{0:T(1024)(128)(4,1)}), s8[1048576]{0:T(1024)(128)(4,1)S(1)}, s32[]{:S(2)}) async-start(s8[5242880]{0:T(1024)(128)(4,1)} %bitcast.4), calls=%async_computation.5 | async-start | bytes 2097152
  24.3 14.9 %collective-permute-start.2 = (bf16[32,3,8,128]{3,2,1,0:T(8,128)(2,1)S(1)}, bf16[32,3,8,128]{3,2,1,0:T(8,128)(2,1)S(1)}, u32[]{:S(2)}, u32[]{:S(2)}) collective-permute-start(bf16[32,3,8,128]{3,2,1,0:T(8,128)(2,1)S(1)} %shard_map.103.own_0), channel_id=1, source_target_pairs={{0,2},{1,3},{2,0},{3,1},{4,6},{5,7},{6,4},{7,5},{8,10},{9,11},{10,... | collective-permute-start | bytes 589832 | tf_op jit(solution)/shard_map/ppermute | solution.py:279
  25.3 13.9 %collective-permute-start.3 = (bf16[32,3,8,128]{3,2,1,0:T(8,128)(2,1)S(1)}, bf16[32,3,8,128]{3,2,1,0:T(8,128)(2,1)S(1)}, u32[]{:S(2)}, u32[]{:S(2)}) collective-permute-start(bf16[32,3,8,128]{3,2,1,0:T(8,128)(2,1)S(1)} %shard_map.103.own_0), channel_id=1, source_target_pairs={{0,4},{1,5},{2,6},{3,7},{4,0},{5,1},{6,2},{7,3},{8,12},{9,13},{10,... | collective-permute-start | bytes 589832 | tf_op jit(solution)/shard_map/ppermute | solution.py:279
  26.8 12.5 %collective-permute-start.4 = (bf16[32,3,8,128]{3,2,1,0:T(8,128)(2,1)S(1)}, bf16[32,3,8,128]{3,2,1,0:T(8,128)(2,1)S(1)}, u32[]{:S(2)}, u32[]{:S(2)}) collective-permute-start(bf16[32,3,8,128]{3,2,1,0:T(8,128)(2,1)S(1)} %shard_map.103.own_0), channel_id=1, source_target_pairs={{0,6},{1,7},{2,4},{3,5},{4,2},{5,3},{6,0},{7,1},{8,14},{9,15},{10,... | collective-permute-start | bytes 589832 | tf_op jit(solution)/shard_map/ppermute | solution.py:279
  28.9 12.9 %copy-start.4 = (bf16[640,1280]{1,0:T(8,128)(2,1)S(1)}, bf16[640,1280]{1,0:T(8,128)(2,1)}, u32[]{:S(2)}) copy-start(bf16[640,1280]{1,0:T(8,128)(2,1)} %refs_4_.1) | copy-start | bytes 4915204
  39.4 2.4 %collective-permute-start.5 = (bf16[12,256,128]{2,1,0:T(8,128)(2,1)S(1)}, bf16[12,256,128]{2,1,0:T(8,128)(2,1)S(1)}, u32[]{:S(2)}, u32[]{:S(2)}) collective-permute-start(bf16[12,256,128]{2,1,0:T(8,128)(2,1)S(1)} %shard_map.104._.refs_2_), channel_id=1, source_target_pairs={{0,1},{1,0},{2,3},{3,2},{4,5},{5,4},{6,7},{7,6},{8,9},{9,8},{10,11... | collective-permute-start | bytes 2359304 | tf_op jit(solution)/shard_map/ppermute | solution.py:299
  41.3 15.5 %copy-start.3 = (bf16[8192,256]{1,0:T(8,128)(2,1)S(1)}, bf16[8192,256]{1,0:T(8,128)(2,1)}, u32[]{:S(2)}) copy-start(bf16[8192,256]{1,0:T(8,128)(2,1)} %w_ref.3) | copy-start | bytes 12582916
  56.7 10.5 %copy-start.1 = (bf16[1,8192]{1,0:T(2,128)(2,1)S(1)}, bf16[1,8192]{1,0:T(2,128)(2,1)}, u32[]{:S(2)}) copy-start(bf16[1,8192]{1,0:T(2,128)(2,1)} %dec_x_ref.1) | copy-start | bytes 49156

commit v7 on v6

--- a/solution.py
+++ b/solution.py
@@ -28,7 +28,8 @@
 
 
 def pack_kernel(width, rows_in_ref, out_ref, rows_ref):
-    x = rows_in_ref[SUB : SUB + 1, :].astype(F32)
+    rows_in = rows_in_ref[...].astype(F32)
+    x = rows_in[SUB : SUB + 1]
     scale = lax.rsqrt(jnp.mean(x * x, axis=-1, keepdims=True) + 1e-05)
     normed = x * scale
     groups = x.shape[1] // LANES
@@ -44,7 +45,7 @@
     halves = groups // SUB // 2
     for i in range(2 * halves):
         put(i % halves, rows_ref[i * SUB : (i + 1) * SUB, :], range(i // halves, copies, 2))
-    blocks = [rows_in_ref[:SUB, t : t + LANES] for t in range(0, width, LANES)]
+    blocks = [rows_in[:SUB, t : t + LANES] for t in range(0, width, LANES)]
     share = len(blocks) // (2 * SHARES)
     for i, block in enumerate(blocks[2 * SHARES * share :]):
         put(halves + i, block, range(copies))
@@ -169,11 +170,12 @@
     slots, length, width = keys_ref.shape[0], keys_ref.shape[1], keys_ref.shape[2] // 2
     kv_heads = width // HD
     per = query_ref.shape[0] // kv_heads
+    query = query_ref[...]
     for g in range(kv_heads):
         keys = keys_ref[:, :, g * HD : (g + 1) * HD].reshape(slots * length, HD)
         rows = slice(g * per, (g + 1) * per)
         out_ref[rows, :] = lax.dot_general(
-            query_ref[rows, :], keys, (((1,), (1,)), ((), ())), preferred_element_type=F32
+            query[rows], keys, (((1,), (1,)), ((), ())), preferred_element_type=F32
         ) * HD ** (-0.5)
 
 
@@ -183,12 +185,13 @@
     width = both // 2
     kv_heads = width // HD
     per = query_ref.shape[0] // kv_heads
+    query = query_ref[...]
     features = features_of(*refs[:-1])
     new_keys = jnp.dot(features, w_kv_ref[:, :width], preferred_element_type=F32).astype(BF16)
     scores = []
     for g in range(kv_heads):
         keys = new_keys[:, g * HD : (g + 1) * HD]
-        head = query_ref[g * per : (g + 1) * per, :]
+        head = query[g * per : (g + 1) * per]
         scores.append(lax.dot_general(head, keys, (((1,), (1,)), ((), ())), preferred_element_type=F32))
     new_values = jnp.dot(features, w_kv_ref[:, width:], preferred_element_type=F32).astype(BF16)
     scores = jnp.concatenate(scores, axis=0) * HD ** (-0.5)

time: 68.2 us -> 68.2 us (level)
  no operation moved by 1% of the time
where the time goes in v7:
time: 68.2 us; the launch traced here: 68 us
  blocking collectives  54.8 us (80%)
  Pallas kernels  6.12 us (9%)
  starting transfers between devices  4.24 us (6%)
  between operations  1.44 us (2%)
  other arithmetic  0.83 us (1%)
    all_to_all x4, blocking collectives, exchange(): return lax.all_to_all(sent, 'seq', 0, 0, tiled=True)  54.8 us
    ppermute x3, starting transfers between devices, local(): lax.ppermute(mine, 'seq', [(i, i ^ 2 * j) for i in range(devices)])  3.55 us
    pallas_call x1, Pallas kernels, local(): pl.pallas_call(attend_kernel, out_shape=jax.ShapeDtypeStruct((devices, he...  2.63 us
    pallas_call x2, Pallas kernels, project(): pl.pallas_call(project_kernel, out_shape=jax.ShapeDtypeStruct((devices, 2...  2.02 us
  transfers between devices with their start and end apart: 6, of which 1 were waited for; matrix products, arithmetic and copies ran while one was open for 1% of the time, Pallas kernels for 2%

profile of v7, /device:TPU:0, one launch (start us, length us, event | category | flops | bytes accessed | tf_op | source)
XLA Modules:
  0.0 68.0 jit_solution(4263532018241220561)
XLA Ops:
  0.0 0.5 collective-permute-start.1
  0.5 0.1 collective-permute-start
  0.5 0.8 %pad_maximum_fusion.rows_in_ref = bf16[9,8192]{1,0:T(8,128)(2,1)S(1)} fusion(bf16[1,8192]{1,0:T(2,128)(2,1)} %dec_x_ref.1, bf16[8,4992]{1,0:T(8,128)(2,1)S(1)} %broadcast_in_dim.3, bf16[8,1280]{1,0:T(8,128)(2,1)} %param.10, bf16[8,1920]{1,0:T(8,128)(2,1)} %bitcast.6), kind=kLoop, calls=%fused_computation | loop fusion | flops 589824 | bytes 294912 | tf_op jit(solution)/shard_map/concatenate | solution.py:257
  1.4 0.0 copy-start.2
  1.4 0.2 shard_map.100
  1.6 0.0 slice-start
  1.6 22.7 %all_to_all.20.sent_ref.own_ref.refs_1_ = bf16[32,8,8,128]{3,2,1,0:T(8,128)(2,1)S(1)} all-to-all(bf16[32,8,8,128]{3,2,1,0:T(8,128)(2,1)S(1)} %shard_map.100), channel_id=1, replica_groups=mesh['group'=1,'seq'=32] {'seq'}, dimensions={0} | all-to-all | bytes 1048576 | tf_op jit(solution)/shard_map/all_to_all | solution.py:233
  24.3 0.0 copy-start
  24.3 0.0 slice-start.1
  24.3 1.0 %collective-permute-start.2 = (bf16[32,3,8,128]{3,2,1,0:T(8,128)(2,1)S(1)}, bf16[32,3,8,128]{3,2,1,0:T(8,128)(2,1)S(1)}, u32[]{:S(2)}, u32[]{:S(2)}) collective-permute-start(bf16[32,3,8,128]{3,2,1,0:T(8,128)(2,1)S(1)} %shard_map.103.own_0), channel_id=1, source_target_pairs={{0,2},{1,3},{2,0},{3,1},{4,6},{5,7},{6,4},{7,5},{8,10},{9,11},{10,... | collective-permute-start | bytes 589832 | tf_op jit(solution)/shard_map/ppermute | solution.py:282
  25.3 1.5 %collective-permute-start.3 = (bf16[32,3,8,128]{3,2,1,0:T(8,128)(2,1)S(1)}, bf16[32,3,8,128]{3,2,1,0:T(8,128)(2,1)S(1)}, u32[]{:S(2)}, u32[]{:S(2)}) collective-permute-start(bf16[32,3,8,128]{3,2,1,0:T(8,128)(2,1)S(1)} %shard_map.103.own_0), channel_id=1, source_target_pairs={{0,4},{1,5},{2,6},{3,7},{4,0},{5,1},{6,2},{7,3},{8,12},{9,13},{10,... | collective-permute-start | bytes 589832 | tf_op jit(solution)/shard_map/ppermute | solution.py:282
  26.8 1.1 %collective-permute-start.4 = (bf16[32,3,8,128]{3,2,1,0:T(8,128)(2,1)S(1)}, bf16[32,3,8,128]{3,2,1,0:T(8,128)(2,1)S(1)}, u32[]{:S(2)}, u32[]{:S(2)}) collective-permute-start(bf16[32,3,8,128]{3,2,1,0:T(8,128)(2,1)S(1)} %shard_map.103.own_0), channel_id=1, source_target_pairs={{0,6},{1,7},{2,4},{3,5},{4,2},{5,3},{6,0},{7,1},{8,14},{9,15},{10,... | collective-permute-start | bytes 589832 | tf_op jit(solution)/shard_map/ppermute | solution.py:282
  27.9 0.0 collective-permute-done.1.refs_0_.mate_ref
  27.9 0.0 collective-permute-done.mate_ref
  27.9 0.0 copy-done.2
  27.9 1.0 %shard_map.101 = f32[32,2,2,128]{3,2,1,0:T(2,128)S(1)} custom-call(bf16[32,8,8,128]{3,2,1,0:T(8,128)(2,1)S(1)} %all_to_all.20.sent_ref.own_ref.refs_1_, bf16[8192,256]{1,0:T(8,128)(2,1)S(1)} %copy-done.2, bf16[8192,256]{1,0:T(8,128)(2,1)S(1)} %collective-permute-done.mate_ref, bf16[8192,256]{1,0:T(8,128)(2,1)S(1)} %collective-permute-done.1.refs_0_.mate_ref), custom_call_target="tpu_custom_call" | custom-call | flops 10000000000 | bytes 10000000 | tf_op jit(solution)/shard_map/pallas_call | solution.py:238
  28.9 0.0 copy-start.4
  28.9 10.3 %all_to_all.21.sums_ref = f32[32,2,2,128]{3,2,1,0:T(2,128)S(1)} all-to-all(f32[32,2,2,128]{3,2,1,0:T(2,128)S(1)} %shard_map.101), channel_id=1, replica_groups=mesh['group'=1,'seq'=32] {'seq'}, dimensions={0} | all-to-all | bytes 131072 | tf_op jit(solution)/shard_map/all_to_all | solution.py:233
  39.2 0.0 collective-permute-done.2.own_1
  39.2 0.0 collective-permute-done.3.own_2
  39.3 0.0 collective-permute-done.4.own_3
  39.3 0.1 shard_map.104._.refs_2_
  39.4 0.2 collective-permute-start.5
  40.9 0.0 copy-done
  40.9 0.4 shard_map.105.scores_ref
  41.3 0.5 collective-permute-done.5.refs_3_
  41.8 0.0 slice-done
  41.8 2.6 %shard_map.106 = bf16[32,4,8,128]{3,2,1,0:T(8,128)(2,1)S(1)} custom-call(s32[1]{0:T(128)S(6)} %copy.12.count_ref, bf16[64,128]{1,0:T(8,128)(2,1)S(1)} %shard_map.102.query_ref, f32[64,512]{1,0:T(8,128)S(1)} %shard_map.105.scores_ref, bf16[4,128,2048]{2,1,0:T(8,128)(2,1)S(1)} %bitcast.3, bf16[1280,2048]{1,0:T(8,128)(2,1)S(1)} %bitcast.5, s32[1]{0:T(128)S(6)} %copy.11.refs_0_, ...), custom_call_target="tpu_custom_call" | custom-call | flops 10000000000 | bytes 10000000 | tf_op jit(solution)/shard_map/pallas_call | solution.py:312
  44.4 12.3 %all_to_all.22.sent_ref = bf16[32,4,8,128]{3,2,1,0:T(8,128)(2,1)S(1)} all-to-all(bf16[32,4,8,128]{3,2,1,0:T(8,128)(2,1)S(1)} %shard_map.106), channel_id=1, replica_groups=mesh['group'=1,'seq'=32] {'seq'}, dimensions={0} | all-to-all | bytes 524288 | tf_op jit(solution)/shard_map/all_to_all | solution.py:233
  56.7 1.0 %shard_map.107 = f32[32,2,2,128]{3,2,1,0:T(2,128)S(1)} custom-call(bf16[32,4,8,128]{3,2,1,0:T(8,128)(2,1)S(1)} %all_to_all.22.sent_ref, bf16[8192,256]{1,0:T(8,128)(2,1)S(1)} %copy-done.3, bf16[8192,256]{1,0:T(8,128)(2,1)S(1)} %collective-permute-done.1.refs_0_.mate_ref), custom_call_target="tpu_custom_call" | custom-call | flops 10000000000 | bytes 10000000 | tf_op jit(solution)/shard_map/pallas_call | solution.py:238
  57.7 9.5 %all_to_all.23.sums_ref = f32[32,2,2,128]{3,2,1,0:T(2,128)S(1)} all-to-all(f32[32,2,2,128]{3,2,1,0:T(2,128)S(1)} %shard_map.107), channel_id=1, replica_groups=mesh['group'=1,'seq'=32] {'seq'}, dimensions={0} | all-to-all | bytes 131072 | tf_op jit(solution)/shard_map/all_to_all | solution.py:233
  67.3 0.7 %shard_map.108 = bf16[1,8192]{1,0:T(2,128)(2,1)} custom-call(f32[32,2,2,128]{3,2,1,0:T(2,128)S(1)} %all_to_all.23.sums_ref, bf16[1,8192]{1,0:T(2,128)(2,1)S(1)} %copy-done.1), custom_call_target="tpu_custom_call" | custom-call | flops 10000000000 | bytes 10000000 | tf_op jit(solution)/shard_map/pallas_call | solution.py:325
  (10 shorter events, 0.1 us)
Async XLA Ops:
  0.0 27.9 %collective-permute-start.1 = (bf16[8192,256]{1,0:T(8,128)(2,1)}, bf16[8192,256]{1,0:T(8,128)(2,1)S(1)}, u32[]{:S(2)}, u32[]{:S(2)}) collective-permute-start(bf16[8192,256]{1,0:T(8,128)(2,1)} %w_ref.3), channel_id=1, source_target_pairs={{0,1},{1,0},{2,3},{3,2},{4,5},{5,4},{6,7},{7,6},{8,9},{9,8},{10,11... | collective-permute-start | bytes 12582920 | tf_op jit(solution)/shard_map/ppermute | solution.py:259
  0.5 27.4 %collective-permute-start = (bf16[8192,256]{1,0:T(8,128)(2,1)}, bf16[8192,256]{1,0:T(8,128)(2,1)S(1)}, u32[]{:S(2)}, u32[]{:S(2)}) collective-permute-start(bf16[8192,256]{1,0:T(8,128)(2,1)} %w_ref.2), channel_id=1, source_target_pairs={{0,1},{1,0},{2,3},{3,2},{4,5},{5,4},{6,7},{7,6},{8,9},{9,8},{10,11... | collective-permute-start | bytes 12582920 | tf_op jit(solution)/shard_map/ppermute | solution.py:258
  1.4 26.5 %copy-start.2 = (bf16[8192,256]{1,0:T(8,128)(2,1)S(1)}, bf16[8192,256]{1,0:T(8,128)(2,1)}, u32[]{:S(2)}) copy-start(bf16[8192,256]{1,0:T(8,128)(2,1)} %w_ref.2) | copy-start | bytes 12582916
  1.6 40.2 %slice-start = ((s8[5242880]{0:T(1024)(128)(4,1)}), s8[4194304]{0:T(1024)(128)(4,1)S(1)}, s32[]{:S(2)}) async-start(s8[5242880]{0:T(1024)(128)(4,1)} %bitcast.4), calls=%async_computation.4 | async-start | bytes 8388608
  24.3 16.6 %copy-start = (bf16[1,4,128,2048]{3,2,1,0:T(8,128)(2,1)S(1)}, bf16[1,4,128,2048]{3,2,1,0:T(8,128)(2,1)}, u32[]{:S(2)}) copy-start(bf16[1,4,128,2048]{3,2,1,0:T(8,128)(2,1)} %param.17) | copy-start | bytes 6291460
  24.3 17.5 %slice-start.1 = ((s8[5242880]{0:T(1024)(128)(4,1)}), s8[1048576]{0:T(1024)(128)(4,1)S(1)}, s32[]{:S(2)}) async-start(s8[5242880]{0:T(1024)(128)(4,1)} %bitcast.4), calls=%async_computation.5 | async-start | bytes 2097152
  24.3 14.9 %collective-permute-start.2 = (bf16[32,3,8,128]{3,2,1,0:T(8,128)(2,1)S(1)}, bf16[32,3,8,128]{3,2,1,0:T(8,128)(2,1)S(1)}, u32[]{:S(2)}, u32[]{:S(2)}) collective-permute-start(bf16[32,3,8,128]{3,2,1,0:T(8,128)(2,1)S(1)} %shard_map.103.own_0), channel_id=1, source_target_pairs={{0,2},{1,3},{2,0},{3,1},{4,6},{5,7},{6,4},{7,5},{8,10},{9,11},{10,... | collective-permute-start | bytes 589832 | tf_op jit(solution)/shard_map/ppermute | solution.py:282
  25.3 13.9 %collective-permute-start.3 = (bf16[32,3,8,128]{3,2,1,0:T(8,128)(2,1)S(1)}, bf16[32,3,8,128]{3,2,1,0:T(8,128)(2,1)S(1)}, u32[]{:S(2)}, u32[]{:S(2)}) collective-permute-start(bf16[32,3,8,128]{3,2,1,0:T(8,128)(2,1)S(1)} %shard_map.103.own_0), channel_id=1, source_target_pairs={{0,4},{1,5},{2,6},{3,7},{4,0},{5,1},{6,2},{7,3},{8,12},{9,13},{10,... | collective-permute-start | bytes 589832 | tf_op jit(solution)/shard_map/ppermute | solution.py:282
  26.8 12.5 %collective-permute-start.4 = (bf16[32,3,8,128]{3,2,1,0:T(8,128)(2,1)S(1)}, bf16[32,3,8,128]{3,2,1,0:T(8,128)(2,1)S(1)}, u32[]{:S(2)}, u32[]{:S(2)}) collective-permute-start(bf16[32,3,8,128]{3,2,1,0:T(8,128)(2,1)S(1)} %shard_map.103.own_0), channel_id=1, source_target_pairs={{0,6},{1,7},{2,4},{3,5},{4,2},{5,3},{6,0},{7,1},{8,14},{9,15},{10,... | collective-permute-start | bytes 589832 | tf_op jit(solution)/shard_map/ppermute | solution.py:282
  28.9 12.9 %copy-start.4 = (bf16[640,1280]{1,0:T(8,128)(2,1)S(1)}, bf16[640,1280]{1,0:T(8,128)(2,1)}, u32[]{:S(2)}) copy-start(bf16[640,1280]{1,0:T(8,128)(2,1)} %refs_4_.1) | copy-start | bytes 4915204
  39.4 2.4 %collective-permute-start.5 = (bf16[12,256,128]{2,1,0:T(8,128)(2,1)S(1)}, bf16[12,256,128]{2,1,0:T(8,128)(2,1)S(1)}, u32[]{:S(2)}, u32[]{:S(2)}) collective-permute-start(bf16[12,256,128]{2,1,0:T(8,128)(2,1)S(1)} %shard_map.104._.refs_2_), channel_id=1, source_target_pairs={{0,1},{1,0},{2,3},{3,2},{4,5},{5,4},{6,7},{7,6},{8,9},{9,8},{10,11... | collective-permute-start | bytes 2359304 | tf_op jit(solution)/shard_map/ppermute | solution.py:302
  41.3 15.5 %copy-start.3 = (bf16[8192,256]{1,0:T(8,128)(2,1)S(1)}, bf16[8192,256]{1,0:T(8,128)(2,1)}, u32[]{:S(2)}) copy-start(bf16[8192,256]{1,0:T(8,128)(2,1)} %w_ref.3) | copy-start | bytes 12582916
  56.7 10.5 %copy-start.1 = (bf16[1,8192]{1,0:T(2,128)(2,1)S(1)}, bf16[1,8192]{1,0:T(2,128)(2,1)}, u32[]{:S(2)}) copy-start(bf16[1,8192]{1,0:T(2,128)(2,1)} %dec_x_ref.1) | copy-start | bytes 49156

commit v8 on v7

--- a/solution.py
+++ b/solution.py
@@ -27,7 +27,7 @@
     return pltpu.CompilerParams(vmem_limit_bytes=mib * 1024 * 1024)
 
 
-def pack_kernel(width, rows_in_ref, out_ref, rows_ref):
+def pack_kernel(width, rows_in_ref, out_ref, last_ref, rows_ref):
     rows_in = rows_in_ref[...].astype(F32)
     x = rows_in[SUB : SUB + 1]
     scale = lax.rsqrt(jnp.mean(x * x, axis=-1, keepdims=True) + 1e-05)
@@ -47,8 +47,7 @@
         put(i % halves, rows_ref[i * SUB : (i + 1) * SUB, :], range(i // halves, copies, 2))
     blocks = [rows_in[:SUB, t : t + LANES] for t in range(0, width, LANES)]
     share = len(blocks) // (2 * SHARES)
-    for i, block in enumerate(blocks[2 * SHARES * share :]):
-        put(halves + i, block, range(copies))
+    last_ref[...] = blocks[-1]
     first = out_ref.shape[1] - share
     for i, block in enumerate(blocks[: 2 * SHARES * share]):
         core, chip = divmod(i // share, SHARES)
@@ -56,7 +55,7 @@
 
 
 def project_kernel(sent_ref, w_ref, mate_ref, *refs):
-    out_ref, rows_ref, x_ref = refs[-3:]
+    out_ref, rows_ref, x_ref, sums_ref = refs[-4:]
     docs, half = x_ref.shape
     for i in range(half // (SUB * LANES)):
         rows_ref[...] = sent_ref[:, i].astype(F32).reshape(docs * SUB, LANES)
@@ -64,32 +63,44 @@
             k = i * SUB + j
             x_ref[:, k * LANES : (k + 1) * LANES] = rows_ref[pl.ds(j, docs, stride=SUB), :].astype(BF16)
     core = lax.rem(lax.axis_index("seq"), 2)
-    parts, lanes = out_ref.shape[2:]
+    cols = w_ref.shape[1]
+    heads = 2 * cols // LANES
 
     def multiply(side):
-        for ref, place in ((w_ref, side), (mate_ref, 1 - side)):
-            result = jnp.zeros((docs, ref.shape[1]), F32)
+        results = []
+        for ref in (w_ref, mate_ref)[:: 1 - 2 * side]:
+            result = jnp.zeros((docs, cols), F32)
             for k in range(0, half, CHUNK):
                 rows = slice(side * half + k, side * half + k + CHUNK)
                 result += jnp.dot(x_ref[:, k : k + CHUNK], ref[rows, :], preferred_element_type=F32)
-            result = jnp.stack([result[:, p * lanes : (p + 1) * lanes] for p in range(parts)], axis=1)
-            out_ref[:, place] = result
+            results.append(result)
+        results = jnp.concatenate(results, axis=1)
+        sums_ref[:, :heads] = jnp.stack([results[:, h * LANES : (h + 1) * LANES] for h in range(heads)], axis=1)
 
     for side in range(2):
         pl.when(core == side)(functools.partial(multiply, side))
-
-
-def add_halves(sums_ref, rows_ref):
-    devices, cores, parts, _ = sums_ref.shape
-    for chip in range(devices // 2):
-        for core in range(cores):
-            row = (chip * cores + core) * parts
-            rows_ref[row : row + parts, :] = sums_ref[2 * chip, core] + sums_ref[2 * chip + 1, core]
+    if len(refs) > 4:
+        last = refs[0][...]
+        for device in range(docs):
+            start = device % 2 * (SUB // 2)
+            sums_ref[device, heads:] = last[start : start + SUB // 2]
+    out_ref[...] = sums_ref[...].astype(out_ref.dtype)
+
+
+def add_halves(sums, rows_ref):
+    heads = 2 * rows_ref.shape[0] // sums.shape[0]
+    for chip in range(sums.shape[0] // 2):
+        rows_ref[chip * heads : (chip + 1) * heads, :] = sums[2 * chip, :heads] + sums[2 * chip + 1, :heads]
     return rows_ref[...].astype(BF16)
 
 
-def collect_kernel(sums_ref, out_ref, rows_ref):
-    out_ref[...] = add_halves(sums_ref, rows_ref)
+def collect_kernel(sums_ref, out_ref, last_ref, rows_ref, tail_ref):
+    sums = sums_ref[...].astype(F32)
+    out_ref[...] = add_halves(sums, rows_ref)
+    step = SUB // 2
+    for device in range(sums.shape[0]):
+        tail_ref[device * step : (device + 1) * step, :] = sums[device, sums.shape[1] - step :]
+    last_ref[...] = tail_ref[...].astype(BF16)
 
 
 def share_kernel(own_ref, out_ref):
@@ -101,16 +112,17 @@
     return block.astype(F32).reshape(-1, LANES).astype(BF16)
 
 
-def merge_kernel(query_ref, own_0, own_1, own_2, own_3, out_ref):
+def merge_kernel(last_ref, own_0, own_1, own_2, own_3, out_ref):
     share = out_ref.shape[0] // SHARES
     place = lax.rem(lax.axis_index("seq") // 2, SHARES)
     for j, ref in enumerate((own_0, own_1, own_2, own_3)):
         for i in range(share):
             out_ref[jnp.bitwise_xor(place, j) * share + i] = merge(ref[:, i])
+    out_ref[SHARES * share] = jnp.concatenate([last_ref[...], jnp.zeros(last_ref.shape, BF16)], axis=0)
 
 
 def pick(place, rows, own_ref, other_ref):
-    held = own_ref.shape[0]
+    held = own_ref.shape[0] - 1
     core = lax.rem(lax.axis_index("seq"), 2)
     side, index = divmod(place, held)
     return jnp.where(core == side, own_ref[index, rows], other_ref[index, rows])
@@ -149,15 +161,21 @@
     return jnp.concatenate(attn, axis=1).astype(BF16)
 
 
-def features_of(tile_ref, sent_ref, own_ref, other_ref, w_eo_ref):
+def features_of(tile_ref, own_ref, other_ref, w_eo_ref, tail_ref):
     width, model = w_eo_ref.shape
     mine = rows_of(tile_ref)
-    first, held = 3 * width // LANES, 2 * own_ref.shape[0]
-    enc_x = [pick(t, mine, own_ref, other_ref) for t in range(first, held)]
-    chunk = TILE_LEN // SUB
-    last = sent_ref.shape[1] - held // (2 * SHARES)
-    rest = first + model // LANES - held
-    enc_x += [merge(sent_ref[pl.ds(tile_ref[0] * chunk, chunk), t]) for t in range(last - rest, last)]
+    first, held = 3 * width // LANES, own_ref.shape[0] - 1
+    enc_x = [pick(t, mine, own_ref, other_ref) for t in range(first, 2 * held)]
+    half = TILE_LEN // 2
+    rows = pl.ds(pl.multiple_of(tile_ref[0] * half, half), half)
+    core = lax.rem(lax.axis_index("seq"), 2)
+    for side in range(2):
+        part = jnp.where(core == side, own_ref[held, rows], other_ref[held, rows]).astype(F32)
+        step = SUB // 2
+        for i in range(TILE_LEN // SUB):
+            start = i * SUB + side * step
+            tail_ref[start : start + step, :] = part[i * step : (i + 1) * step]
+    enc_x.append(tail_ref[...].astype(BF16))
     enc_x = jnp.concatenate(enc_x, axis=1).astype(F32)
     attn = attention_of(tile_ref, own_ref, other_ref, width)
     resid = enc_x + jnp.dot(attn, w_eo_ref[...], preferred_element_type=F32)
@@ -180,13 +198,13 @@
 
 
 def attend_kernel(count_ref, query_ref, scores_ref, cache_ref, w_kv_ref, *refs):
-    out_ref = refs[-1]
+    out_ref, tail_ref = refs[-2:]
     slots, length, both = cache_ref.shape
     width = both // 2
     kv_heads = width // HD
     per = query_ref.shape[0] // kv_heads
     query = query_ref[...]
-    features = features_of(*refs[:-1])
+    features = features_of(*refs[:-2], tail_ref)
     new_keys = jnp.dot(features, w_kv_ref[:, :width], preferred_element_type=F32).astype(BF16)
     scores = []
     for g in range(kv_heads):
@@ -213,18 +231,13 @@
             out_ref[copy, g % halves] = part
 
 
-def finish_kernel(attn_ref, dec_x_ref, out_ref):
-    attn = attn_ref[...].astype(F32)
+def finish_kernel(sums_ref, dec_x_ref, out_ref, rows_ref):
+    attn = add_halves(sums_ref[...], rows_ref).astype(F32)
     for k in range(attn.shape[0]):
         cols = slice(k * LANES, (k + 1) * LANES)
         out_ref[:, cols] = (dec_x_ref[:, cols].astype(F32) + attn[k : k + 1]).astype(BF16)
 
 
-def finish_sums_kernel(sums_ref, dec_x_ref, out_ref, rows_ref, attn_ref):
-    attn_ref[...] = add_halves(sums_ref, rows_ref)
-    finish_kernel(attn_ref, dec_x_ref, out_ref)
-
-
 def solution(mesh):
     devices = mesh.shape["seq"]
     swap = [(i, i ^ 1) for i in range(devices)]
@@ -232,23 +245,23 @@
     def exchange(sent):
         return lax.all_to_all(sent, "seq", 0, 0, tiled=True)
 
-    def project(copies, weight, mate, *ready):
+    def project(copies, weight, mate, *more):
         depth, cols = weight.shape
-        lanes = min(cols, LANES)
+        shape = (devices, 2 * cols // LANES + (SUB // 2 if more else 0), LANES)
         sums = pl.pallas_call(
             project_kernel,
-            out_shape=jax.ShapeDtypeStruct((devices, 2, cols // lanes, lanes), F32),
-            in_specs=[VMEM] * 3 + [ANY] * len(ready),
-            out_specs=VMEM,
-            scratch_shapes=[pltpu.VMEM((devices * SUB, LANES), F32), pltpu.VMEM((devices, depth // 2), BF16)],
+            out_shape=jax.ShapeDtypeStruct(shape, BF16 if more else F32),
+            in_specs=[VMEM] * 3 + ([VMEM, ANY] if more else []),
+            out_specs=VMEM,
+            scratch_shapes=[
+                pltpu.VMEM((devices * SUB, LANES), F32),
+                pltpu.VMEM((devices, depth // 2), BF16),
+                pltpu.VMEM(shape, F32),
+            ],
             compiler_params=params(8),
             cost_estimate=LONG,
-        )(copies, weight, mate, *ready)
+        )(copies, weight, mate, *more)
         return exchange(sums)
-
-    def add_up(sums):
-        sums = sums.reshape(devices // 2, 2, -1)
-        return (sums[:, 0] + sums[:, 1]).astype(BF16).reshape(-1, LANES)
 
     def local(enc_x, enc_qkv, w_eo, w_kv, dec_x, w_q, w_o, cache_kv, doc_tile, cached_count):
         width = (enc_qkv.size + enc_x.size) // SUB
@@ -259,14 +272,16 @@
         w_o_mate = lax.ppermute(w_o, "seq", swap)
         blocks = (enc_qkv.size + enc_x.size) // (SUB * LANES)
         share = blocks // (2 * SHARES)
-        rest = blocks - 2 * SHARES * share
-        groups = dec_x.size // (2 * SUB * LANES) + rest + share
+        groups = dec_x.size // (2 * SUB * LANES) + share
         rows = pltpu.VMEM((dec_x.shape[1] // LANES, LANES), F32)
-        packed = pl.pallas_call(
+        packed, last = pl.pallas_call(
             functools.partial(pack_kernel, width),
-            out_shape=jax.ShapeDtypeStruct((devices, groups, SUB, LANES), BF16),
+            out_shape=[
+                jax.ShapeDtypeStruct((devices, groups, SUB, LANES), BF16),
+                jax.ShapeDtypeStruct((SUB, LANES), F32),
+            ],
             in_specs=[VMEM],
-            out_specs=VMEM,
+            out_specs=[VMEM] * 2,
             scratch_shapes=[rows],
             compiler_params=params(2),
             cost_estimate=LONG,
@@ -280,25 +295,25 @@
             compiler_params=params(1),
         )(copies)
         shares = [lax.ppermute(mine, "seq", [(i, i ^ (2 * j)) for i in range(devices)]) for j in range(1, SHARES)]
-        sums = project(copies, w_q, w_q_mate, w_o_mate)
-        if sums.shape[-1] == LANES:
-            query = pl.pallas_call(
-                collect_kernel,
-                out_shape=jax.ShapeDtypeStruct((sums.size // (2 * LANES), LANES), BF16),
-                in_specs=[VMEM],
-                out_specs=VMEM,
-                scratch_shapes=[rows],
-                compiler_params=params(1),
-            )(sums)
-        else:
-            query = add_up(sums)
+        sums = project(copies, w_q, w_q_mate, last, w_o_mate)
+        query, last = pl.pallas_call(
+            collect_kernel,
+            out_shape=[
+                jax.ShapeDtypeStruct((dec_x.shape[1] // LANES, LANES), BF16),
+                jax.ShapeDtypeStruct((devices * SUB // 2, LANES), BF16),
+            ],
+            in_specs=[VMEM],
+            out_specs=[VMEM] * 2,
+            scratch_shapes=[rows, pltpu.VMEM((devices * SUB // 2, LANES), F32)],
+            compiler_params=params(1),
+        )(sums)
         merged = pl.pallas_call(
             merge_kernel,
-            out_shape=jax.ShapeDtypeStruct((SHARES * share, devices * SUB, LANES), BF16),
+            out_shape=jax.ShapeDtypeStruct((SHARES * share + 1, devices * SUB, LANES), BF16),
             in_specs=[VMEM] * 5,
             out_specs=VMEM,
             compiler_params=params(4),
-        )(query, mine, *shares)
+        )(last, mine, *shares)
         swapped = lax.ppermute(merged, "seq", swap)
         cache = cache_kv[0]
         scores = pl.pallas_call(
@@ -312,25 +327,22 @@
         copies = pl.pallas_call(
             attend_kernel,
             out_shape=jax.ShapeDtypeStruct((devices, heads // (2 * SUB), SUB, LANES), BF16),
-            in_specs=[SMEM] + [VMEM] * 4 + [SMEM] + [VMEM] * 4,
-            out_specs=VMEM,
+            in_specs=[SMEM] + [VMEM] * 4 + [SMEM] + [VMEM] * 3,
+            out_specs=VMEM,
+            scratch_shapes=[pltpu.VMEM((TILE_LEN, LANES), F32)],
             compiler_params=params(16),
             cost_estimate=LONG,
-        )(cached_count, query, scores, cache, w_kv, doc_tile, copies, merged, swapped, w_eo)
+        )(cached_count, query, scores, cache, w_kv, doc_tile, merged, swapped, w_eo)
         sums = project(exchange(copies), w_o, w_o_mate)
-        if sums.shape[-1] == LANES:
-            kernel, scratch, attn = finish_sums_kernel, [rows, pltpu.VMEM((heads, LANES), BF16)], sums
-        else:
-            kernel, scratch, attn = finish_kernel, [], add_up(sums)
         return pl.pallas_call(
-            kernel,
+            finish_kernel,
             out_shape=jax.ShapeDtypeStruct(dec_x.shape, BF16),
             in_specs=[VMEM] * 2,
             out_specs=VMEM,
-            scratch_shapes=scratch,
+            scratch_shapes=[rows],
             compiler_params=params(2),
             cost_estimate=LONG,
-        )(attn, dec_x)
+        )(sums, dec_x)
 
     return jax.shard_map(
         local,

time: 68.2 us -> 66.9 us (0.981)
  blocking collectives: 54.8 us -> 53.4 us
    all_to_all x4, blocking collectives: 54.8 us -> 53.4 us  [exchange(): return lax.all_to_all(sent, 'seq', 0, 0, tiled=True)]
where the time goes in v8:
time: 66.9 us; the launch traced here: 66.6 us
  blocking collectives  53.4 us (80%)
  Pallas kernels  6.13 us (9%)
  starting transfers between devices  4.24 us (6%)
  between operations  1.44 us (2%)
  other arithmetic  0.83 us (1%)
    all_to_all x4, blocking collectives, exchange(): return lax.all_to_all(sent, 'seq', 0, 0, tiled=True)  53.4 us
    ppermute x3, starting transfers between devices, local(): lax.ppermute(mine, 'seq', [(i, i ^ 2 * j) for i in range(devices)])  3.55 us
    pallas_call x1, Pallas kernels, local(): pl.pallas_call(attend_kernel, out_shape=jax.ShapeDtypeStruct((devices, he...  2.62 us
    pallas_call x2, Pallas kernels, project(): pl.pallas_call(project_kernel, out_shape=jax.ShapeDtypeStruct(shape, BF16...  2.05 us
  transfers between devices with their start and end apart: 6, of which 1 were waited for; matrix products, arithmetic and copies ran while one was open for 1% of the time, Pallas kernels for 2%

profile of v8, /device:TPU:0, one launch (start us, length us, event | category | flops | bytes accessed | tf_op | source)
XLA Modules:
  0.0 66.6 jit_solution(8162447095040824616)
XLA Ops:
  0.0 0.5 collective-permute-start.1
  0.5 0.1 collective-permute-start
  0.5 0.8 %pad_maximum_fusion.rows_in_ref = bf16[9,8192]{1,0:T(8,128)(2,1)S(1)} fusion(bf16[1,8192]{1,0:T(2,128)(2,1)} %dec_x_ref.1, bf16[8,4992]{1,0:T(8,128)(2,1)S(1)} %broadcast_in_dim.3, bf16[8,1280]{1,0:T(8,128)(2,1)} %param.10, bf16[8,1920]{1,0:T(8,128)(2,1)} %bitcast.6), kind=kLoop, calls=%fused_computation | loop fusion | flops 589824 | bytes 294912 | tf_op jit(solution)/shard_map/concatenate | solution.py:270
  1.4 0.0 copy-start.2
  1.4 0.2 shard_map.100
  1.6 21.5 %all_to_all.20.sent_ref.own_ref = bf16[32,7,8,128]{3,2,1,0:T(8,128)(2,1)S(1)} all-to-all(bf16[32,7,8,128]{3,2,1,0:T(8,128)(2,1)S(1)} %get-tuple-element.9), channel_id=1, replica_groups=mesh['group'=1,'seq'=32] {'seq'}, dimensions={0} | all-to-all | bytes 917504 | tf_op jit(solution)/shard_map/all_to_all | solution.py:246
  23.1 0.8 %collective-permute-start.2 = (bf16[32,3,8,128]{3,2,1,0:T(8,128)(2,1)S(1)}, bf16[32,3,8,128]{3,2,1,0:T(8,128)(2,1)S(1)}, u32[]{:S(2)}, u32[]{:S(2)}) collective-permute-start(bf16[32,3,8,128]{3,2,1,0:T(8,128)(2,1)S(1)} %shard_map.103.own_0), channel_id=1, source_target_pairs={{0,2},{1,3},{2,0},{3,1},{4,6},{5,7},{6,4},{7,5},{8,10},{9,11},{10,... | collective-permute-start | bytes 589832 | tf_op jit(solution)/shard_map/ppermute | solution.py:297
  23.8 1.5 %collective-permute-start.3 = (bf16[32,3,8,128]{3,2,1,0:T(8,128)(2,1)S(1)}, bf16[32,3,8,128]{3,2,1,0:T(8,128)(2,1)S(1)}, u32[]{:S(2)}, u32[]{:S(2)}) collective-permute-start(bf16[32,3,8,128]{3,2,1,0:T(8,128)(2,1)S(1)} %shard_map.103.own_0), channel_id=1, source_target_pairs={{0,4},{1,5},{2,6},{3,7},{4,0},{5,1},{6,2},{7,3},{8,12},{9,13},{10,... | collective-permute-start | bytes 589832 | tf_op jit(solution)/shard_map/ppermute | solution.py:297
  25.3 1.3 %collective-permute-start.4 = (bf16[32,3,8,128]{3,2,1,0:T(8,128)(2,1)S(1)}, bf16[32,3,8,128]{3,2,1,0:T(8,128)(2,1)S(1)}, u32[]{:S(2)}, u32[]{:S(2)}) collective-permute-start(bf16[32,3,8,128]{3,2,1,0:T(8,128)(2,1)S(1)} %shard_map.103.own_0), channel_id=1, source_target_pairs={{0,6},{1,7},{2,4},{3,5},{4,2},{5,3},{6,0},{7,1},{8,14},{9,15},{10,... | collective-permute-start | bytes 589832 | tf_op jit(solution)/shard_map/ppermute | solution.py:297
  26.6 0.0 collective-permute-done.1.refs_1_.mate_ref
  26.6 0.0 collective-permute-done.mate_ref
  26.6 0.0 copy-done.2
  26.6 0.0 copy-start
  26.7 0.0 slice-start.1
  26.7 1.0 %shard_map.101 = bf16[32,8,128]{2,1,0:T(8,128)(2,1)S(1)} custom-call(bf16[32,7,8,128]{3,2,1,0:T(8,128)(2,1)S(1)} %all_to_all.20.sent_ref.own_ref, bf16[8192,256]{1,0:T(8,128)(2,1)S(1)} %copy-done.2, bf16[8192,256]{1,0:T(8,128)(2,1)S(1)} %collective-permute-done.mate_ref, f32[8,128]{1,0:T(8,128)S(1)} %get-tuple-element.10.refs_0_, ...), custom_call_target="tpu_custom_call" | custom-call | flops 10000000000 | bytes 10000000 | tf_op jit(solution)/shard_map/pallas_call | solution.py:251
  27.7 0.0 copy-start.4
  27.7 10.1 %all_to_all.21.sums_ref = bf16[32,8,128]{2,1,0:T(8,128)(2,1)S(1)} all-to-all(bf16[32,8,128]{2,1,0:T(8,128)(2,1)S(1)} %shard_map.101), channel_id=1, replica_groups=mesh['group'=1,'seq'=32] {'seq'}, dimensions={0} | all-to-all | bytes 131072 | tf_op jit(solution)/shard_map/all_to_all | solution.py:246
  37.8 0.0 collective-permute-done.2.own_1
  37.8 0.0 collective-permute-done.3.own_2
  37.8 0.0 collective-permute-done.4.own_3
  37.9 0.2 shard_map.104._.refs_1_
  38.0 0.2 collective-permute-start.5
  39.5 0.0 copy-done
  39.5 0.4 shard_map.105.scores_ref
  39.9 0.6 collective-permute-done.5.refs_2_
  40.5 2.6 %shard_map.106 = bf16[32,4,8,128]{3,2,1,0:T(8,128)(2,1)S(1)} custom-call(s32[1]{0:T(128)S(6)} %copy.12.count_ref, bf16[64,128]{1,0:T(8,128)(2,1)S(1)} %get-tuple-element.11.query_ref, f32[64,512]{1,0:T(8,128)S(1)} %shard_map.105.scores_ref, bf16[4,128,2048]{2,1,0:T(8,128)(2,1)S(1)} %bitcast.3, bf16[1280,2048]{1,0:T(8,128)(2,1)S(1)} %bitcast.5, ...), custom_call_target="tpu_custom_call" | custom-call | flops 10000000000 | bytes 10000000 | tf_op jit(solution)/shard_map/pallas_call | solution.py:327
  43.1 12.3 %all_to_all.22.sent_ref = bf16[32,4,8,128]{3,2,1,0:T(8,128)(2,1)S(1)} all-to-all(bf16[32,4,8,128]{3,2,1,0:T(8,128)(2,1)S(1)} %shard_map.106), channel_id=1, replica_groups=mesh['group'=1,'seq'=32] {'seq'}, dimensions={0} | all-to-all | bytes 524288 | tf_op jit(solution)/shard_map/all_to_all | solution.py:246
  55.4 0.0 copy-done.3
  55.4 1.0 %shard_map.107 = f32[32,4,128]{2,1,0:T(4,128)S(1)} custom-call(bf16[32,4,8,128]{3,2,1,0:T(8,128)(2,1)S(1)} %all_to_all.22.sent_ref, bf16[8192,256]{1,0:T(8,128)(2,1)S(1)} %copy-done.3, bf16[8192,256]{1,0:T(8,128)(2,1)S(1)} %collective-permute-done.1.refs_1_.mate_ref), custom_call_target="tpu_custom_call" | custom-call | flops 10000000000 | bytes 10000000 | tf_op jit(solution)/shard_map/pallas_call | solution.py:251
  56.4 9.5 %all_to_all.23.sums_ref = f32[32,4,128]{2,1,0:T(4,128)S(1)} all-to-all(f32[32,4,128]{2,1,0:T(4,128)S(1)} %shard_map.107), channel_id=1, replica_groups=mesh['group'=1,'seq'=32] {'seq'}, dimensions={0} | all-to-all | bytes 131072 | tf_op jit(solution)/shard_map/all_to_all | solution.py:246
  66.0 0.0 copy-done.1
  66.0 0.7 %shard_map.108 = bf16[1,8192]{1,0:T(2,128)(2,1)} custom-call(f32[32,4,128]{2,1,0:T(4,128)S(1)} %all_to_all.23.sums_ref, bf16[1,8192]{1,0:T(2,128)(2,1)S(1)} %copy-done.1), custom_call_target="tpu_custom_call" | custom-call | flops 10000000000 | bytes 10000000 | tf_op jit(solution)/shard_map/pallas_call | solution.py:337
  (10 shorter events, 0.1 us)
Async XLA Ops:
  0.0 26.6 %collective-permute-start.1 = (bf16[8192,256]{1,0:T(8,128)(2,1)}, bf16[8192,256]{1,0:T(8,128)(2,1)S(1)}, u32[]{:S(2)}, u32[]{:S(2)}) collective-permute-start(bf16[8192,256]{1,0:T(8,128)(2,1)} %w_ref.3), channel_id=1, source_target_pairs={{0,1},{1,0},{2,3},{3,2},{4,5},{5,4},{6,7},{7,6},{8,9},{9,8},{10,11... | collective-permute-start | bytes 12582920 | tf_op jit(solution)/shard_map/ppermute | solution.py:272
  0.5 26.2 %collective-permute-start = (bf16[8192,256]{1,0:T(8,128)(2,1)}, bf16[8192,256]{1,0:T(8,128)(2,1)S(1)}, u32[]{:S(2)}, u32[]{:S(2)}) collective-permute-start(bf16[8192,256]{1,0:T(8,128)(2,1)} %w_ref.2), channel_id=1, source_target_pairs={{0,1},{1,0},{2,3},{3,2},{4,5},{5,4},{6,7},{7,6},{8,9},{9,8},{10,11... | collective-permute-start | bytes 12582920 | tf_op jit(solution)/shard_map/ppermute | solution.py:271
  1.4 25.3 %copy-start.2 = (bf16[8192,256]{1,0:T(8,128)(2,1)S(1)}, bf16[8192,256]{1,0:T(8,128)(2,1)}, u32[]{:S(2)}) copy-start(bf16[8192,256]{1,0:T(8,128)(2,1)} %w_ref.2) | copy-start | bytes 12582916
  23.1 14.7 %collective-permute-start.2 = (bf16[32,3,8,128]{3,2,1,0:T(8,128)(2,1)S(1)}, bf16[32,3,8,128]{3,2,1,0:T(8,128)(2,1)S(1)}, u32[]{:S(2)}, u32[]{:S(2)}) collective-permute-start(bf16[32,3,8,128]{3,2,1,0:T(8,128)(2,1)S(1)} %shard_map.103.own_0), channel_id=1, source_target_pairs={{0,2},{1,3},{2,0},{3,1},{4,6},{5,7},{6,4},{7,5},{8,10},{9,11},{10,... | collective-permute-start | bytes 589832 | tf_op jit(solution)/shard_map/ppermute | solution.py:297
  23.8 14.0 %collective-permute-start.3 = (bf16[32,3,8,128]{3,2,1,0:T(8,128)(2,1)S(1)}, bf16[32,3,8,128]{3,2,1,0:T(8,128)(2,1)S(1)}, u32[]{:S(2)}, u32[]{:S(2)}) collective-permute-start(bf16[32,3,8,128]{3,2,1,0:T(8,128)(2,1)S(1)} %shard_map.103.own_0), channel_id=1, source_target_pairs={{0,4},{1,5},{2,6},{3,7},{4,0},{5,1},{6,2},{7,3},{8,12},{9,13},{10,... | collective-permute-start | bytes 589832 | tf_op jit(solution)/shard_map/ppermute | solution.py:297
  25.3 12.5 %collective-permute-start.4 = (bf16[32,3,8,128]{3,2,1,0:T(8,128)(2,1)S(1)}, bf16[32,3,8,128]{3,2,1,0:T(8,128)(2,1)S(1)}, u32[]{:S(2)}, u32[]{:S(2)}) collective-permute-start(bf16[32,3,8,128]{3,2,1,0:T(8,128)(2,1)S(1)} %shard_map.103.own_0), channel_id=1, source_target_pairs={{0,6},{1,7},{2,4},{3,5},{4,2},{5,3},{6,0},{7,1},{8,14},{9,15},{10,... | collective-permute-start | bytes 589832 | tf_op jit(solution)/shard_map/ppermute | solution.py:297
  26.6 13.8 %slice-start = ((s8[5242880]{0:T(1024)(128)(4,1)}), s8[4194304]{0:T(1024)(128)(4,1)S(1)}, s32[]{:S(2)}) async-start(s8[5242880]{0:T(1024)(128)(4,1)} %bitcast.4), calls=%async_computation.4 | async-start | bytes 8388608
  26.6 12.8 %copy-start = (bf16[1,4,128,2048]{3,2,1,0:T(8,128)(2,1)S(1)}, bf16[1,4,128,2048]{3,2,1,0:T(8,128)(2,1)}, u32[]{:S(2)}) copy-start(bf16[1,4,128,2048]{3,2,1,0:T(8,128)(2,1)} %param.17) | copy-start | bytes 6291460
  26.7 13.8 %slice-start.1 = ((s8[5242880]{0:T(1024)(128)(4,1)}), s8[1048576]{0:T(1024)(128)(4,1)S(1)}, s32[]{:S(2)}) async-start(s8[5242880]{0:T(1024)(128)(4,1)} %bitcast.4), calls=%async_computation.5 | async-start | bytes 2097152
  27.7 12.8 %copy-start.4 = (bf16[640,1280]{1,0:T(8,128)(2,1)S(1)}, bf16[640,1280]{1,0:T(8,128)(2,1)}, u32[]{:S(2)}) copy-start(bf16[640,1280]{1,0:T(8,128)(2,1)} %refs_3_.1) | copy-start | bytes 4915204
  38.0 2.4 %collective-permute-start.5 = (bf16[13,256,128]{2,1,0:T(8,128)(2,1)S(1)}, bf16[13,256,128]{2,1,0:T(8,128)(2,1)S(1)}, u32[]{:S(2)}, u32[]{:S(2)}) collective-permute-start(bf16[13,256,128]{2,1,0:T(8,128)(2,1)S(1)} %shard_map.104._.refs_1_), channel_id=1, source_target_pairs={{0,1},{1,0},{2,3},{3,2},{4,5},{5,4},{6,7},{7,6},{8,9},{9,8},{10,11... | collective-permute-start | bytes 2555912 | tf_op jit(solution)/shard_map/ppermute | solution.py:317
  39.9 15.5 %copy-start.3 = (bf16[8192,256]{1,0:T(8,128)(2,1)S(1)}, bf16[8192,256]{1,0:T(8,128)(2,1)}, u32[]{:S(2)}) copy-start(bf16[8192,256]{1,0:T(8,128)(2,1)} %w_ref.3) | copy-start | bytes 12582916
  55.4 10.5 %copy-start.1 = (bf16[1,8192]{1,0:T(2,128)(2,1)S(1)}, bf16[1,8192]{1,0:T(2,128)(2,1)}, u32[]{:S(2)}) copy-start(bf16[1,8192]{1,0:T(2,128)(2,1)} %dec_x_ref.1) | copy-start | bytes 49156

commit v9 on v8

--- a/solution.py
+++ b/solution.py
@@ -75,16 +75,21 @@
                 result += jnp.dot(x_ref[:, k : k + CHUNK], ref[rows, :], preferred_element_type=F32)
             results.append(result)
         results = jnp.concatenate(results, axis=1)
-        sums_ref[:, :heads] = jnp.stack([results[:, h * LANES : (h + 1) * LANES] for h in range(heads)], axis=1)
+        sums_ref[...] = jnp.stack([results[:, h * LANES : (h + 1) * LANES] for h in range(heads)], axis=1)
 
     for side in range(2):
         pl.when(core == side)(functools.partial(multiply, side))
-    if len(refs) > 4:
-        last = refs[0][...]
-        for device in range(docs):
-            start = device % 2 * (SUB // 2)
-            sums_ref[device, heads:] = last[start : start + SUB // 2]
-    out_ref[...] = sums_ref[...].astype(out_ref.dtype)
+    if len(refs) == 4:
+        out_ref[...] = sums_ref[...]
+        return
+    sums = sums_ref[...]
+    high = sums.astype(BF16)
+    out_ref[:, 0, :heads] = high
+    out_ref[:, 1, :heads] = (sums - high.astype(F32)).astype(BF16)
+    last = refs[0][...].astype(BF16)
+    for device in range(docs):
+        start = device % 2 * (SUB // 2)
+        out_ref[device, 2] = last[start : start + SUB // 2]
 
 
 def add_halves(sums, rows_ref):
@@ -95,11 +100,12 @@
 
 
 def collect_kernel(sums_ref, out_ref, last_ref, rows_ref, tail_ref):
-    sums = sums_ref[...].astype(F32)
+    sums = sums_ref[:, 0].astype(F32) + sums_ref[:, 1].astype(F32)
     out_ref[...] = add_halves(sums, rows_ref)
     step = SUB // 2
-    for device in range(sums.shape[0]):
-        tail_ref[device * step : (device + 1) * step, :] = sums[device, sums.shape[1] - step :]
+    last = sums_ref[:, 2].astype(F32)
+    for device in range(last.shape[0]):
+        tail_ref[device * step : (device + 1) * step, :] = last[device]
     last_ref[...] = tail_ref[...].astype(BF16)
 
 
@@ -247,10 +253,10 @@
 
     def project(copies, weight, mate, *more):
         depth, cols = weight.shape
-        shape = (devices, 2 * cols // LANES + (SUB // 2 if more else 0), LANES)
+        shape = (devices, 2 * cols // LANES, LANES)
         sums = pl.pallas_call(
             project_kernel,
-            out_shape=jax.ShapeDtypeStruct(shape, BF16 if more else F32),
+            out_shape=jax.ShapeDtypeStruct((devices, 3, SUB // 2, LANES) if more else shape, BF16 if more else F32),
             in_specs=[VMEM] * 3 + ([VMEM, ANY] if more else []),
             out_specs=VMEM,
             scratch_shapes=[

time: 66.9 us -> 67.3 us (level)
  transfers between devices with their start and end apart: 6 -> 6, of which waited for: 1 -> 1; matrix products, arithmetic and copies ran while one was open for 1% -> 1% of each run, Pallas kernels for 2% -> 3%
where the time goes in v9:
time: 67.3 us; the launch traced here: 67.1 us
  blocking collectives  53.8 us (80%)
  Pallas kernels  6.15 us (9%)
  starting transfers between devices  4.25 us (6%)
  between operations  1.45 us (2%)
  other arithmetic  0.83 us (1%)
    all_to_all x4, blocking collectives, exchange(): return lax.all_to_all(sent, 'seq', 0, 0, tiled=True)  53.8 us
    ppermute x3, starting transfers between devices, local(): lax.ppermute(mine, 'seq', [(i, i ^ 2 * j) for i in range(devices)])  3.55 us
    pallas_call x1, Pallas kernels, local(): pl.pallas_call(attend_kernel, out_shape=jax.ShapeDtypeStruct((devices, he...  2.62 us
    pallas_call x2, Pallas kernels, project(): pl.pallas_call(project_kernel, out_shape=jax.ShapeDtypeStruct((devices, 3...  2.06 us
  transfers between devices with their start and end apart: 6, of which 1 were waited for; matrix products, arithmetic and copies ran while one was open for 1% of the time, Pallas kernels for 3%

profile of v9, /device:TPU:0, one launch (start us, length us, event | category | flops | bytes accessed | tf_op | source)
XLA Modules:
  0.0 67.1 jit_solution(15261236762254726095)
XLA Ops:
  0.0 0.5 collective-permute-start.1
  0.5 0.1 collective-permute-start
  0.5 0.8 %pad_maximum_fusion.rows_in_ref = bf16[9,8192]{1,0:T(8,128)(2,1)S(1)} fusion(bf16[1,8192]{1,0:T(2,128)(2,1)} %dec_x_ref.1, bf16[8,4992]{1,0:T(8,128)(2,1)S(1)} %broadcast_in_dim.3, bf16[8,1280]{1,0:T(8,128)(2,1)} %param.10, bf16[8,1920]{1,0:T(8,128)(2,1)} %bitcast.6), kind=kLoop, calls=%fused_computation | loop fusion | flops 589824 | bytes 294912 | tf_op jit(solution)/shard_map/concatenate | solution.py:276
  1.4 0.0 copy-start.2
  1.4 0.2 shard_map.100
  1.6 21.5 %all_to_all.20.sent_ref.own_ref = bf16[32,7,8,128]{3,2,1,0:T(8,128)(2,1)S(1)} all-to-all(bf16[32,7,8,128]{3,2,1,0:T(8,128)(2,1)S(1)} %get-tuple-element.9), channel_id=1, replica_groups=mesh['group'=1,'seq'=32] {'seq'}, dimensions={0} | all-to-all | bytes 917504 | tf_op jit(solution)/shard_map/all_to_all | solution.py:252
  23.1 0.8 %collective-permute-start.2 = (bf16[32,3,8,128]{3,2,1,0:T(8,128)(2,1)S(1)}, bf16[32,3,8,128]{3,2,1,0:T(8,128)(2,1)S(1)}, u32[]{:S(2)}, u32[]{:S(2)}) collective-permute-start(bf16[32,3,8,128]{3,2,1,0:T(8,128)(2,1)S(1)} %shard_map.103.own_0), channel_id=1, source_target_pairs={{0,2},{1,3},{2,0},{3,1},{4,6},{5,7},{6,4},{7,5},{8,10},{9,11},{10,... | collective-permute-start | bytes 589832 | tf_op jit(solution)/shard_map/ppermute | solution.py:303
  23.8 1.5 %collective-permute-start.3 = (bf16[32,3,8,128]{3,2,1,0:T(8,128)(2,1)S(1)}, bf16[32,3,8,128]{3,2,1,0:T(8,128)(2,1)S(1)}, u32[]{:S(2)}, u32[]{:S(2)}) collective-permute-start(bf16[32,3,8,128]{3,2,1,0:T(8,128)(2,1)S(1)} %shard_map.103.own_0), channel_id=1, source_target_pairs={{0,4},{1,5},{2,6},{3,7},{4,0},{5,1},{6,2},{7,3},{8,12},{9,13},{10,... | collective-permute-start | bytes 589832 | tf_op jit(solution)/shard_map/ppermute | solution.py:303
  25.3 1.3 %collective-permute-start.4 = (bf16[32,3,8,128]{3,2,1,0:T(8,128)(2,1)S(1)}, bf16[32,3,8,128]{3,2,1,0:T(8,128)(2,1)S(1)}, u32[]{:S(2)}, u32[]{:S(2)}) collective-permute-start(bf16[32,3,8,128]{3,2,1,0:T(8,128)(2,1)S(1)} %shard_map.103.own_0), channel_id=1, source_target_pairs={{0,6},{1,7},{2,4},{3,5},{4,2},{5,3},{6,0},{7,1},{8,14},{9,15},{10,... | collective-permute-start | bytes 589832 | tf_op jit(solution)/shard_map/ppermute | solution.py:303
  26.6 0.0 collective-permute-done.1.refs_1_.mate_ref
  26.6 0.0 collective-permute-done.mate_ref
  26.6 0.0 copy-done.2
  26.6 0.0 copy-start
  26.7 0.0 slice-start.1
  26.7 1.0 %shard_map.101 = bf16[32,3,4,128]{3,2,1,0:T(4,128)(2,1)S(1)} custom-call(bf16[32,7,8,128]{3,2,1,0:T(8,128)(2,1)S(1)} %all_to_all.20.sent_ref.own_ref, bf16[8192,256]{1,0:T(8,128)(2,1)S(1)} %copy-done.2, bf16[8192,256]{1,0:T(8,128)(2,1)S(1)} %collective-permute-done.mate_ref, f32[8,128]{1,0:T(8,128)S(1)} %get-tuple-element.10.refs_0_, ...), custom_call_target="tpu_custom_call" | custom-call | flops 10000000000 | bytes 10000000 | tf_op jit(solution)/shard_map/pallas_call | solution.py:257
  27.7 0.0 copy-start.4
  27.7 10.5 %all_to_all.21.sums_ref = bf16[32,3,4,128]{3,2,1,0:T(4,128)(2,1)S(1)} all-to-all(bf16[32,3,4,128]{3,2,1,0:T(4,128)(2,1)S(1)} %shard_map.101), channel_id=1, replica_groups=mesh['group'=1,'seq'=32] {'seq'}, dimensions={0} | all-to-all | bytes 196608 | tf_op jit(solution)/shard_map/all_to_all | solution.py:252
  38.2 0.0 collective-permute-done.2.own_1
  38.3 0.0 collective-permute-done.3.own_2
  38.3 0.0 collective-permute-done.4.own_3
  38.3 0.2 shard_map.104._.refs_1_
  38.4 0.2 collective-permute-start.5
  39.9 0.0 copy-done
  39.9 0.4 shard_map.105.scores_ref
  40.3 0.6 collective-permute-done.5.refs_2_
  40.9 0.0 slice-done
  40.9 0.0 slice-done.1
  40.9 2.6 %shard_map.106 = bf16[32,4,8,128]{3,2,1,0:T(8,128)(2,1)S(1)} custom-call(s32[1]{0:T(128)S(6)} %copy.12.count_ref, bf16[64,128]{1,0:T(8,128)(2,1)S(1)} %get-tuple-element.11.query_ref, f32[64,512]{1,0:T(8,128)S(1)} %shard_map.105.scores_ref, bf16[4,128,2048]{2,1,0:T(8,128)(2,1)S(1)} %bitcast.3, bf16[1280,2048]{1,0:T(8,128)(2,1)S(1)} %bitcast.5, ...), custom_call_target="tpu_custom_call" | custom-call | flops 10000000000 | bytes 10000000 | tf_op jit(solution)/shard_map/pallas_call | solution.py:333
  43.5 12.3 %all_to_all.22.sent_ref = bf16[32,4,8,128]{3,2,1,0:T(8,128)(2,1)S(1)} all-to-all(bf16[32,4,8,128]{3,2,1,0:T(8,128)(2,1)S(1)} %shard_map.106), channel_id=1, replica_groups=mesh['group'=1,'seq'=32] {'seq'}, dimensions={0} | all-to-all | bytes 524288 | tf_op jit(solution)/shard_map/all_to_all | solution.py:252
  55.8 1.0 %shard_map.107 = f32[32,4,128]{2,1,0:T(4,128)S(1)} custom-call(bf16[32,4,8,128]{3,2,1,0:T(8,128)(2,1)S(1)} %all_to_all.22.sent_ref, bf16[8192,256]{1,0:T(8,128)(2,1)S(1)} %copy-done.3, bf16[8192,256]{1,0:T(8,128)(2,1)S(1)} %collective-permute-done.1.refs_1_.mate_ref), custom_call_target="tpu_custom_call" | custom-call | flops 10000000000 | bytes 10000000 | tf_op jit(solution)/shard_map/pallas_call | solution.py:257
  56.9 9.5 %all_to_all.23.sums_ref = f32[32,4,128]{2,1,0:T(4,128)S(1)} all-to-all(f32[32,4,128]{2,1,0:T(4,128)S(1)} %shard_map.107), channel_id=1, replica_groups=mesh['group'=1,'seq'=32] {'seq'}, dimensions={0} | all-to-all | bytes 131072 | tf_op jit(solution)/shard_map/all_to_all | solution.py:252
  66.4 0.7 %shard_map.108 = bf16[1,8192]{1,0:T(2,128)(2,1)} custom-call(f32[32,4,128]{2,1,0:T(4,128)S(1)} %all_to_all.23.sums_ref, bf16[1,8192]{1,0:T(2,128)(2,1)S(1)} %copy-done.1), custom_call_target="tpu_custom_call" | custom-call | flops 10000000000 | bytes 10000000 | tf_op jit(solution)/shard_map/pallas_call | solution.py:343
  (10 shorter events, 0.1 us)
Async XLA Ops:
  0.0 26.6 %collective-permute-start.1 = (bf16[8192,256]{1,0:T(8,128)(2,1)}, bf16[8192,256]{1,0:T(8,128)(2,1)S(1)}, u32[]{:S(2)}, u32[]{:S(2)}) collective-permute-start(bf16[8192,256]{1,0:T(8,128)(2,1)} %w_ref.3), channel_id=1, source_target_pairs={{0,1},{1,0},{2,3},{3,2},{4,5},{5,4},{6,7},{7,6},{8,9},{9,8},{10,11... | collective-permute-start | bytes 12582920 | tf_op jit(solution)/shard_map/ppermute | solution.py:278
  0.5 26.2 %collective-permute-start = (bf16[8192,256]{1,0:T(8,128)(2,1)}, bf16[8192,256]{1,0:T(8,128)(2,1)S(1)}, u32[]{:S(2)}, u32[]{:S(2)}) collective-permute-start(bf16[8192,256]{1,0:T(8,128)(2,1)} %w_ref.2), channel_id=1, source_target_pairs={{0,1},{1,0},{2,3},{3,2},{4,5},{5,4},{6,7},{7,6},{8,9},{9,8},{10,11... | collective-permute-start | bytes 12582920 | tf_op jit(solution)/shard_map/ppermute | solution.py:277
  1.4 25.3 %copy-start.2 = (bf16[8192,256]{1,0:T(8,128)(2,1)S(1)}, bf16[8192,256]{1,0:T(8,128)(2,1)}, u32[]{:S(2)}) copy-start(bf16[8192,256]{1,0:T(8,128)(2,1)} %w_ref.2) | copy-start | bytes 12582916
  23.1 15.2 %collective-permute-start.2 = (bf16[32,3,8,128]{3,2,1,0:T(8,128)(2,1)S(1)}, bf16[32,3,8,128]{3,2,1,0:T(8,128)(2,1)S(1)}, u32[]{:S(2)}, u32[]{:S(2)}) collective-permute-start(bf16[32,3,8,128]{3,2,1,0:T(8,128)(2,1)S(1)} %shard_map.103.own_0), channel_id=1, source_target_pairs={{0,2},{1,3},{2,0},{3,1},{4,6},{5,7},{6,4},{7,5},{8,10},{9,11},{10,... | collective-permute-start | bytes 589832 | tf_op jit(solution)/shard_map/ppermute | solution.py:303
  23.8 14.4 %collective-permute-start.3 = (bf16[32,3,8,128]{3,2,1,0:T(8,128)(2,1)S(1)}, bf16[32,3,8,128]{3,2,1,0:T(8,128)(2,1)S(1)}, u32[]{:S(2)}, u32[]{:S(2)}) collective-permute-start(bf16[32,3,8,128]{3,2,1,0:T(8,128)(2,1)S(1)} %shard_map.103.own_0), channel_id=1, source_target_pairs={{0,4},{1,5},{2,6},{3,7},{4,0},{5,1},{6,2},{7,3},{8,12},{9,13},{10,... | collective-permute-start | bytes 589832 | tf_op jit(solution)/shard_map/ppermute | solution.py:303
  25.3 12.9 %collective-permute-start.4 = (bf16[32,3,8,128]{3,2,1,0:T(8,128)(2,1)S(1)}, bf16[32,3,8,128]{3,2,1,0:T(8,128)(2,1)S(1)}, u32[]{:S(2)}, u32[]{:S(2)}) collective-permute-start(bf16[32,3,8,128]{3,2,1,0:T(8,128)(2,1)S(1)} %shard_map.103.own_0), channel_id=1, source_target_pairs={{0,6},{1,7},{2,4},{3,5},{4,2},{5,3},{6,0},{7,1},{8,14},{9,15},{10,... | collective-permute-start | bytes 589832 | tf_op jit(solution)/shard_map/ppermute | solution.py:303
  26.6 14.3 %slice-start = ((s8[5242880]{0:T(1024)(128)(4,1)}), s8[4194304]{0:T(1024)(128)(4,1)S(1)}, s32[]{:S(2)}) async-start(s8[5242880]{0:T(1024)(128)(4,1)} %bitcast.4), calls=%async_computation.4 | async-start | bytes 8388608
  26.6 13.3 %copy-start = (bf16[1,4,128,2048]{3,2,1,0:T(8,128)(2,1)S(1)}, bf16[1,4,128,2048]{3,2,1,0:T(8,128)(2,1)}, u32[]{:S(2)}) copy-start(bf16[1,4,128,2048]{3,2,1,0:T(8,128)(2,1)} %param.17) | copy-start | bytes 6291460
  26.7 14.2 %slice-start.1 = ((s8[5242880]{0:T(1024)(128)(4,1)}), s8[1048576]{0:T(1024)(128)(4,1)S(1)}, s32[]{:S(2)}) async-start(s8[5242880]{0:T(1024)(128)(4,1)} %bitcast.4), calls=%async_computation.5 | async-start | bytes 2097152
  27.7 13.2 %copy-start.4 = (bf16[640,1280]{1,0:T(8,128)(2,1)S(1)}, bf16[640,1280]{1,0:T(8,128)(2,1)}, u32[]{:S(2)}) copy-start(bf16[640,1280]{1,0:T(8,128)(2,1)} %refs_3_.1) | copy-start | bytes 4915204
  38.4 2.4 %collective-permute-start.5 = (bf16[13,256,128]{2,1,0:T(8,128)(2,1)S(1)}, bf16[13,256,128]{2,1,0:T(8,128)(2,1)S(1)}, u32[]{:S(2)}, u32[]{:S(2)}) collective-permute-start(bf16[13,256,128]{2,1,0:T(8,128)(2,1)S(1)} %shard_map.104._.refs_1_), channel_id=1, source_target_pairs={{0,1},{1,0},{2,3},{3,2},{4,5},{5,4},{6,7},{7,6},{8,9},{9,8},{10,11... | collective-permute-start | bytes 2555912 | tf_op jit(solution)/shard_map/ppermute | solution.py:323
  40.3 15.5 %copy-start.3 = (bf16[8192,256]{1,0:T(8,128)(2,1)S(1)}, bf16[8192,256]{1,0:T(8,128)(2,1)}, u32[]{:S(2)}) copy-start(bf16[8192,256]{1,0:T(8,128)(2,1)} %w_ref.3) | copy-start | bytes 12582916
  55.8 10.5 %copy-start.1 = (bf16[1,8192]{1,0:T(2,128)(2,1)S(1)}, bf16[1,8192]{1,0:T(2,128)(2,1)}, u32[]{:S(2)}) copy-start(bf16[1,8192]{1,0:T(2,128)(2,1)} %dec_x_ref.1) | copy-start | bytes 49156
